TPU v7x, 32 devices: a whole 2x2x4 slice. The times are simulated.
32 devices in a mesh: cp: 4 (over y, x), dp: 8 (over z, core).
Axes of the slice: x: 2, y: 2, z: 4, core: 2. Of those that a mesh axis runs over, the one named last changes fastest.
Arguments:
- queries: bfloat16 [8, 768, 512], P('dp', 'cp'), may hold values from -6 to 6
- key_rows: bfloat16 [8, 768, 512], P('dp', 'cp'), may hold values from -6 to 6
- value_rows: bfloat16 [8, 768, 512], P('dp', 'cp'), may hold values from -6 to 6
- stream_in: bfloat16 [8, 768, 1024], P('dp', 'cp'), may hold values from -6 to 6
- out_grad: bfloat16 [8, 768, 1024], P('dp', 'cp'), may hold values from -6 to 6
- out_weight: bfloat16 [512, 1024], P('cp'), may hold values from -0.25 to 0.25
- conv_weight: float32 [7, 1024], replicated, may hold values from -3 to 3
- lengths: int32 [8], P('dp'), may hold values from 384 to 768, as said below
- offsets: int32 [8, 2], P('dp'), may hold values from 0 to 2, as said below
Outputs:
- query_grad: bfloat16 [8, 768, 512], P('dp', 'cp')
- key_grad: bfloat16 [8, 768, 512], P('dp', 'cp')
- value_grad: bfloat16 [8, 768, 512], P('dp', 'cp')
- stream_grad: bfloat16 [8, 768, 1024], P('dp', 'cp')
- weight_grad: float32 [512, 1024], P('cp')
- conv_grad: float32 [7, 1024], replicated
Inputs may be any that keep to these rules, and one draw needn't show every extreme that they name: `lengths`: each a multiple of 24; some utterance has exactly 768 frames. `offsets`: column 0 is the number of earlier blocks that a block attends, at most 2; column 1 the number of later blocks, at most 1; some utterance has 2 and 1.
All inputs are finite; a program needn't handle non-finite values.
Results may differ from a plain program's by a relative error of at most 0.0069.
Values may be sent and summed in bfloat16 or wider, within the bound.
No kernel may reach another device: no remote copies, remote signals or barrier semaphores. Data moves between devices by JAX's collectives and lax.ppermute only.
A program may use at most 64 MiB of HBM per device.

v0:
```python
import jax
import jax.numpy as jnp
from jax import lax
from jax.sharding import PartitionSpec as P

HEADS = 8
HSZ = 64
BLK = 24
KW = 7


neg_big = -1e30


def passed_along(array, axis, by):
    devices = lax.axis_size(axis)
    pairs = [(i, i + by) for i in range(devices) if 0 <= i + by < devices]
    return lax.ppermute(array, axis, pairs)


def extended(block, sides, width):
    for axis, dim in sides:
        count = lax.axis_size(axis)
        forward = [(i, i + 1) for i in range(count - 1)]
        backward = [(target, source) for source, target in forward]
        low = lax.ppermute(
            lax.slice_in_dim(block, block.shape[dim] - width, None, axis=dim), axis, forward
        )
        high = lax.ppermute(lax.slice_in_dim(block, 0, width, axis=dim), axis, backward)
        block = jnp.concatenate([low, block, high], axis=dim)
    return block


def attend_forward(query4, key4, value4, allowed, valid_rows, score_scale):
    scores = (
        jnp.einsum("nqhd,nkhd->nhqk", query4, key4, preferred_element_type=jnp.float32)
        * score_scale
    )
    masked = jnp.where(allowed[:, None, None, :], scores, neg_big)
    top_score = jnp.max(masked, axis=3, keepdims=True)
    exp_terms = jnp.exp(masked - top_score)
    softmax_w = exp_terms / jnp.sum(exp_terms, axis=3, keepdims=True)
    weight_b = softmax_w.astype(jnp.bfloat16)
    attended = jnp.einsum("nhqk,nkhd->nqhd", weight_b, value4, preferred_element_type=jnp.float32)
    row_total = query4.shape[0] * query4.shape[1]
    attended = attended.reshape(row_total, -1)
    attended = (attended * valid_rows[:, None]).astype(jnp.bfloat16)
    return (attended, softmax_w, weight_b)


def attend_backward(query4, key4, value4, softmax_w, weight_b, grad4, score_scale):
    dprob = jnp.einsum("nqhd,nkhd->nhqk", grad4, value4, preferred_element_type=jnp.float32)
    inner = jnp.sum(softmax_w * dprob, axis=3, keepdims=True)
    dscore = (softmax_w * (dprob - inner)).astype(jnp.bfloat16)
    query_g = (
        jnp.einsum("nhqk,nkhd->nqhd", dscore, key4, preferred_element_type=jnp.float32)
        * score_scale
    ).astype(jnp.bfloat16)
    key_g = (
        jnp.einsum("nhqk,nqhd->nkhd", dscore, query4, preferred_element_type=jnp.float32)
        * score_scale
    )
    value_g = jnp.einsum("nhqk,nqhd->nkhd", weight_b, grad4, preferred_element_type=jnp.float32)
    return (query_g, key_g, value_g)


def body(
    queries, key_rows, value_rows, stream_in, out_grad, out_weight, conv_weight, lengths, offsets
):
    row_count = queries.shape[1]
    head_feats = queries.shape[2]
    model_width = stream_in.shape[2]
    cp_place = lax.axis_index("cp")
    length = lengths[0]
    look_back = offsets[0, 0]
    look_ahead = offsets[0, 1]
    query_rows = queries[0]
    key_local = key_rows[0]
    value_local = value_rows[0]
    rim_rows = 2 * BLK
    span_rows = row_count + 3 * BLK
    block_count = row_count // BLK
    window_len = 4 * BLK
    half_width = KW // 2
    score_scale = HSZ ** (-0.5)
    before_k, before_v = passed_along(
        (key_local[row_count - rim_rows :], value_local[row_count - rim_rows :]), "cp", 1
    )
    after_k, after_v = passed_along((key_local[:BLK], value_local[:BLK]), "cp", -1)
    key_all = jnp.concatenate([before_k, key_local, after_k], 0)
    value_all = jnp.concatenate([before_v, value_local, after_v], 0)

    def windows_of(array):
        slabs = [
            array[shift_at * BLK : shift_at * BLK + row_count].reshape(block_count, BLK, head_feats)
            for shift_at in range(4)
        ]
        return jnp.stack(slabs, 1).reshape(block_count, window_len, HEADS, HSZ)

    key4 = windows_of(key_all)
    value4 = windows_of(value_all)
    query4 = query_rows.reshape(block_count, BLK, HEADS, HSZ)
    frames = cp_place * row_count + jnp.arange(row_count, dtype=jnp.int32)
    within = jnp.arange(window_len, dtype=jnp.int32)
    key_frames = (
        cp_place * row_count
        + jnp.arange(block_count, dtype=jnp.int32)[:, None] * BLK
        + within[None, :]
        - rim_rows
    )
    relative = within // BLK - 2
    in_reach = (relative >= -look_back) & (relative <= look_ahead)
    allowed = in_reach[None, :] & (key_frames >= 0) & (key_frames < length)
    valid_rows = (frames < length).astype(jnp.float32)
    attended, softmax_w, weight_b = attend_forward(
        query4, key4, value4, allowed, valid_rows, score_scale
    )
    full_weight = lax.all_gather(out_weight, "cp", axis=0, tiled=True)
    projected = jnp.dot(attended, full_weight, preferred_element_type=jnp.float32)
    mixed_rows = (stream_in[0].astype(jnp.float32) + projected) * valid_rows[:, None]
    grad_masked = out_grad[0] * valid_rows[:, None].astype(jnp.bfloat16)
    grad_ext = extended(grad_masked, (("cp", 0),), half_width)
    grad_ext_f = grad_ext.astype(jnp.float32)
    conv_sum = jnp.zeros((row_count, model_width), jnp.float32)
    conv_terms = []
    for tap in range(KW):
        shifted = grad_ext_f[2 * half_width - tap : 2 * half_width - tap + row_count]
        conv_sum = conv_sum + conv_weight[tap][None, :] * shifted
        conv_terms.append(jnp.sum(mixed_rows * shifted, axis=0))
    conv_local = jnp.stack(conv_terms, 0)
    stream_grad = (conv_sum * valid_rows[:, None]).astype(jnp.bfloat16)
    attn_grad = jnp.einsum(
        "td,ed->te", stream_grad, full_weight, preferred_element_type=jnp.float32
    ).astype(jnp.bfloat16)
    grad4 = attn_grad.reshape(block_count, BLK, HEADS, HSZ)
    query_g, key_wg, value_wg = attend_backward(
        query4, key4, value4, softmax_w, weight_b, grad4, score_scale
    )

    def fold_back(window_grad):
        parts = window_grad.reshape(block_count, 4, BLK, head_feats)
        total = jnp.zeros((block_count + 3, BLK, head_feats), jnp.float32)
        for shift_at in range(4):
            total = total + jnp.pad(parts[:, shift_at], ((shift_at, 3 - shift_at), (0, 0), (0, 0)))
        return total.reshape(span_rows, head_feats)

    key_g = fold_back(key_wg)
    value_g = fold_back(value_wg)
    back_k, back_v = passed_along((key_g[:rim_rows], value_g[:rim_rows]), "cp", -1)
    front_k, front_v = passed_along((key_g[span_rows - BLK :], value_g[span_rows - BLK :]), "cp", 1)
    key_sum = key_g[rim_rows : rim_rows + row_count]
    key_sum = (
        key_sum
        + jnp.pad(front_k, ((0, row_count - BLK), (0, 0)))
        + jnp.pad(back_k, ((row_count - rim_rows, 0), (0, 0)))
    )
    value_sum = value_g[rim_rows : rim_rows + row_count]
    value_sum = (
        value_sum
        + jnp.pad(front_v, ((0, row_count - BLK), (0, 0)))
        + jnp.pad(back_v, ((row_count - rim_rows, 0), (0, 0)))
    )
    weight_part = lax.psum_scatter(
        jnp.einsum("te,td->ed", attended, stream_grad, preferred_element_type=jnp.float32),
        "cp",
        scatter_dimension=0,
        tiled=True,
    )
    weight_grad = lax.psum(weight_part, "dp")
    conv_grad = lax.psum(conv_local, ("cp", "dp"))
    query_grad = query_g.reshape(row_count, head_feats)
    return (
        query_grad[None],
        key_sum.astype(jnp.bfloat16)[None],
        value_sum.astype(jnp.bfloat16)[None],
        stream_grad[None],
        weight_grad,
        conv_grad,
    )


def solution(mesh):
    return jax.shard_map(
        body,
        mesh=mesh,
        in_specs=(
            P("dp", "cp", None),
            P("dp", "cp", None),
            P("dp", "cp", None),
            P("dp", "cp", None),
            P("dp", "cp", None),
            P("cp", None),
            P(),
            P("dp"),
            P("dp", None),
        ),
        out_specs=(
            P("dp", "cp", None),
            P("dp", "cp", None),
            P("dp", "cp", None),
            P("dp", "cp", None),
            P("cp", None),
            P(),
        ),
        check_vma=False,
    )
```

profile of v0, /device:TPU:0, one launch (start us, length us, event | category | flops | bytes accessed | tf_op | source)
XLA Modules:
  0.0 202.1 jit_solution(10428984485713003544)
XLA Ops:
  12.8 6.1 %collective-permute-start.4 = (bf16[48,512]{1,0:T(8,128)(2,1)S(1)}, bf16[48,512]{1,0:T(8,128)(2,1)S(1)}, u32[]{:S(2)}, u32[]{:S(2)}) collective-permute-start(bf16[48,512]{1,0:T(8,128)(2,1)S(1)} %slice_bitcast_fusion.8), channel_id=1, source_target_pairs={{0,8},{8,16},{16,24},{1,9},{9,17},{17,25},{2,10},{10,18},{18,26},{... | collective-permute-start | bytes 147464 | tf_op jit(solution)/shard_map/ppermute | solution.py:18
  20.7 4.8 %collective-permute-start.2 = (bf16[3,1024]{1,0:T(4,128)(2,1)S(1)}, bf16[3,1024]{1,0:T(4,128)(2,1)S(1)}, u32[]{:S(2)}, u32[]{:S(2)}) collective-permute-start(bf16[3,1024]{1,0:T(4,128)(2,1)S(1)} %get-tuple-element.21), channel_id=1, source_target_pairs={{0,8},{8,16},{16,24},{1,9},{9,17},{17,25},{2,10},{10,18},{18,26},{... | collective-permute-start | bytes 18440 | tf_op jit(solution)/shard_map/ppermute | solution.py:26
  32.0 1.9 reshape_squeeze.3
  33.9 4.6 %collective-permute-start = (bf16[48,512]{1,0:T(8,128)(2,1)S(1)}, bf16[48,512]{1,0:T(8,128)(2,1)S(1)}, u32[]{:S(2)}, u32[]{:S(2)}) collective-permute-start(bf16[48,512]{1,0:T(8,128)(2,1)S(1)} %slice_bitcast_fusion.9), channel_id=1, source_target_pairs={{0,8},{8,16},{16,24},{1,9},{9,17},{17,25},{2,10},{10,18},{18,26},{... | collective-permute-start | bytes 147464 | tf_op jit(solution)/shard_map/ppermute | solution.py:18
  38.6 1.4 multiply_convert_fusion.1
  41.0 1.7 copy.46
  44.8 1.4 fusion.5
  47.3 4.9 %convolution_bitcast_fusion.1 = f32[8,24,8,64]{3,1,2,0:T(8,128)} fusion(bf16[8,96,8,64]{1,3,2,0:T(8,128)(2,1)} %copy.46, f32[8,8,24]{2,1,0:T(8,128)S(1)} %get-tuple-element.38, f32[8,8,24,96]{3,2,1,0:T(8,128)S(1)} %fusion.5), kind=kOutput, calls=%fused_computation.4 | convolution fusion | flops 19318368 | bytes 1775616 | tf_op jit(solution)/shard_map/nhqk,nkhd->nqhd/dot_general | solution.py:44
  53.8 1.9 fusion.27
  56.0 1.4 fusion.45
  57.4 1.8 convolution_convert_fusion
  59.5 1.9 multiply_reduce_fusion.7
  63.6 4.8 %convolution_bitcast_fusion = f32[8,96,8,64]{1,3,2,0:T(8,128)S(1)} fusion(bf16[8,24,8,64]{3,2,1,0:T(8,128)(2,1)} %copy-done.11, f32[8,8,24]{2,1,0:T(8,128)S(1)} %get-tuple-element.38, f32[8,8,24,96]{3,2,1,0:T(8,128)} %copy-done.2), kind=kOutput, calls=%fused_computation.2 | convolution fusion | flops 19318368 | bytes 2365440 | tf_op jit(solution)/shard_map/nhqk,nqhd->nkhd/dot_general | solution.py:63
  68.4 2.3 %copy.55 = f32[8,96,8,64]{3,2,1,0:T(8,128)} copy(f32[8,96,8,64]{1,3,2,0:T(8,128)S(1)} %convolution_bitcast_fusion) | data formatting | bytes 3145728 | tf_op jit(solution)/shard_map/nhqk,nqhd->nkhd/transpose | solution.py:63
  70.7 2.9 %reshape.119 = f32[8,4,24,512]{3,2,1,0:T(8,128)S(1)} reshape(f32[8,96,8,64]{3,2,1,0:T(8,128)} %copy.55) | data formatting | bytes 3145728 | tf_op jit(solution)/shard_map/reshape | solution.py:141
  73.8 5.4 %collective-permute-start.8 = (f32[24,512]{1,0:T(8,128)S(1)}, f32[24,512]{1,0:T(8,128)}, u32[]{:S(2)}, u32[]{:S(2)}) collective-permute-start(f32[24,512]{1,0:T(8,128)S(1)} %add_bitcast_fusion), channel_id=1, source_target_pairs={{0,8},{8,16},{16,24},{1,9},{9,17},{17,25},{2,10},{10,18},{18,26},{... | collective-permute-start | bytes 147464 | tf_op jit(solution)/shard_map/ppermute | solution.py:18
  81.9 2.3 %copy.50 = f32[8,96,8,64]{3,2,1,0:T(8,128)} copy(f32[8,96,8,64]{1,3,2,0:T(8,128)S(1)} %multiply_bitcast_fusion) | data formatting | bytes 3145728 | tf_op jit(solution)/shard_map/mul | solution.py:60
  84.2 2.9 %reshape.118 = f32[8,4,24,512]{3,2,1,0:T(8,128)S(1)} reshape(f32[8,96,8,64]{3,2,1,0:T(8,128)} %copy.50) | data formatting | bytes 3145728 | tf_op jit(solution)/shard_map/reshape | solution.py:141
  87.3 4.7 %collective-permute-start.6 = (f32[24,512]{1,0:T(8,128)S(1)}, f32[24,512]{1,0:T(8,128)S(1)}, u32[]{:S(2)}, u32[]{:S(2)}) collective-permute-start(f32[24,512]{1,0:T(8,128)S(1)} %add_bitcast_fusion.1), channel_id=1, source_target_pairs={{0,8},{8,16},{16,24},{1,9},{9,17},{17,25},{2,10},{10,18},{18,26},{... | collective-permute-start | bytes 147464 | tf_op jit(solution)/shard_map/ppermute | solution.py:18
  92.2 1.4 collective-permute-start.7
  94.8 41.4 %psum.15 = f32[7,1024]{1,0:T(8,128)} all-reduce(f32[7,1024]{1,0:T(8,128)S(1)} %stack.39), channel_id=1, replica_groups=mesh['cp'=4,'dp'=8] {'cp','dp'}, use_global_device_ids=true, to_apply=%region_12.13 | all-reduce | flops 7168 | bytes 57344 | tf_op jit(solution)/shard_map/psum | solution.py:170
  136.2 1.5 fusion.9
  138.5 55.3 %all-reduce.14.cloned.1.call-done = f32[128,1024]{1,0:T(8,128)} async-done(((f32[128,1024]{1,0:T(8,128)}), f32[128,1024]{1,0:T(8,128)}) %all-reduce.14.cloned.1.call-update) | async-done | bytes 524304 | tf_op jit(solution)/shard_map/psum | solution.py:169
  193.7 1.9 copy.79
  (98 shorter events, 26.0 us)
Async XLA Ops:
  7.2 50.3 %all-gather.2.cloned.1.call-start = ((), (), s32[]{:S(2)}) async-start(), calls=%async_computation.1 | async-start | bytes 1310720 | tf_op jit(solution)/shard_map/all_gather | solution.py:118
  7.9 128.3 %reduce-scatter.2.cloned.1.call-start = ((), (), s32[]{:S(2)}) async-start(), calls=%async_computation.2 | async-start | bytes 2621440 | tf_op jit(solution)/shard_map/reduce_scatter | solution.py:163
  8.7 31.3 %collective-permute-start.5 = (bf16[24,512]{1,0:T(8,128)(2,1)S(1)}, bf16[24,512]{1,0:T(8,128)(2,1)S(1)}, u32[]{:S(2)}, u32[]{:S(2)}) collective-permute-start(bf16[24,512]{1,0:T(8,128)(2,1)S(1)} %slice_bitcast_fusion.10), channel_id=1, source_target_pairs={{8,0},{16,8},{24,16},{9,1},{17,9},{25,17},{10,2},{18,10},{26,18},{... | collective-permute-start | bytes 73736 | tf_op jit(solution)/shard_map/ppermute | solution.py:18
  10.7 32.0 %collective-permute-start.1 = (bf16[24,512]{1,0:T(8,128)(2,1)S(1)}, bf16[24,512]{1,0:T(8,128)(2,1)S(1)}, u32[]{:S(2)}, u32[]{:S(2)}) collective-permute-start(bf16[24,512]{1,0:T(8,128)(2,1)S(1)} %slice_bitcast_fusion.11), channel_id=1, source_target_pairs={{8,0},{16,8},{24,16},{9,1},{17,9},{25,17},{10,2},{18,10},{26,18},{... | collective-permute-start | bytes 73736 | tf_op jit(solution)/shard_map/ppermute | solution.py:18
  12.8 27.2 %collective-permute-start.4 = (bf16[48,512]{1,0:T(8,128)(2,1)S(1)}, bf16[48,512]{1,0:T(8,128)(2,1)S(1)}, u32[]{:S(2)}, u32[]{:S(2)}) collective-permute-start(bf16[48,512]{1,0:T(8,128)(2,1)S(1)} %slice_bitcast_fusion.8), channel_id=1, source_target_pairs={{0,8},{8,16},{16,24},{1,9},{9,17},{17,25},{2,10},{10,18},{18,26},{... | collective-permute-start | bytes 147464 | tf_op jit(solution)/shard_map/ppermute | solution.py:18
  20.7 13.2 %collective-permute-start.2 = (bf16[3,1024]{1,0:T(4,128)(2,1)S(1)}, bf16[3,1024]{1,0:T(4,128)(2,1)S(1)}, u32[]{:S(2)}, u32[]{:S(2)}) collective-permute-start(bf16[3,1024]{1,0:T(4,128)(2,1)S(1)} %get-tuple-element.21), channel_id=1, source_target_pairs={{0,8},{8,16},{16,24},{1,9},{9,17},{17,25},{2,10},{10,18},{18,26},{... | collective-permute-start | bytes 18440 | tf_op jit(solution)/shard_map/ppermute | solution.py:26
  25.5 12.9 %collective-permute-start.3 = (bf16[3,1024]{1,0:T(4,128)(2,1)S(1)}, bf16[3,1024]{1,0:T(4,128)(2,1)S(1)}, u32[]{:S(2)}, u32[]{:S(2)}) collective-permute-start(bf16[3,1024]{1,0:T(4,128)(2,1)S(1)} %get-tuple-element.22), channel_id=1, source_target_pairs={{8,0},{16,8},{24,16},{9,1},{17,9},{25,17},{10,2},{18,10},{26,18},{... | collective-permute-start | bytes 18440 | tf_op jit(solution)/shard_map/ppermute | solution.py:29
  32.0 24.0 %copy-start.12 = (f32[192]{0:T(256)}, f32[192]{0:T(256)S(1)}, u32[]{:S(2)}) copy-start(f32[192]{0:T(256)S(1)} %compare_convert_fusion) | copy-start | bytes 2308
  33.9 8.8 %collective-permute-start = (bf16[48,512]{1,0:T(8,128)(2,1)S(1)}, bf16[48,512]{1,0:T(8,128)(2,1)S(1)}, u32[]{:S(2)}, u32[]{:S(2)}) collective-permute-start(bf16[48,512]{1,0:T(8,128)(2,1)S(1)} %slice_bitcast_fusion.9), channel_id=1, source_target_pairs={{0,8},{8,16},{16,24},{1,9},{9,17},{17,25},{2,10},{10,18},{18,26},{... | collective-permute-start | bytes 147464 | tf_op jit(solution)/shard_map/ppermute | solution.py:18
  40.2 2.5 %copy-start.9 = (bf16[1,192,512]{2,1,0:T(8,128)(2,1)S(1)}, bf16[1,192,512]{2,1,0:T(8,128)(2,1)}, u32[]{:S(2)}) copy-start(bf16[1,192,512]{2,1,0:T(8,128)(2,1)} %param.10) | copy-start | bytes 589828
  55.8 138.0 %all-reduce.14.cloned.1.call-start = ((), (), s32[]{:S(2)}) async-start(), calls=%async_computation.3 | async-start | bytes 1048576 | tf_op jit(solution)/shard_map/psum | solution.py:169
  57.4 2.0 %copy-start.3 = (f32[8,8,24,96]{3,2,1,0:T(8,128)S(1)}, f32[8,8,24,96]{3,2,1,0:T(8,128)}, u32[]{:S(2)}) copy-start(f32[8,8,24,96]{3,2,1,0:T(8,128)} %get-tuple-element.39) | copy-start | bytes 1769476
  59.5 1.9 copy-start.11
  59.5 1.9 copy-start.4
  73.8 7.6 %copy-start.1 = (bf16[8,24,8,64]{3,2,1,0:T(8,128)(2,1)S(1)}, bf16[8,24,8,64]{3,2,1,0:T(8,128)(2,1)}, u32[]{:S(2)}) copy-start(bf16[8,24,8,64]{3,2,1,0:T(8,128)(2,1)} %reshape_squeeze.3) | copy-start | bytes 589828
  73.8 62.4 %collective-permute-start.8 = (f32[24,512]{1,0:T(8,128)S(1)}, f32[24,512]{1,0:T(8,128)}, u32[]{:S(2)}, u32[]{:S(2)}) collective-permute-start(f32[24,512]{1,0:T(8,128)S(1)} %add_bitcast_fusion), channel_id=1, source_target_pairs={{0,8},{8,16},{16,24},{1,9},{9,17},{17,25},{2,10},{10,18},{18,26},{... | collective-permute-start | bytes 147464 | tf_op jit(solution)/shard_map/ppermute | solution.py:18
  80.1 56.1 %collective-permute-start.9 = (f32[48,512]{1,0:T(8,128)S(1)}, f32[48,512]{1,0:T(8,128)S(1)}, u32[]{:S(2)}, u32[]{:S(2)}) collective-permute-start(f32[48,512]{1,0:T(8,128)S(1)} %bitcast.156), channel_id=1, source_target_pairs={{8,0},{16,8},{24,16},{9,1},{17,9},{25,17},{10,2},{18,10},{26,18},{... | collective-permute-start | bytes 294920 | tf_op jit(solution)/shard_map/ppermute | solution.py:18
  87.3 6.4 %copy-start.7 = (f32[192,512]{1,0:T(8,128)S(1)}, f32[192,512]{1,0:T(8,128)}, u32[]{:S(2)}) copy-start(f32[192,512]{1,0:T(8,128)} %copy-done.6) | copy-start | bytes 1179652
  87.3 6.4 %copy-start.10 = (bf16[512,1024]{1,0:T(8,128)(2,1)S(1)}, bf16[512,1024]{1,0:T(8,128)(2,1)}, u32[]{:S(2)}) copy-start(bf16[512,1024]{1,0:T(8,128)(2,1)} %all-gather.2.cloned.1.call-done) | copy-start | bytes 3145732
  87.3 6.4 %copy-start.13 = (f32[192]{0:T(256)S(1)}, f32[192]{0:T(256)}, u32[]{:S(2)}) copy-start(f32[192]{0:T(256)} %copy-done.12) | copy-start | bytes 2308
  87.3 6.4 %copy-start.15 = (bf16[1,192,1024]{2,1,0:T(8,128)(2,1)S(1)}, bf16[1,192,1024]{2,1,0:T(8,128)(2,1)}, u32[]{:S(2)}) copy-start(bf16[1,192,1024]{2,1,0:T(8,128)(2,1)} %param.12) | copy-start | bytes 1179652
  87.3 50.4 %collective-permute-start.6 = (f32[24,512]{1,0:T(8,128)S(1)}, f32[24,512]{1,0:T(8,128)S(1)}, u32[]{:S(2)}, u32[]{:S(2)}) collective-permute-start(f32[24,512]{1,0:T(8,128)S(1)} %add_bitcast_fusion.1), channel_id=1, source_target_pairs={{0,8},{8,16},{16,24},{1,9},{9,17},{17,25},{2,10},{10,18},{18,26},{... | collective-permute-start | bytes 147464 | tf_op jit(solution)/shard_map/ppermute | solution.py:18
  92.2 44.0 %slice-start = ((f32[11,24,512]{2,1,0:T(8,128)}), f32[8,24,512]{2,1,0:T(8,128)S(1)}, s32[]{:S(2)}) async-start(f32[11,24,512]{2,1,0:T(8,128)} %copy-done.5), calls=%async_computation.4 | async-start | bytes 786432 | tf_op jit(solution)/shard_map/slice | solution.py:157
  92.2 45.5 %collective-permute-start.7 = (f32[48,512]{1,0:T(8,128)S(1)}, f32[48,512]{1,0:T(8,128)S(1)}, u32[]{:S(2)}, u32[]{:S(2)}) collective-permute-start(f32[48,512]{1,0:T(8,128)S(1)} %bitcast.157), channel_id=1, source_target_pairs={{8,0},{16,8},{24,16},{9,1},{17,9},{25,17},{10,2},{18,10},{26,18},{... | collective-permute-start | bytes 294920 | tf_op jit(solution)/shard_map/ppermute | solution.py:18
  (6 other events, 8.8 us)
Sparse Core Ops, SparseCore 0:
  9.8 30.1 all-gather.1
  55.9 38.0 reduce-scatter.1
  136.3 57.3 all-reduce.13
where the time goes:
time: 203 us; the launch traced here: 202 us
  waiting for transfers between devices  56 us (28%)
  blocking collectives  41.4 us (20%)
  starting transfers between devices  32.4 us (16%)
  local copies, waits for them, and re-layouts  28 us (14%)
  matrix products  18.9 us (9%)
  between operations  15.6 us (8%)
  other arithmetic  9.88 us (5%)
    psum x1, waiting for transfers between devices, body(): weight_grad = lax.psum(weight_part, 'dp')  55.3 us
    psum x1, blocking collectives, body(): conv_grad = lax.psum(conv_local, ('cp', 'dp'))  41.4 us
    ppermute x8, starting transfers between devices, passed_along(): return lax.ppermute(array, axis, pairs)  26 us
    reshape x2, local copies, waits for them, and re-layouts, fold_back(): parts = window_grad.reshape(block_count, 4, BLK, head_feats)  5.76 us
    dot_general x1, matrix products, attend_forward(): jnp.einsum('nhqk,nkhd->nqhd', weight_b, value4, preferred_element_type=jn...  4.91 us
    ppermute x1, starting transfers between devices, extended(): lax.ppermute(lax.slice_in_dim(block, block.shape[dim] - width, None, axis...  4.81 us
    dot_general x1, matrix products, attend_backward(): jnp.einsum('nhqk,nqhd->nkhd', weight_b, grad4, preferred_element_type=jnp...  4.78 us
    reshape x4, local copies, waits for them, and re-layouts, windows_of(): return jnp.stack(slabs, 1).reshape(block_count, window_len, HEADS, HSZ)  4.33 us
  transfers between devices with their start and end apart: 13, of which 1 were waited for; matrix products, arithmetic and copies ran while one was open for 27% of the time, Pallas kernels for 0%

commit v1 on v0

v1 whole, which is shorter than its diff:
```python
import functools

import jax
import jax.numpy as jnp
from jax import lax
from jax.experimental import pallas as pl
from jax.experimental.pallas import tpu as pltpu
from jax.sharding import PartitionSpec as P

HEADS = 8
HSZ = 64
BLK = 24
KW = 7
HALF = KW // 2
BACK = 2 * BLK
AHEAD = 32
EDGE = 16
TILE = 4 * BLK
REACH = 176
GROUP = 4
FEATS = GROUP * HSZ
LANES = GROUP * TILE
NEG = -1e30
BF = jnp.bfloat16
F32 = jnp.float32
VMEM = pl.BlockSpec(memory_space=pltpu.VMEM)
SMEM = pl.BlockSpec(memory_space=pltpu.SMEM)
ANY = pl.BlockSpec(memory_space=pl.ANY)


def nt(a, b):
    return lax.dot_general(a, b, (((1,), (1,)), ((), ())), preferred_element_type=F32)


def nn(a, b):
    return lax.dot_general(a, b, (((1,), (0,)), ((), ())), preferred_element_type=F32)


def tn(a, b):
    return lax.dot_general(a, b, (((0,), (0,)), ((), ())), preferred_element_type=F32)


def call(kernel, outs, ins, args, scratch=(), flops=0, moved=0):
    return pl.pallas_call(
        kernel,
        out_shape=outs,
        in_specs=ins,
        out_specs=jax.tree.map(lambda _: VMEM, outs),
        scratch_shapes=scratch,
        compiler_params=pltpu.CompilerParams(vmem_limit_bytes=40 * 1024 * 1024),
        cost_estimate=pl.CostEstimate(flops=flops, bytes_accessed=moved, transcendentals=0),
    )(*args)


def shape(dims, kind):
    return jax.ShapeDtypeStruct(dims, kind)


def pack_kernel(k, v, g, w, ahead, behind, w_half, sems):
    rows, feats = k.shape
    half = w.shape[0] // 2
    core = lax.rem(lax.axis_index("dp"), 2)
    tail = rows - BACK
    pairs = [
        (k.at[pl.ds(tail, BACK)], ahead.at[pl.ds(0, BACK)]),
        (v.at[pl.ds(tail, BACK)], ahead.at[pl.ds(BACK, BACK)]),
        (k.at[pl.ds(0, AHEAD)], behind.at[pl.ds(0, AHEAD)]),
        (v.at[pl.ds(0, AHEAD)], behind.at[pl.ds(AHEAD, AHEAD)]),
        (w.at[pl.ds(pl.multiple_of(core * half, half), half)], w_half),
    ]
    for part in range(2):
        cols = pl.ds(part * feats, feats)
        at = part * EDGE
        pairs.append((g.at[pl.ds(rows - EDGE, EDGE), cols], ahead.at[pl.ds(2 * BACK + at, EDGE)]))
        pairs.append((g.at[pl.ds(0, EDGE), cols], behind.at[pl.ds(2 * AHEAD + at, EDGE)]))
    copies = [pltpu.make_async_copy(a, b, sems.at[i]) for i, (a, b) in enumerate(pairs)]
    for copy in copies:
        copy.start()
    for copy in copies:
        copy.wait()


def packed(k, v, g, w):
    feats = k.shape[1]
    outs = (
        shape((2 * BACK + 2 * EDGE, feats), BF),
        shape((2 * AHEAD + 2 * EDGE, feats), BF),
        shape((w.shape[0] // 2, w.shape[1]), BF),
    )
    return pl.pallas_call(
        pack_kernel,
        out_shape=outs,
        in_specs=[ANY] * 4,
        out_specs=(ANY,) * 3,
        scratch_shapes=[pltpu.SemaphoreType.DMA((9,))],
    )(k, v, g, w)


def head_of(dims):
    return lax.broadcasted_iota(jnp.int32, dims, 1) // HSZ


def stacked(tile, amount):
    head = head_of((1, FEATS))
    return jnp.concatenate(
        [tile * jnp.where(head == h, amount, 0.0).astype(BF) for h in range(GROUP)], 0
    )


def unstacked(product):
    head = head_of((TILE, FEATS))
    out = product[:TILE]
    for h in range(1, GROUP):
        out = jnp.where(head == h, product[h * TILE : (h + 1) * TILE], out)
    return out


def fill_ext(ext, before, local, after):
    rows = local.shape[0]
    ext[0:BACK] = before
    ext[BACK : BACK + rows] = local[...]
    ext[BACK + rows : BACK + rows + AHEAD] = after


def allowed_in(tile, base, length, back, ahead):
    lane = lax.broadcasted_iota(jnp.int32, (1, LANES), 1)
    within = lane
    for h in range(1, GROUP):
        within = within - jnp.where(lane >= h * TILE, TILE, 0)
    block = jnp.zeros_like(lane)
    for b in range(1, TILE // BLK):
        block = block + jnp.where(within >= b * BLK, 1, 0)
    origin = base + tile * TILE - BACK
    low = jnp.maximum((block + 2 - back) * BLK, -origin)
    high = jnp.minimum((block + 3 + ahead) * BLK, length - origin)
    row = lax.broadcasted_iota(jnp.int32, (REACH, LANES), 0)
    return (row >= low) & (row < high)


def probabilities(key_tile, query_stack, allowed):
    scores = jnp.where(allowed, nt(key_tile, query_stack), NEG)
    terms = jnp.exp(scores - jnp.max(scores, axis=0, keepdims=True))
    return terms * (1.0 / jnp.sum(terms, axis=0, keepdims=True))


def fill_grad(gx, g, near, far, base, length):
    rows, width = g.shape
    feats = width // 2

    def masked(block, start):
        frame = start + lax.broadcasted_iota(jnp.int32, block.shape, 0)
        return jnp.where(frame < length, block.astype(F32), 0.0)

    for part in range(2):
        cols = slice(part * feats, (part + 1) * feats)
        top = 2 * BACK + part * EDGE
        low = 2 * AHEAD + part * EDGE
        gx[0:8, cols] = masked(near[top : top + EDGE].astype(F32)[8:], base - 8)
        gx[8 + rows : 16 + rows, cols] = masked(far[low : low + EDGE].astype(F32)[:8], base + rows)
    gx[8 : 8 + rows, :] = masked(g[...], base)


def forward_kernel(
    q, k, v, near, far, g, taps, lengths, offsets,
    stream_grad, send, keep, att_out, kx, vx, gx, att_t,
):
    rows, feats = q.shape
    width = g.shape[1]
    place = lax.axis_index("cp")
    core = lax.rem(lax.axis_index("dp"), 2)
    base = place * rows
    length = lengths[0]
    fill_ext(kx, near[0:BACK], k, far[0:AHEAD])
    fill_ext(vx, near[BACK : 2 * BACK], v, far[AHEAD : 2 * AHEAD])
    for tile in range(rows // TILE):
        start = tile * TILE
        allowed = allowed_in(tile, base, length, offsets[0, 0], offsets[0, 1])
        frame = base + start + lax.broadcasted_iota(jnp.int32, (TILE, FEATS), 0)
        for group in range(feats // FEATS):
            cols = slice(group * FEATS, (group + 1) * FEATS)
            query_stack = stacked(q[start : start + TILE, cols], HSZ**-0.5)
            probs = probabilities(kx[start : start + REACH, cols], query_stack, allowed)
            product = tn(probs.astype(BF), vx[start : start + REACH, cols])
            attended = jnp.where(frame < length, unstacked(product), 0.0).astype(BF)
            att_out[start : start + TILE, cols] = attended
    att_t[...] = att_out[...].astype(F32).T.astype(BF)
    fill_grad(gx, g, near, far, base, length)
    step = 128
    frame = base + lax.broadcasted_iota(jnp.int32, (rows, step), 0)
    for at in range(0, width, step):
        cols = slice(at, at + step)
        total = taps[0:1, cols] * gx[8 + HALF : 8 + HALF + rows, cols]
        for tap in range(1, KW):
            top = 8 + HALF - tap
            total = total + taps[tap : tap + 1, cols] * gx[top : top + rows, cols]
        stream_grad[:, cols] = jnp.where(frame < length, total, 0.0).astype(BF)
    half = send.shape[1]
    for part in range(send.shape[0]):
        there = pl.multiple_of(2 * half * part + half * (1 - core), half)
        here = pl.multiple_of(2 * half * part + half * core, half)
        send[part] = nn(att_t[pl.ds(there, half)], stream_grad[...]).astype(BF)
        keep[part] = nn(att_t[pl.ds(here, half)], stream_grad[...])


def split_kernel(parts, keep, got, own, *pieces):
    place = lax.axis_index("cp")
    own[...] = keep[place] + got[place].astype(F32)
    for k, piece in enumerate(pieces, 1):
        at = lax.bitwise_xor(place, k)
        piece[...] = (keep[at] + got[at].astype(F32)).astype(BF)


def tree_sum(terms):
    while len(terms) > 1:
        terms = [a + b for a, b in zip(terms[::2], terms[1::2])]
    return terms[0]


def rescatter_kernel(count, own, *refs):
    got, outs = refs[: count - 1], refs[count - 1 :]
    total = own[...]
    for ref in got:
        total = total + ref[...].astype(F32)
    (mine, *pieces), hold = outs[:-1], outs[-1]
    hold[...] = total
    chunk = mine.shape[0]
    floor = lax.div(lax.axis_index("dp"), 2)
    mine[...] = hold[pl.ds(pl.multiple_of(floor * chunk, chunk), chunk)]
    for k, piece in enumerate(pieces, 1):
        at = lax.bitwise_xor(floor, k)
        piece[...] = hold[pl.ds(pl.multiple_of(at * chunk, chunk), chunk)].astype(BF)


def chunk_kernel(count, own, *refs):
    total = own[...]
    for ref in refs[: count - 1]:
        total = total + ref[...].astype(F32)
    refs[-1][...] = total.astype(BF)


def final_kernel(count, *refs):
    mine, theirs = refs[:count], refs[count : 2 * count]
    conv_here, conv_there, weight_grad, conv_grad = refs[2 * count :]
    chunk = mine[0].shape[0]
    half = chunk * count
    core = lax.rem(lax.axis_index("dp"), 2)
    floor = lax.div(lax.axis_index("dp"), 2)
    for side, group in ((core, mine), (1 - core, theirs)):
        for k, ref in enumerate(group):
            at = side * half + lax.bitwise_xor(floor, k) * chunk
            weight_grad[pl.ds(pl.multiple_of(at, chunk), chunk)] = ref[...].astype(F32)
    conv_grad[...] = (conv_here[...] + conv_there[...])[:KW]


def backward_kernel(
    count, q, k, v, near, far, g, stream, stream_grad, att, w, lengths, offsets, *refs
):
    got = refs[: count - 1]
    passed = refs[count - 1 : 2 * count - 2]
    query_g, key_g, value_g, key_up, key_down, conv, kx, vx, gx, wx, kg, vg, mixed, ag = refs[2 * count - 2 :]
    rows, feats = q.shape
    width = g.shape[1]
    place = lax.axis_index("cp")
    core = lax.rem(lax.axis_index("dp"), 2)
    base = place * rows
    length = lengths[0]
    shard = w.shape[0]
    half = shard // 2
    wx[pl.ds(pl.multiple_of(place * shard, shard), shard)] = w[...]
    for k_at, (a, b) in enumerate(zip(got, passed), 1):
        at = lax.bitwise_xor(place, k_at) * shard
        wx[pl.ds(pl.multiple_of(at + core * half, half), half)] = a[...]
        wx[pl.ds(pl.multiple_of(at + (1 - core) * half, half), half)] = b[...]
    ag[...] = nt(stream_grad[...], wx[...]).astype(BF)
    fill_ext(kx, near[0:BACK], k, far[0:AHEAD])
    fill_ext(vx, near[BACK : 2 * BACK], v, far[AHEAD : 2 * AHEAD])
    kg[...] = jnp.zeros_like(kg)
    vg[...] = jnp.zeros_like(vg)
    for tile in range(rows // TILE):
        start = tile * TILE
        allowed = allowed_in(tile, base, length, offsets[0, 0], offsets[0, 1])
        span = slice(start, start + REACH)
        for group in range(feats // FEATS):
            cols = slice(group * FEATS, (group + 1) * FEATS)
            query_stack = stacked(q[start : start + TILE, cols], HSZ**-0.5)
            grad_stack = stacked(ag[start : start + TILE, cols], 1.0)
            probs = probabilities(kx[span, cols], query_stack, allowed)
            dprob = nt(vx[span, cols], grad_stack)
            inner = jnp.sum(probs * dprob, axis=0, keepdims=True)
            dscore = (probs * (dprob - inner)).astype(BF)
            query_g[start : start + TILE, cols] = (
                unstacked(tn(dscore, kx[span, cols])) * HSZ**-0.5
            ).astype(BF)
            kg[span, cols] += nn(dscore, query_stack)
            vg[span, cols] += nn(probs.astype(BF), grad_stack)
    key_g[...] = kg[BACK : BACK + rows]
    value_g[...] = vg[BACK : BACK + rows]
    key_up[0:BACK] = kg[0:BACK].astype(BF)
    key_up[BACK : 2 * BACK] = vg[0:BACK].astype(BF)
    key_down[0:AHEAD] = kg[BACK + rows : BACK + rows + AHEAD].astype(BF)
    key_down[AHEAD : 2 * AHEAD] = vg[BACK + rows : BACK + rows + AHEAD].astype(BF)
    fill_grad(gx, g, near, far, base, length)
    step = 128
    frame = base + lax.broadcasted_iota(jnp.int32, (rows, width), 0)
    total = stream[...].astype(F32) + nn(att[...], wx[...])
    mixed[...] = jnp.where(frame < length, total, 0.0)
    conv[KW:] = jnp.zeros((8 - KW, width), F32)
    for at in range(0, width, step):
        cols = slice(at, at + step)
        block = mixed[:, cols]
        for tap in range(KW):
            top = 8 + HALF - tap
            conv[tap : tap + 1, cols] = jnp.sum(
                block * gx[top : top + rows, cols], axis=0, keepdims=True
            )


def join_kernel(key_g, value_g, up, down, key_out, value_out):
    rows = key_g.shape[0]
    for at, grad, out in ((0, key_g, key_out), (1, value_g, value_out)):
        first = down[at * AHEAD : (at + 1) * AHEAD].astype(F32)
        last = up[at * BACK : (at + 1) * BACK].astype(F32)
        out[0:AHEAD] = (grad[0:AHEAD] + first).astype(BF)
        out[AHEAD : rows - BACK] = grad[AHEAD : rows - BACK].astype(BF)
        out[rows - BACK :] = (grad[rows - BACK :] + last).astype(BF)


def conv_sum_kernel(*refs):
    refs[-1][...] = tree_sum([ref[...] for ref in refs[:-1]])


def body(
    queries, key_rows, value_rows, stream_in, out_grad, out_weight, conv_weight, lengths, offsets
):
    rows, feats = queries.shape[1:]
    width = stream_in.shape[2]
    cps, dps = lax.axis_size("cp"), lax.axis_size("dp")
    floors = dps // 2
    q, k, v, g, stream = queries[0], key_rows[0], value_rows[0], out_grad[0], stream_in[0]
    shard = out_weight.shape[0]
    half = shard // 2
    up = [(i, i + 1) for i in range(cps - 1)]
    down = [(i + 1, i) for i in range(cps - 1)]
    other_core = [(i, i ^ 1) for i in range(dps)]

    def over_cp(array, by):
        return lax.ppermute(array, "cp", [(i, i ^ by) for i in range(cps)])

    def over_z(array, by):
        return lax.ppermute(array, "dp", [(i, i ^ (2 * by)) for i in range(dps)])

    def over_core(array):
        return lax.ppermute(array, "dp", other_core)

    ahead, behind, w_half = packed(k, v, g, out_weight)
    near = lax.ppermute(ahead, "cp", up)
    far = lax.ppermute(behind, "cp", down)
    w_got = [over_cp(w_half, by) for by in range(1, cps)]
    ext = rows + BACK + AHEAD
    stream_grad, send, keep, att = call(
        forward_kernel,
        (
            shape((rows, width), BF),
            shape((cps, half, width), BF),
            shape((cps, half, width), F32),
            shape((rows, feats), BF),
        ),
        [VMEM] * 7 + [SMEM] * 2,
        (q, k, v, near, far, g, conv_weight, lengths, offsets),
        [
            pltpu.VMEM((ext, feats), BF),
            pltpu.VMEM((ext, feats), BF),
            pltpu.VMEM((rows + 16, width), F32),
            pltpu.VMEM((feats, rows), BF),
        ],
        flops=2 * rows * feats * width,
        moved=6 * 2**20,
    )
    w_passed = [over_core(part) for part in w_got]
    core_got = over_core(send)
    own, *pieces = call(
        functools.partial(split_kernel, cps),
        (shape((half, width), F32),) + (shape((half, width), BF),) * (cps - 1),
        [VMEM] * 2,
        (keep, core_got),
        moved=3 * 2**20,
    )
    cp_got = [over_cp(piece, by) for by, piece in enumerate(pieces, 1)]
    query_g, key_g, value_g, key_up, key_down, conv = call(
        functools.partial(backward_kernel, cps),
        (
            shape((rows, feats), BF),
            shape((rows, feats), F32),
            shape((rows, feats), F32),
            shape((2 * BACK, feats), BF),
            shape((2 * AHEAD, feats), BF),
            shape((8, width), F32),
        ),
        [VMEM] * 10 + [SMEM] * 2 + [VMEM] * (2 * cps - 2),
        (q, k, v, near, far, g, stream, stream_grad, att, out_weight, lengths, offsets)
        + tuple(w_got)
        + tuple(w_passed),
        [
            pltpu.VMEM((ext, feats), BF),
            pltpu.VMEM((ext, feats), BF),
            pltpu.VMEM((rows + 16, width), F32),
            pltpu.VMEM((feats, width), BF),
            pltpu.VMEM((ext, feats), F32),
            pltpu.VMEM((ext, feats), F32),
            pltpu.VMEM((rows, width), F32),
            pltpu.VMEM((rows, feats), BF),
        ],
        flops=4 * rows * feats * width,
        moved=8 * 2**20,
    )
    from_up = lax.ppermute(key_up, "cp", down)
    from_down = lax.ppermute(key_down, "cp", up)
    conv_cp = call(
        conv_sum_kernel,
        shape((8, width), F32),
        [VMEM] * cps,
        (conv, *[over_cp(conv, by) for by in range(1, cps)]),
    )
    if floors != 4 or half % (16 * floors):
        summed = own
        for got in cp_got:
            summed = summed + got.astype(F32)
        at = (lax.axis_index("dp") % 2) * half
        whole = lax.dynamic_update_slice(jnp.zeros((shard, width), F32), summed, (at, 0))
        weight_grad = lax.psum(whole, "dp")
        conv_grad = lax.psum(conv_cp, "dp")[:KW]
    else:
        chunk = half // floors
        mine, *z_pieces = call(
            lambda *refs: rescatter_kernel(cps, *refs),
            (shape((chunk, width), F32),) + (shape((chunk, width), BF),) * (floors - 1),
            [VMEM] * cps,
            (own, *cp_got),
            [pltpu.VMEM((half, width), F32)],
            moved=2**20,
        )
        z_got = [over_z(piece, by) for by, piece in enumerate(z_pieces, 1)]
        conv_z = call(
            conv_sum_kernel,
            shape((8, width), F32),
            [VMEM] * floors,
            (conv_cp, *[over_z(conv_cp, by) for by in range(1, floors)]),
        )
        final = call(
            lambda *refs: chunk_kernel(floors, *refs),
            shape((chunk, width), BF),
            [VMEM] * floors,
            (mine, *z_got),
        )
        here = [final] + [over_z(final, by) for by in range(1, floors)]
        there = [over_core(part) for part in here]
        weight_grad, conv_grad = call(
            lambda *refs: final_kernel(floors, *refs),
            (shape((shard, width), F32), shape((KW, width), F32)),
            [VMEM] * (2 * floors + 2),
            (*here, *there, conv_z, over_core(conv_z)),
        )
    key_grad, value_grad = call(
        join_kernel,
        (shape((rows, feats), BF),) * 2,
        [VMEM] * 4,
        (key_g, value_g, from_up, from_down),
        moved=2**20,
    )
    return (
        query_g[None],
        key_grad[None],
        value_grad[None],
        stream_grad[None],
        weight_grad,
        conv_grad,
    )


def solution(mesh):
    rows_spec = P("dp", "cp", None)
    return jax.shard_map(
        body,
        mesh=mesh,
        in_specs=(rows_spec,) * 5 + (P("cp", None), P(), P("dp"), P("dp", None)),
        out_specs=(rows_spec,) * 4 + (P("cp", None), P()),
        check_vma=False,
    )
```

time: 203 us -> 77.5 us (0.38)
  blocking collectives: 41.4 us -> 0 us
  waiting for transfers between devices: 56 us -> 15.9 us
  local copies, waits for them, and re-layouts: 28 us -> 0.04 us
  Pallas kernels: 0 us -> 22.2 us
  matrix products: 18.9 us -> 0 us
  between operations: 15.6 us -> 1.55 us
  other arithmetic: 9.88 us -> 0 us
  starting transfers between devices: 32.4 us -> 37.5 us
    psum x1 -> x0, waiting for transfers between devices: 55.3 us -> none  [body(): weight_grad = lax.psum(weight_part, 'dp')]
    psum x1 -> x0, blocking collectives: 41.4 us -> none  [body(): conv_grad = lax.psum(conv_local, ('cp', 'dp'))]
    pallas_call x0 -> x10, Pallas kernels: none -> 22.2 us  [the longest x1 12.1 us: packed(): pl.pallas_call(pack_kernel, out_shape=outs, in_specs=[ANY] * 4, out_specs...]
    dot_general x9 -> x0, matrix products: 18.9 us -> none  [the longest x1 4.91 us: attend_forward(): jnp.einsum('nhqk,nkhd->nqhd', weight_b, value4, preferred_element_type=jn...]
    ppermute x10 -> x31, waiting for transfers between devices: 0.03 us -> 15.9 us  [the longest x9 6.05 us: over_cp(): return lax.ppermute(array, 'cp', [(i, i ^ by) for i in range(cps)])]
    reshape x8 -> x0, local copies, waits for them, and re-layouts: 10.5 us -> none  [the longest x2 5.76 us: fold_back(): parts = window_grad.reshape(block_count, 4, BLK, head_feats)]
    slice x10 -> x0, local copies, waits for them, and re-layouts: 5.5 us -> none  [the longest x1 1.31 us: body(): look_back = offsets[0, 0]]
    ppermute x10 -> x31, starting transfers between devices: 32.1 us -> 37.5 us  [the longest x9 13.3 us: over_z(): return lax.ppermute(array, 'dp', [(i, i ^ 2 * by) for i in range(dps)])]
  transfers between devices with their start and end apart: 13 -> 31, of which waited for: 1 -> 6; matrix products, arithmetic and copies ran while one was open for 27% -> 0% of each run, Pallas kernels for 0% -> 7%
where the time goes in v1:
time: 77.5 us; the launch traced here: 77.3 us
  starting transfers between devices  37.5 us (48%)
  Pallas kernels  22.2 us (29%)
  waiting for transfers between devices  15.9 us (21%)
  between operations  1.55 us (2%)
    ppermute x9, starting transfers between devices, over_z(): return lax.ppermute(array, 'dp', [(i, i ^ 2 * by) for i in range(dps)])  13.3 us
    pallas_call x1, Pallas kernels, packed(): pl.pallas_call(pack_kernel, out_shape=outs, in_specs=[ANY] * 4, out_specs...  12.1 us
    ppermute x9, starting transfers between devices, over_cp(): return lax.ppermute(array, 'cp', [(i, i ^ by) for i in range(cps)])  10.7 us
    pallas_call x9, Pallas kernels, call(): pl.pallas_call(kernel, out_shape=outs, in_specs=ins, out_specs=jax.tree.m...  10.1 us
    ppermute x9, waiting for transfers between devices, over_cp(): return lax.ppermute(array, 'cp', [(i, i ^ by) for i in range(cps)])  6.05 us
    ppermute x1, waiting for transfers between devices, body(): far = lax.ppermute(behind, 'cp', down)  5.03 us
    ppermute x1, starting transfers between devices, body(): near = lax.ppermute(ahead, 'cp', up)  4.85 us
    ppermute x9, waiting for transfers between devices, over_z(): return lax.ppermute(array, 'dp', [(i, i ^ 2 * by) for i in range(dps)])  4.78 us
  transfers between devices with their start and end apart: 31, of which 6 were waited for; matrix products, arithmetic and copies ran while one was open for 0% of the time, Pallas kernels for 7%

profile of v1, /device:TPU:0, one launch (start us, length us, event | category | flops | bytes accessed | tf_op | source)
XLA Modules:
  0.0 77.3 jit_solution(5689203012632022458)
XLA Ops:
  0.7 12.1 %shard_map.136 = (bf16[128,512]{1,0:T(8,128)(2,1)}, bf16[96,512]{1,0:T(8,128)(2,1)}, bf16[64,1024]{1,0:T(8,128)(2,1)}) custom-call(bf16[192,512]{1,0:T(8,128)(2,1)} %bitcast.12, bf16[192,512]{1,0:T(8,128)(2,1)} %bitcast.15, bf16[192,1024]{1,0:T(8,128)(2,1)} %bitcast.9, bf16[128,1024]{1,0:T(8,128)(2,1)} %w.3), custom_call_target="tpu_custom_call" | custom-call | tf_op jit(solution)/shard_map/pallas_call | solution.py:90
  12.8 4.8 %collective-permute-start = (bf16[128,512]{1,0:T(8,128)(2,1)}, bf16[128,512]{1,0:T(8,128)(2,1)S(1)}, u32[]{:S(2)}, u32[]{:S(2)}) collective-permute-start(bf16[128,512]{1,0:T(8,128)(2,1)} %get-tuple-element.31), channel_id=1, source_target_pairs={{0,8},{8,16},{16,24},{1,9},{9,17},{17,25},{2,10},{10,18},{18,26},{... | collective-permute-start | bytes 393224 | tf_op jit(solution)/shard_map/ppermute | solution.py:356
  17.6 1.3 %collective-permute-start.1 = (bf16[96,512]{1,0:T(8,128)(2,1)}, bf16[96,512]{1,0:T(8,128)(2,1)S(1)}, u32[]{:S(2)}, u32[]{:S(2)}) collective-permute-start(bf16[96,512]{1,0:T(8,128)(2,1)} %get-tuple-element.32), channel_id=1, source_target_pairs={{8,0},{16,8},{24,16},{9,1},{17,9},{25,17},{10,2},{18,10},{26,18},{... | collective-permute-start | bytes 294920 | tf_op jit(solution)/shard_map/ppermute | solution.py:357
  19.6 5.0 %collective-permute-done.1.far = bf16[96,512]{1,0:T(8,128)(2,1)S(1)} collective-permute-done((bf16[96,512]{1,0:T(8,128)(2,1)}, bf16[96,512]{1,0:T(8,128)(2,1)S(1)}, u32[]{:S(2)}, u32[]{:S(2)}) %collective-permute-start.1) | collective-permute-done | bytes 98336 | tf_op jit(solution)/shard_map/ppermute | solution.py:357
  24.7 4.0 %shard_map.137 = (bf16[192,1024]{1,0:T(8,128)(2,1)}, bf16[4,64,1024]{2,1,0:T(8,128)(2,1)S(1)}, f32[4,64,1024]{2,1,0:T(8,128)S(1)}, bf16[192,512]{1,0:T(8,128)(2,1)S(1)}) custom-call(bf16[192,512]{1,0:T(8,128)(2,1)S(1)} %bitcast.18, bf16[192,512]{1,0:T(8,128)(2,1)S(1)} %bitcast.13, bf16[192,512]{1,0:T(8,128)(2,1)S(1)} %bitcast.16, ...), custom_call_target="tpu_custom_call" | custom-call | flops 201326592 | bytes 6291456 | tf_op jit(solution)/shard_map/pallas_call | solution.py:44
  29.1 3.2 %collective-permute-start.3 = (bf16[64,1024]{1,0:T(8,128)(2,1)S(1)}, bf16[64,1024]{1,0:T(8,128)(2,1)S(1)}, u32[]{:S(2)}, u32[]{:S(2)}) collective-permute-start(bf16[64,1024]{1,0:T(8,128)(2,1)S(1)} %copy-done.9), channel_id=1, source_target_pairs={{0,16},{8,24},{16,0},{24,8},{1,17},{9,25},{17,1},{25,9},{2,18},{10... | collective-permute-start | bytes 393224 | tf_op jit(solution)/shard_map/ppermute | solution.py:347
  32.3 3.6 %collective-permute-done.4.refs_2_ = bf16[64,1024]{1,0:T(8,128)(2,1)S(1)} collective-permute-done((bf16[64,1024]{1,0:T(8,128)(2,1)S(1)}, bf16[64,1024]{1,0:T(8,128)(2,1)S(1)}, u32[]{:S(2)}, u32[]{:S(2)}) %collective-permute-start.4) | collective-permute-done | bytes 131104 | tf_op jit(solution)/shard_map/ppermute | solution.py:347
  35.9 2.4 %collective-permute-done.3.refs_1_ = bf16[64,1024]{1,0:T(8,128)(2,1)S(1)} collective-permute-done((bf16[64,1024]{1,0:T(8,128)(2,1)S(1)}, bf16[64,1024]{1,0:T(8,128)(2,1)S(1)}, u32[]{:S(2)}, u32[]{:S(2)}) %collective-permute-start.3) | collective-permute-done | bytes 131104 | tf_op jit(solution)/shard_map/ppermute | solution.py:347
  39.0 1.6 %collective-permute-start.11 = (bf16[64,1024]{1,0:T(8,128)(2,1)S(1)}, bf16[64,1024]{1,0:T(8,128)(2,1)S(1)}, u32[]{:S(2)}, u32[]{:S(2)}) collective-permute-start(bf16[64,1024]{1,0:T(8,128)(2,1)S(1)} %get-tuple-element.46), channel_id=1, source_target_pairs={{0,8},{8,0},{16,24},{24,16},{1,9},{9,1},{17,25},{25,17},{2,10},{10... | collective-permute-start | bytes 393224 | tf_op jit(solution)/shard_map/ppermute | solution.py:347
  41.3 1.3 %collective-permute-start.13 = (bf16[64,1024]{1,0:T(8,128)(2,1)S(1)}, bf16[64,1024]{1,0:T(8,128)(2,1)S(1)}, u32[]{:S(2)}, u32[]{:S(2)}) collective-permute-start(bf16[64,1024]{1,0:T(8,128)(2,1)S(1)} %get-tuple-element.48), channel_id=1, source_target_pairs={{0,24},{8,16},{16,8},{24,0},{1,25},{9,17},{17,9},{25,1},{2,26},{10... | collective-permute-start | bytes 393224 | tf_op jit(solution)/shard_map/ppermute | solution.py:347
  42.5 4.3 %shard_map.138 = (bf16[192,512]{1,0:T(8,128)(2,1)}, f32[192,512]{1,0:T(8,128)S(1)}, f32[192,512]{1,0:T(8,128)S(1)}, bf16[96,512]{1,0:T(8,128)(2,1)S(1)}, bf16[64...) custom-call(bf16[192,512]{1,0:T(8,128)(2,1)S(1)} %bitcast.19, bf16[192,512]{1,0:T(8,128)(2,1)S(1)} %bitcast.14, ...), custom_call_target="tpu_custom_call" | custom-call | flops 402653184 | bytes 8388608 | tf_op jit(solution)/shard_map/pallas_call | solution.py:44
  46.8 1.7 %collective-permute-start.26 = (f32[8,1024]{1,0:T(8,128)S(1)}, f32[8,1024]{1,0:T(8,128)S(1)}, u32[]{:S(2)}, u32[]{:S(2)}) collective-permute-start(f32[8,1024]{1,0:T(8,128)S(1)} %get-tuple-element.53.refs_0_), channel_id=1, source_target_pairs={{0,24},{8,16},{16,8},{24,0},{1,25},{9,17},{17,9},{25,1},{2,26},{10... | collective-permute-start | bytes 98312 | tf_op jit(solution)/shard_map/ppermute | solution.py:347
  48.5 1.3 %collective-permute-start.25 = (f32[8,1024]{1,0:T(8,128)S(1)}, f32[8,1024]{1,0:T(8,128)S(1)}, u32[]{:S(2)}, u32[]{:S(2)}) collective-permute-start(f32[8,1024]{1,0:T(8,128)S(1)} %get-tuple-element.53.refs_0_), channel_id=1, source_target_pairs={{0,16},{8,24},{16,0},{24,8},{1,17},{9,25},{17,1},{25,9},{2,18},{10... | collective-permute-start | bytes 98312 | tf_op jit(solution)/shard_map/ppermute | solution.py:347
  50.4 1.3 %collective-permute-start.8 = (bf16[96,512]{1,0:T(8,128)(2,1)S(1)}, bf16[96,512]{1,0:T(8,128)(2,1)S(1)}, u32[]{:S(2)}, u32[]{:S(2)}) collective-permute-start(bf16[96,512]{1,0:T(8,128)(2,1)S(1)} %get-tuple-element.39), channel_id=1, source_target_pairs={{8,0},{16,8},{24,16},{9,1},{17,9},{25,17},{10,2},{18,10},{26,18},{... | collective-permute-start | bytes 294920 | tf_op jit(solution)/shard_map/ppermute | solution.py:416
  51.8 1.6 %collective-permute-start.14 = (bf16[16,1024]{1,0:T(8,128)(2,1)S(1)}, bf16[16,1024]{1,0:T(8,128)(2,1)S(1)}, u32[]{:S(2)}, u32[]{:S(2)}) collective-permute-start(bf16[16,1024]{1,0:T(8,128)(2,1)S(1)} %get-tuple-element.50), channel_id=1, source_target_pairs={{0,2},{1,3},{2,0},{3,1},{4,6},{5,7},{6,4},{7,5},{8,10},{9,11},{10,... | collective-permute-start | bytes 98312 | tf_op jit(solution)/shard_map/ppermute | solution.py:350
  53.4 2.6 %collective-permute-start.15 = (bf16[16,1024]{1,0:T(8,128)(2,1)S(1)}, bf16[16,1024]{1,0:T(8,128)(2,1)S(1)}, u32[]{:S(2)}, u32[]{:S(2)}) collective-permute-start(bf16[16,1024]{1,0:T(8,128)(2,1)S(1)} %get-tuple-element.51), channel_id=1, source_target_pairs={{0,4},{1,5},{2,6},{3,7},{4,0},{5,1},{6,2},{7,3},{8,12},{9,13},{10,... | collective-permute-start | bytes 98312 | tf_op jit(solution)/shard_map/ppermute | solution.py:350
  56.2 4.5 %collective-permute-start.9 = (bf16[64,512]{1,0:T(8,128)(2,1)S(1)}, bf16[64,512]{1,0:T(8,128)(2,1)S(1)}, u32[]{:S(2)}, u32[]{:S(2)}) collective-permute-start(bf16[64,512]{1,0:T(8,128)(2,1)S(1)} %get-tuple-element.40), channel_id=1, source_target_pairs={{0,8},{8,16},{16,24},{1,9},{9,17},{17,25},{2,10},{10,18},{18,26},{... | collective-permute-start | bytes 196616 | tf_op jit(solution)/shard_map/ppermute | solution.py:417
  60.8 3.7 %collective-permute-start.29 = (f32[8,1024]{1,0:T(8,128)S(1)}, f32[8,1024]{1,0:T(8,128)S(1)}, u32[]{:S(2)}, u32[]{:S(2)}) collective-permute-start(f32[8,1024]{1,0:T(8,128)S(1)} %shard_map.143.refs_0_), channel_id=1, source_target_pairs={{0,6},{1,7},{2,4},{3,5},{4,2},{5,3},{6,0},{7,1},{8,14},{9,15},{10,... | collective-permute-start | bytes 98312 | tf_op jit(solution)/shard_map/ppermute | solution.py:350
  64.5 0.8 %collective-permute-start.27 = (f32[8,1024]{1,0:T(8,128)S(1)}, f32[8,1024]{1,0:T(8,128)S(1)}, u32[]{:S(2)}, u32[]{:S(2)}) collective-permute-start(f32[8,1024]{1,0:T(8,128)S(1)} %shard_map.143.refs_0_), channel_id=1, source_target_pairs={{0,2},{1,3},{2,0},{3,1},{4,6},{5,7},{6,4},{7,5},{8,10},{9,11},{10,... | collective-permute-start | bytes 98312 | tf_op jit(solution)/shard_map/ppermute | solution.py:350
  65.3 1.3 %collective-permute-done.29.refs_3_ = f32[8,1024]{1,0:T(8,128)S(1)} collective-permute-done((f32[8,1024]{1,0:T(8,128)S(1)}, f32[8,1024]{1,0:T(8,128)S(1)}, u32[]{:S(2)}, u32[]{:S(2)}) %collective-permute-start.29) | collective-permute-done | bytes 32800 | tf_op jit(solution)/shard_map/ppermute | solution.py:350
  66.6 3.7 %collective-permute-start.19 = (bf16[16,1024]{1,0:T(8,128)(2,1)S(1)}, bf16[16,1024]{1,0:T(8,128)(2,1)S(1)}, u32[]{:S(2)}, u32[]{:S(2)}) collective-permute-start(bf16[16,1024]{1,0:T(8,128)(2,1)S(1)} %shard_map.142.refs_0_), channel_id=1, source_target_pairs={{0,6},{1,7},{2,4},{3,5},{4,2},{5,3},{6,0},{7,1},{8,14},{9,15},{10,... | collective-permute-start | bytes 98312 | tf_op jit(solution)/shard_map/ppermute | solution.py:350
  72.3 2.8 %collective-permute-done.18.refs_2_ = bf16[16,1024]{1,0:T(8,128)(2,1)S(1)} collective-permute-done((bf16[16,1024]{1,0:T(8,128)(2,1)S(1)}, bf16[16,1024]{1,0:T(8,128)(2,1)S(1)}, u32[]{:S(2)}, u32[]{:S(2)}) %collective-permute-start.18) | collective-permute-done | bytes 32800 | tf_op jit(solution)/shard_map/ppermute | solution.py:350
  75.6 0.8 %shard_map.139 = (bf16[192,512]{1,0:T(8,128)(2,1)}, bf16[192,512]{1,0:T(8,128)(2,1)}) custom-call(f32[192,512]{1,0:T(8,128)S(1)} %get-tuple-element.37.key_g, f32[192,512]{1,0:T(8,128)S(1)} %get-tuple-element.38.value_g, bf16[96,512]{1,0:T(8,128)(2,1)S(1)} %collective-permute-done.8.up, bf16[64,512]{1,0:T(8,128)(2,1)S(1)} %collective-permute-done.9.down), custom_call_target="tpu_custom_call" | custom-call | bytes 1048576 | tf_op jit(solution)/shard_map/pallas_call | solution.py:44
  76.4 0.8 %shard_map.145 = (f32[128,1024]{1,0:T(8,128)}, f32[7,1024]{1,0:T(8,128)}) custom-call(bf16[16,1024]{1,0:T(8,128)(2,1)S(1)} %shard_map.142.refs_0_, bf16[16,1024]{1,0:T(8,128)(2,1)S(1)} %collective-permute-done.17.refs_1_, bf16[16,1024]{1,0:T(8,128)(2,1)S(1)} %collective-permute-done.18.refs_2_, bf16[16,1024]{1,0:T(8,128)(2,1)S(1)} %collective-permute-done.19.refs_3_, ...), custom_call_target="tpu_custom_call" | custom-call | tf_op jit(solution)/shard_map/pallas_call | solution.py:44
  (68 shorter events, 5.3 us)
Async XLA Ops:
  12.8 11.9 %collective-permute-start = (bf16[128,512]{1,0:T(8,128)(2,1)}, bf16[128,512]{1,0:T(8,128)(2,1)S(1)}, u32[]{:S(2)}, u32[]{:S(2)}) collective-permute-start(bf16[128,512]{1,0:T(8,128)(2,1)} %get-tuple-element.31), channel_id=1, source_target_pairs={{0,8},{8,16},{16,24},{1,9},{9,17},{17,25},{2,10},{10,18},{18,26},{... | collective-permute-start | bytes 393224 | tf_op jit(solution)/shard_map/ppermute | solution.py:356
  17.6 7.0 %collective-permute-start.1 = (bf16[96,512]{1,0:T(8,128)(2,1)}, bf16[96,512]{1,0:T(8,128)(2,1)S(1)}, u32[]{:S(2)}, u32[]{:S(2)}) collective-permute-start(bf16[96,512]{1,0:T(8,128)(2,1)} %get-tuple-element.32), channel_id=1, source_target_pairs={{8,0},{16,8},{24,16},{9,1},{17,9},{25,17},{10,2},{18,10},{26,18},{... | collective-permute-start | bytes 294920 | tf_op jit(solution)/shard_map/ppermute | solution.py:357
  28.7 10.1 %collective-permute-start.10 = (bf16[4,64,1024]{2,1,0:T(8,128)(2,1)S(1)}, bf16[4,64,1024]{2,1,0:T(8,128)(2,1)S(1)}, u32[]{:S(2)}, u32[]{:S(2)}) collective-permute-start(bf16[4,64,1024]{2,1,0:T(8,128)(2,1)S(1)} %get-tuple-element.44), channel_id=1, source_target_pairs={{0,1},{1,0},{2,3},{3,2},{4,5},{5,4},{6,7},{7,6},{8,9},{9,8},{10,11... | collective-permute-start | bytes 1572872 | tf_op jit(solution)/shard_map/ppermute | solution.py:353
  28.7 7.2 %collective-permute-start.4 = (bf16[64,1024]{1,0:T(8,128)(2,1)S(1)}, bf16[64,1024]{1,0:T(8,128)(2,1)S(1)}, u32[]{:S(2)}, u32[]{:S(2)}) collective-permute-start(bf16[64,1024]{1,0:T(8,128)(2,1)S(1)} %copy-done.9), channel_id=1, source_target_pairs={{0,24},{8,16},{16,8},{24,0},{1,25},{9,17},{17,9},{25,1},{2,26},{10... | collective-permute-start | bytes 393224 | tf_op jit(solution)/shard_map/ppermute | solution.py:347
  29.1 9.2 %collective-permute-start.3 = (bf16[64,1024]{1,0:T(8,128)(2,1)S(1)}, bf16[64,1024]{1,0:T(8,128)(2,1)S(1)}, u32[]{:S(2)}, u32[]{:S(2)}) collective-permute-start(bf16[64,1024]{1,0:T(8,128)(2,1)S(1)} %copy-done.9), channel_id=1, source_target_pairs={{0,16},{8,24},{16,0},{24,8},{1,17},{9,25},{17,1},{25,9},{2,18},{10... | collective-permute-start | bytes 393224 | tf_op jit(solution)/shard_map/ppermute | solution.py:347
  32.3 6.1 %collective-permute-start.2 = (bf16[64,1024]{1,0:T(8,128)(2,1)S(1)}, bf16[64,1024]{1,0:T(8,128)(2,1)S(1)}, u32[]{:S(2)}, u32[]{:S(2)}) collective-permute-start(bf16[64,1024]{1,0:T(8,128)(2,1)S(1)} %copy-done.9), channel_id=1, source_target_pairs={{0,8},{8,0},{16,24},{24,16},{1,9},{9,1},{17,25},{25,17},{2,10},{10... | collective-permute-start | bytes 393224 | tf_op jit(solution)/shard_map/ppermute | solution.py:347
  35.9 5.3 %collective-permute-start.7 = (bf16[64,1024]{1,0:T(8,128)(2,1)S(1)}, bf16[64,1024]{1,0:T(8,128)(2,1)S(1)}, u32[]{:S(2)}, u32[]{:S(2)}) collective-permute-start(bf16[64,1024]{1,0:T(8,128)(2,1)S(1)} %collective-permute-done.4.refs_2_), channel_id=1, source_target_pairs={{0,1},{1,0},{2,3},{3,2},{4,5},{5,4},{6,7},{7,6},{8,9},{9,8},{10,11... | collective-permute-start | bytes 393224 | tf_op jit(solution)/shard_map/ppermute | solution.py:353
  39.0 10.9 %collective-permute-start.11 = (bf16[64,1024]{1,0:T(8,128)(2,1)S(1)}, bf16[64,1024]{1,0:T(8,128)(2,1)S(1)}, u32[]{:S(2)}, u32[]{:S(2)}) collective-permute-start(bf16[64,1024]{1,0:T(8,128)(2,1)S(1)} %get-tuple-element.46), channel_id=1, source_target_pairs={{0,8},{8,0},{16,24},{24,16},{1,9},{9,1},{17,25},{25,17},{2,10},{10... | collective-permute-start | bytes 393224 | tf_op jit(solution)/shard_map/ppermute | solution.py:347
  40.5 9.8 %collective-permute-start.12 = (bf16[64,1024]{1,0:T(8,128)(2,1)S(1)}, bf16[64,1024]{1,0:T(8,128)(2,1)S(1)}, u32[]{:S(2)}, u32[]{:S(2)}) collective-permute-start(bf16[64,1024]{1,0:T(8,128)(2,1)S(1)} %get-tuple-element.47), channel_id=1, source_target_pairs={{0,16},{8,24},{16,0},{24,8},{1,17},{9,25},{17,1},{25,9},{2,18},{10... | collective-permute-start | bytes 393224 | tf_op jit(solution)/shard_map/ppermute | solution.py:347
  41.3 10.4 %collective-permute-start.13 = (bf16[64,1024]{1,0:T(8,128)(2,1)S(1)}, bf16[64,1024]{1,0:T(8,128)(2,1)S(1)}, u32[]{:S(2)}, u32[]{:S(2)}) collective-permute-start(bf16[64,1024]{1,0:T(8,128)(2,1)S(1)} %get-tuple-element.48), channel_id=1, source_target_pairs={{0,24},{8,16},{16,8},{24,0},{1,25},{9,17},{17,9},{25,1},{2,26},{10... | collective-permute-start | bytes 393224 | tf_op jit(solution)/shard_map/ppermute | solution.py:347
  46.8 6.6 %collective-permute-start.26 = (f32[8,1024]{1,0:T(8,128)S(1)}, f32[8,1024]{1,0:T(8,128)S(1)}, u32[]{:S(2)}, u32[]{:S(2)}) collective-permute-start(f32[8,1024]{1,0:T(8,128)S(1)} %get-tuple-element.53.refs_0_), channel_id=1, source_target_pairs={{0,24},{8,16},{16,8},{24,0},{1,25},{9,17},{17,9},{25,1},{2,26},{10... | collective-permute-start | bytes 98312 | tf_op jit(solution)/shard_map/ppermute | solution.py:347
  48.5 7.5 %collective-permute-start.25 = (f32[8,1024]{1,0:T(8,128)S(1)}, f32[8,1024]{1,0:T(8,128)S(1)}, u32[]{:S(2)}, u32[]{:S(2)}) collective-permute-start(f32[8,1024]{1,0:T(8,128)S(1)} %get-tuple-element.53.refs_0_), channel_id=1, source_target_pairs={{0,16},{8,24},{16,0},{24,8},{1,17},{9,25},{17,1},{25,9},{2,18},{10... | collective-permute-start | bytes 98312 | tf_op jit(solution)/shard_map/ppermute | solution.py:347
  49.9 6.4 %collective-permute-start.24 = (f32[8,1024]{1,0:T(8,128)S(1)}, f32[8,1024]{1,0:T(8,128)S(1)}, u32[]{:S(2)}, u32[]{:S(2)}) collective-permute-start(f32[8,1024]{1,0:T(8,128)S(1)} %get-tuple-element.53.refs_0_), channel_id=1, source_target_pairs={{0,8},{8,0},{16,24},{24,16},{1,9},{9,1},{17,25},{25,17},{2,10},{10... | collective-permute-start | bytes 98312 | tf_op jit(solution)/shard_map/ppermute | solution.py:347
  50.4 20.7 %collective-permute-start.8 = (bf16[96,512]{1,0:T(8,128)(2,1)S(1)}, bf16[96,512]{1,0:T(8,128)(2,1)S(1)}, u32[]{:S(2)}, u32[]{:S(2)}) collective-permute-start(bf16[96,512]{1,0:T(8,128)(2,1)S(1)} %get-tuple-element.39), channel_id=1, source_target_pairs={{8,0},{16,8},{24,16},{9,1},{17,9},{25,17},{10,2},{18,10},{26,18},{... | collective-permute-start | bytes 294920 | tf_op jit(solution)/shard_map/ppermute | solution.py:416
  51.8 9.0 %collective-permute-start.14 = (bf16[16,1024]{1,0:T(8,128)(2,1)S(1)}, bf16[16,1024]{1,0:T(8,128)(2,1)S(1)}, u32[]{:S(2)}, u32[]{:S(2)}) collective-permute-start(bf16[16,1024]{1,0:T(8,128)(2,1)S(1)} %get-tuple-element.50), channel_id=1, source_target_pairs={{0,2},{1,3},{2,0},{3,1},{4,6},{5,7},{6,4},{7,5},{8,10},{9,11},{10,... | collective-permute-start | bytes 98312 | tf_op jit(solution)/shard_map/ppermute | solution.py:350
  53.4 11.1 %collective-permute-start.15 = (bf16[16,1024]{1,0:T(8,128)(2,1)S(1)}, bf16[16,1024]{1,0:T(8,128)(2,1)S(1)}, u32[]{:S(2)}, u32[]{:S(2)}) collective-permute-start(bf16[16,1024]{1,0:T(8,128)(2,1)S(1)} %get-tuple-element.51), channel_id=1, source_target_pairs={{0,4},{1,5},{2,6},{3,7},{4,0},{5,1},{6,2},{7,3},{8,12},{9,13},{10,... | collective-permute-start | bytes 98312 | tf_op jit(solution)/shard_map/ppermute | solution.py:350
  56.0 8.5 %collective-permute-start.16 = (bf16[16,1024]{1,0:T(8,128)(2,1)S(1)}, bf16[16,1024]{1,0:T(8,128)(2,1)S(1)}, u32[]{:S(2)}, u32[]{:S(2)}) collective-permute-start(bf16[16,1024]{1,0:T(8,128)(2,1)S(1)} %get-tuple-element.52), channel_id=1, source_target_pairs={{0,6},{1,7},{2,4},{3,5},{4,2},{5,3},{6,0},{7,1},{8,14},{9,15},{10,... | collective-permute-start | bytes 98312 | tf_op jit(solution)/shard_map/ppermute | solution.py:350
  56.2 14.8 %collective-permute-start.9 = (bf16[64,512]{1,0:T(8,128)(2,1)S(1)}, bf16[64,512]{1,0:T(8,128)(2,1)S(1)}, u32[]{:S(2)}, u32[]{:S(2)}) collective-permute-start(bf16[64,512]{1,0:T(8,128)(2,1)S(1)} %get-tuple-element.40), channel_id=1, source_target_pairs={{0,8},{8,16},{16,24},{1,9},{9,17},{17,25},{2,10},{10,18},{18,26},{... | collective-permute-start | bytes 196616 | tf_op jit(solution)/shard_map/ppermute | solution.py:417
  60.8 5.8 %collective-permute-start.29 = (f32[8,1024]{1,0:T(8,128)S(1)}, f32[8,1024]{1,0:T(8,128)S(1)}, u32[]{:S(2)}, u32[]{:S(2)}) collective-permute-start(f32[8,1024]{1,0:T(8,128)S(1)} %shard_map.143.refs_0_), channel_id=1, source_target_pairs={{0,6},{1,7},{2,4},{3,5},{4,2},{5,3},{6,0},{7,1},{8,14},{9,15},{10,... | collective-permute-start | bytes 98312 | tf_op jit(solution)/shard_map/ppermute | solution.py:350
  64.5 5.8 %collective-permute-start.28 = (f32[8,1024]{1,0:T(8,128)S(1)}, f32[8,1024]{1,0:T(8,128)S(1)}, u32[]{:S(2)}, u32[]{:S(2)}) collective-permute-start(f32[8,1024]{1,0:T(8,128)S(1)} %shard_map.143.refs_0_), channel_id=1, source_target_pairs={{0,4},{1,5},{2,6},{3,7},{4,0},{5,1},{6,2},{7,3},{8,12},{9,13},{10,... | collective-permute-start | bytes 98312 | tf_op jit(solution)/shard_map/ppermute | solution.py:350
  64.5 5.8 %collective-permute-start.27 = (f32[8,1024]{1,0:T(8,128)S(1)}, f32[8,1024]{1,0:T(8,128)S(1)}, u32[]{:S(2)}, u32[]{:S(2)}) collective-permute-start(f32[8,1024]{1,0:T(8,128)S(1)} %shard_map.143.refs_0_), channel_id=1, source_target_pairs={{0,2},{1,3},{2,0},{3,1},{4,6},{5,7},{6,4},{7,5},{8,10},{9,11},{10,... | collective-permute-start | bytes 98312 | tf_op jit(solution)/shard_map/ppermute | solution.py:350
  66.6 5.7 %collective-permute-start.19 = (bf16[16,1024]{1,0:T(8,128)(2,1)S(1)}, bf16[16,1024]{1,0:T(8,128)(2,1)S(1)}, u32[]{:S(2)}, u32[]{:S(2)}) collective-permute-start(bf16[16,1024]{1,0:T(8,128)(2,1)S(1)} %shard_map.142.refs_0_), channel_id=1, source_target_pairs={{0,6},{1,7},{2,4},{3,5},{4,2},{5,3},{6,0},{7,1},{8,14},{9,15},{10,... | collective-permute-start | bytes 98312 | tf_op jit(solution)/shard_map/ppermute | solution.py:350
  71.0 5.4 %collective-permute-start.30 = (f32[8,1024]{1,0:T(8,128)S(1)}, f32[8,1024]{1,0:T(8,128)S(1)}, u32[]{:S(2)}, u32[]{:S(2)}) collective-permute-start(f32[8,1024]{1,0:T(8,128)S(1)} %shard_map.144.refs_8_), channel_id=1, source_target_pairs={{0,1},{1,0},{2,3},{3,2},{4,5},{5,4},{6,7},{7,6},{8,9},{9,8},{10,11... | collective-permute-start | bytes 98312 | tf_op jit(solution)/shard_map/ppermute | solution.py:353
  71.1 5.3 %collective-permute-start.20 = (bf16[16,1024]{1,0:T(8,128)(2,1)S(1)}, bf16[16,1024]{1,0:T(8,128)(2,1)S(1)}, u32[]{:S(2)}, u32[]{:S(2)}) collective-permute-start(bf16[16,1024]{1,0:T(8,128)(2,1)S(1)} %shard_map.142.refs_0_), channel_id=1, source_target_pairs={{0,1},{1,0},{2,3},{3,2},{4,5},{5,4},{6,7},{7,6},{8,9},{9,8},{10,11... | collective-permute-start | bytes 98312 | tf_op jit(solution)/shard_map/ppermute | solution.py:353
  (17 other events, 165.0 us)

commit v2 on v1

v2 whole, which is shorter than its diff:
```python
import functools

import jax
import jax.numpy as jnp
from jax import lax
from jax.experimental import pallas as pl
from jax.experimental.pallas import tpu as pltpu
from jax.sharding import PartitionSpec as P

HEADS = 8
HSZ = 64
BLK = 24
KW = 7
HALF = KW // 2
BACK = 2 * BLK
AHEAD = 32
EDGE = 16
TILE = 4 * BLK
REACH = 176
GROUP = 4
FEATS = GROUP * HSZ
LANES = GROUP * TILE
NEG = -1e30
BF = jnp.bfloat16
F32 = jnp.float32
VMEM = pl.BlockSpec(memory_space=pltpu.VMEM)
SMEM = pl.BlockSpec(memory_space=pltpu.SMEM)
ANY = pl.BlockSpec(memory_space=pl.ANY)


def nt(a, b):
    return lax.dot_general(a, b, (((1,), (1,)), ((), ())), preferred_element_type=F32)


def nn(a, b):
    return lax.dot_general(a, b, (((1,), (0,)), ((), ())), preferred_element_type=F32)


def tn(a, b):
    return lax.dot_general(a, b, (((0,), (0,)), ((), ())), preferred_element_type=F32)


def call(kernel, outs, ins, args, scratch=(), flops=0, moved=0):
    return pl.pallas_call(
        kernel,
        out_shape=outs,
        in_specs=ins,
        out_specs=jax.tree.map(lambda _: VMEM, outs),
        scratch_shapes=scratch,
        compiler_params=pltpu.CompilerParams(vmem_limit_bytes=40 * 1024 * 1024),
        cost_estimate=pl.CostEstimate(flops=flops, bytes_accessed=moved, transcendentals=0),
    )(*args)


def shape(dims, kind):
    return jax.ShapeDtypeStruct(dims, kind)


def pack_kernel(k, v, g, w, ahead, behind, w_half, edge, sems):
    rows = k.shape[0]
    feats = k.shape[1]
    half = w.shape[0] // 2
    core = lax.rem(lax.axis_index("dp"), 2)
    pairs = [
        (k.at[pl.ds(rows - BACK, BACK)], ahead.at[pl.ds(0, BACK)]),
        (v.at[pl.ds(rows - BACK, BACK)], ahead.at[pl.ds(BACK, BACK)]),
        (k.at[pl.ds(0, AHEAD)], behind.at[pl.ds(0, AHEAD)]),
        (v.at[pl.ds(0, AHEAD)], behind.at[pl.ds(AHEAD, AHEAD)]),
        (g.at[pl.ds(rows - EDGE, EDGE)], edge.at[0]),
        (g.at[pl.ds(0, EDGE)], edge.at[1]),
        (w.at[pl.ds(pl.multiple_of(core * half, half), half)], w_half),
    ]
    copies = [pltpu.make_async_copy(a, b, sems.at[i]) for i, (a, b) in enumerate(pairs)]
    for copy in copies:
        copy.start()
    for copy in copies:
        copy.wait()
    last = edge[0].astype(F32)[8:]
    first = edge[1].astype(F32)[:8]
    for out, block in ((ahead, last), (behind, first)):
        two = jnp.concatenate([block[:, :feats], block[:, feats:]], 0)
        out[out.shape[0] - EDGE :] = two.astype(BF)


def packed(k, v, g, w):
    feats = k.shape[1]
    outs = (
        shape((2 * BACK + EDGE, feats), BF),
        shape((2 * AHEAD + EDGE, feats), BF),
        shape((w.shape[0] // 2, w.shape[1]), BF),
    )
    return pl.pallas_call(
        pack_kernel,
        out_shape=outs,
        in_specs=[ANY] * 4,
        out_specs=(VMEM,) * 3,
        scratch_shapes=[pltpu.VMEM((2, EDGE, g.shape[1]), BF), pltpu.SemaphoreType.DMA((7,))],
    )(k, v, g, w)


def head_of(dims):
    return lax.broadcasted_iota(jnp.int32, dims, 1) // HSZ


def stacked(tile, amount):
    head = head_of((1, FEATS))
    return jnp.concatenate(
        [tile * jnp.where(head == h, amount, 0.0).astype(BF) for h in range(GROUP)], 0
    )


def unstacked(product):
    head = head_of((TILE, FEATS))
    out = product[:TILE]
    for h in range(1, GROUP):
        out = jnp.where(head == h, product[h * TILE : (h + 1) * TILE], out)
    return out


def fill_ext(kx, vx, k, v, near, far):
    rows = k.shape[0]
    for at, ext, local in ((0, kx, k), (1, vx, v)):
        ext[0:BACK] = near[at * BACK : (at + 1) * BACK]
        ext[BACK : BACK + rows] = local[...]
        ext[BACK + rows :] = far[at * AHEAD : (at + 1) * AHEAD]


def allowed_in(tile, base, length, back, ahead):
    lane = lax.broadcasted_iota(jnp.int32, (1, LANES), 1)
    within = lane
    for h in range(1, GROUP):
        within = within - jnp.where(lane >= h * TILE, TILE, 0)
    block = jnp.zeros_like(lane)
    for b in range(1, TILE // BLK):
        block = block + jnp.where(within >= b * BLK, 1, 0)
    origin = base + tile * TILE - BACK
    low = jnp.maximum((block + 2 - back) * BLK, -origin)
    high = jnp.minimum((block + 3 + ahead) * BLK, length - origin)
    row = lax.broadcasted_iota(jnp.int32, (REACH, LANES), 0)
    return (row >= low) & (row < high)


def probabilities(key_tile, query_stack, allowed):
    scores = jnp.where(allowed, nt(key_tile, query_stack), NEG)
    terms = jnp.exp(scores - jnp.max(scores, axis=0, keepdims=True))
    return terms * (1.0 / jnp.sum(terms, axis=0, keepdims=True))


def masked(block, start, length):
    frame = start + lax.broadcasted_iota(jnp.int32, block.shape, 0)
    return jnp.where((frame >= 0) & (frame < length), block.astype(F32), 0.0)


def fill_rims(gx, at, near, far, base, rows, length):
    feats = near.shape[1]
    before = near[2 * BACK :].astype(F32)
    after = far[2 * AHEAD :].astype(F32)
    for part in range(2):
        cols = slice(part * feats, (part + 1) * feats)
        here = slice(part * 8, (part + 1) * 8)
        gx[0:8, cols] = masked(before[here], base - 8, length)
        gx[at : at + 8, cols] = masked(after[here], base + rows, length)


def convolve(out, out_at, gx, gx_at, taps, start, count, length):
    width = out.shape[1]
    step = 128
    frame = start + lax.broadcasted_iota(jnp.int32, (count, step), 0)
    for at in range(0, width, step):
        cols = slice(at, at + step)
        total = taps[0:1, cols] * gx[gx_at + HALF : gx_at + HALF + count, cols]
        for tap in range(1, KW):
            top = gx_at + HALF - tap
            total = total + taps[tap : tap + 1, cols] * gx[top : top + count, cols]
        out[out_at : out_at + count, cols] = jnp.where(frame < length, total, 0.0).astype(BF)


def inner_conv_kernel(g, taps, lengths, out, gx):
    rows = g.shape[0]
    base = lax.axis_index("cp") * rows
    gx[0:8] = jnp.zeros((8, gx.shape[1]), F32)
    gx[8 + rows :] = jnp.zeros((8, gx.shape[1]), F32)
    gx[8 : 8 + rows] = masked(g[...], base, lengths[0])
    convolve(out, 0, gx, 8, taps, base, rows, lengths[0])


def forward_kernel(
    q, k, v, near, far, g, taps, inner, lengths, offsets,
    stream_grad, send, keep, att_out, kx, vx, gx, att_t,
):
    rows, feats = q.shape
    place = lax.axis_index("cp")
    core = lax.rem(lax.axis_index("dp"), 2)
    base = place * rows
    length = lengths[0]
    fill_ext(kx, vx, k, v, near, far)
    for tile in range(rows // TILE):
        start = tile * TILE
        allowed = allowed_in(tile, base, length, offsets[0, 0], offsets[0, 1])
        frame = base + start + lax.broadcasted_iota(jnp.int32, (TILE, FEATS), 0)
        for group in range(feats // FEATS):
            cols = slice(group * FEATS, (group + 1) * FEATS)
            query_stack = stacked(q[start : start + TILE, cols], HSZ**-0.5)
            probs = probabilities(kx[start : start + REACH, cols], query_stack, allowed)
            product = tn(probs.astype(BF), vx[start : start + REACH, cols])
            attended = jnp.where(frame < length, unstacked(product), 0.0).astype(BF)
            att_out[start : start + TILE, cols] = attended
    att_t[...] = att_out[...].astype(F32).T.astype(BF)
    fill_rims(gx, 56, near, far, base, rows, length)
    gx[8:32] = masked(g[0:32].astype(F32)[:24], base, length)
    gx[32:56] = masked(g[rows - 32 :].astype(F32)[8:], base + rows - 24, length)
    stream_grad[EDGE : rows - EDGE] = inner[EDGE : rows - EDGE]
    convolve(stream_grad, 0, gx, 8, taps, base, EDGE, length)
    convolve(stream_grad, rows - EDGE, gx, 40, taps, base + rows - EDGE, EDGE, length)
    half = send.shape[1]
    for part in range(send.shape[0]):
        there = pl.multiple_of(2 * half * part + half * (1 - core), half)
        here = pl.multiple_of(2 * half * part + half * core, half)
        send[part] = nn(att_t[pl.ds(there, half)], stream_grad[...]).astype(BF)
        keep[part] = nn(att_t[pl.ds(here, half)], stream_grad[...])


def folded(conv, half):
    extra = 8 * conv.shape[1] // half
    return jnp.concatenate(
        [conv[:, at : at + extra] for at in range(0, conv.shape[1], extra)], 0
    )


def split_kernel(keep, got, conv, own, *pieces):
    place = lax.axis_index("cp")
    half, width = keep.shape[1:]
    tail = folded(conv[...], half).astype(BF)
    own[:, :width] = keep[place] + got[place].astype(F32)
    own[:, width:] = tail.astype(F32)
    for by, piece in enumerate(pieces, 1):
        at = lax.bitwise_xor(place, by)
        piece[:, :width] = (keep[at] + got[at].astype(F32)).astype(BF)
        piece[:, width:] = tail


def tree_sum(terms):
    while len(terms) > 1:
        terms = [a + b for a, b in zip(terms[::2], terms[1::2])]
    return terms[0]


def cp_sum_kernel(after, own, *refs):
    got = refs[:-5]
    back, onward, part, back_out, onward_out = refs[-5:]
    total = tree_sum([own[...]] + [ref[...].astype(F32) for ref in got])
    part[...] = total.astype(BF)
    back_out[...] = back[...]
    onward_out[...] = onward[...]


def z_sum_kernel(after, *refs):
    refs[-1][...] = tree_sum([ref[...].astype(F32) for ref in refs[:-1]])


def final_kernel(mine, theirs, weight_grad, conv_grad):
    half = mine.shape[0]
    width = weight_grad.shape[1]
    core = lax.rem(lax.axis_index("dp"), 2)
    weight_grad[pl.ds(pl.multiple_of(core * half, half), half)] = mine[:, :width]
    weight_grad[pl.ds(pl.multiple_of((1 - core) * half, half), half)] = theirs[:, :width]
    extra = mine.shape[1] - width
    total = mine[:, width:] + theirs[:, width:]
    for at in range(0, half, 8):
        cols = slice(at // 8 * extra, (at // 8 + 1) * extra)
        conv_grad[:, cols] = total[at : at + KW]


def weight_stack_kernel(after, *refs):
    for k, ref in enumerate(refs[:-1]):
        refs[-1][k] = ref[...]


def conv_kernel(att, w, passed, stream, g, near, far, lengths, *refs):
    got = refs[:-4]
    conv, wx, gx, mixed = refs[-4:]
    rows, width = g.shape
    place = lax.axis_index("cp")
    core = lax.rem(lax.axis_index("dp"), 2)
    base = place * rows
    length = lengths[0]
    shard = w.shape[0]
    half = shard // 2
    wx[pl.ds(pl.multiple_of(place * shard, shard), shard)] = w[...]
    for by, ref in enumerate(got, 1):
        at = lax.bitwise_xor(place, by) * shard
        wx[pl.ds(pl.multiple_of(at + core * half, half), half)] = ref[...]
        wx[pl.ds(pl.multiple_of(at + (1 - core) * half, half), half)] = passed[by - 1]
    fill_rims(gx, 8 + rows, near, far, base, rows, length)
    gx[8 : 8 + rows] = masked(g[...], base, length)
    total = stream[...].astype(F32) + nn(att[...], wx[...])
    mixed[...] = masked(total, base, length)
    conv[KW:] = jnp.zeros((8 - KW, width), F32)
    step = 128
    for at in range(0, width, step):
        cols = slice(at, at + step)
        block = mixed[:, cols]
        for tap in range(KW):
            top = 8 + HALF - tap
            conv[tap : tap + 1, cols] = jnp.sum(
                block * gx[top : top + rows, cols], axis=0, keepdims=True
            )


def backward_kernel(
    after, q, k, v, near, far, stream_grad, wx, lengths, offsets,
    query_g, key_g, value_g, back, onward, kx, vx, kg, vg, ag,
):
    rows, feats = q.shape
    base = lax.axis_index("cp") * rows
    length = lengths[0]
    ag[...] = nt(stream_grad[...], wx[...]).astype(BF)
    fill_ext(kx, vx, k, v, near, far)
    kg[...] = jnp.zeros_like(kg)
    vg[...] = jnp.zeros_like(vg)
    for tile in range(rows // TILE):
        start = tile * TILE
        allowed = allowed_in(tile, base, length, offsets[0, 0], offsets[0, 1])
        span = slice(start, start + REACH)
        for group in range(feats // FEATS):
            cols = slice(group * FEATS, (group + 1) * FEATS)
            query_stack = stacked(q[start : start + TILE, cols], HSZ**-0.5)
            grad_stack = stacked(ag[start : start + TILE, cols], 1.0)
            probs = probabilities(kx[span, cols], query_stack, allowed)
            dprob = nt(vx[span, cols], grad_stack)
            inner = jnp.sum(probs * dprob, axis=0, keepdims=True)
            dscore = (probs * (dprob - inner)).astype(BF)
            query_g[start : start + TILE, cols] = (
                unstacked(tn(dscore, kx[span, cols])) * HSZ**-0.5
            ).astype(BF)
            kg[span, cols] += nn(dscore, query_stack)
            vg[span, cols] += nn(probs.astype(BF), grad_stack)
    key_g[...] = kg[BACK : BACK + rows]
    value_g[...] = vg[BACK : BACK + rows]
    for at, ext in ((0, kg), (1, vg)):
        back[at * BACK : (at + 1) * BACK] = ext[0:BACK].astype(BF)
        onward[at * AHEAD : (at + 1) * AHEAD] = ext[BACK + rows :].astype(BF)


def join_kernel(key_g, value_g, last, first, key_out, value_out):
    rows = key_g.shape[0]
    for at, grad, out in ((0, key_g, key_out), (1, value_g, value_out)):
        out[0:AHEAD] = (
            grad[0:AHEAD] + first[at * AHEAD : (at + 1) * AHEAD].astype(F32)
        ).astype(BF)
        out[AHEAD : rows - BACK] = grad[AHEAD : rows - BACK].astype(BF)
        out[rows - BACK :] = (
            grad[rows - BACK :] + last[at * BACK : (at + 1) * BACK].astype(F32)
        ).astype(BF)


def body(
    queries, key_rows, value_rows, stream_in, out_grad, out_weight, conv_weight, lengths, offsets
):
    rows, feats = queries.shape[1:]
    width = stream_in.shape[2]
    cps, dps = lax.axis_size("cp"), lax.axis_size("dp")
    floors = dps // 2
    q, k, v, g, stream = queries[0], key_rows[0], value_rows[0], out_grad[0], stream_in[0]
    shard = out_weight.shape[0]
    half = shard // 2
    ext = rows + BACK + AHEAD
    upward = [(i, (i + 1) % cps) for i in range(cps)]
    downward = [(i, (i - 1) % cps) for i in range(cps)]

    def over_cp(arrays):
        return [
            lax.ppermute(array, "cp", [(i, i ^ by) for i in range(cps)])
            for by, array in enumerate(arrays, 1)
        ]

    def over_z(array):
        return [
            lax.ppermute(array, "dp", [(i, i ^ (2 * by)) for i in range(dps)])
            for by in range(1, floors)
        ]

    def over_core(array):
        return lax.ppermute(array, "dp", [(i, i ^ 1) for i in range(dps)])

    ahead, behind, w_half = packed(k, v, g, out_weight)
    near = lax.ppermute(ahead, "cp", upward)
    far = lax.ppermute(behind, "cp", downward)
    w_got = over_cp([w_half] * (cps - 1))
    inner = call(
        inner_conv_kernel,
        shape((rows, width), BF),
        [VMEM] * 2 + [SMEM],
        (g, conv_weight, lengths),
        [pltpu.VMEM((rows + 16, width), F32)],
    )
    ext_scratch = [pltpu.VMEM((ext, feats), BF)] * 2
    stream_grad, send, keep, att = call(
        forward_kernel,
        (
            shape((rows, width), BF),
            shape((cps, half, width), BF),
            shape((cps, half, width), F32),
            shape((rows, feats), BF),
        ),
        [VMEM] * 8 + [SMEM] * 2,
        (q, k, v, near, far, g, conv_weight, inner, lengths, offsets),
        ext_scratch + [pltpu.VMEM((64, width), F32), pltpu.VMEM((feats, rows), BF)],
    )
    core_got = over_core(send)
    passed = over_core(
        call(
            weight_stack_kernel,
            shape((cps - 1, half, width), BF),
            [ANY] + [VMEM] * (cps - 1),
            (att, *w_got),
        )
    )
    conv, wx = call(
        conv_kernel,
        (shape((8, width), F32), shape((feats, width), BF)),
        [VMEM] * 7 + [SMEM] + [VMEM] * (cps - 1),
        (att, out_weight, passed, stream, g, near, far, lengths, *w_got),
        [pltpu.VMEM((rows + 16, width), F32), pltpu.VMEM((rows, width), F32)],
    )
    wide = width + 8 * width // half
    own, *pieces = call(
        split_kernel,
        (shape((half, wide), F32),) + (shape((half, wide), BF),) * (cps - 1),
        [VMEM] * 3,
        (keep, core_got, conv),
    )
    cp_got = over_cp(pieces)
    query_g, key_g, value_g, back, onward = call(
        backward_kernel,
        (
            shape((rows, feats), BF),
            shape((rows, feats), F32),
            shape((rows, feats), F32),
            shape((2 * BACK, feats), BF),
            shape((2 * AHEAD, feats), BF),
        ),
        [ANY] + [VMEM] * 7 + [SMEM] * 2,
        (own, q, k, v, near, far, stream_grad, wx, lengths, offsets),
        ext_scratch
        + [pltpu.VMEM((ext, feats), F32)] * 2
        + [pltpu.VMEM((rows, feats), BF)],
        moved=10 * 2**20,
    )
    part, back, onward = call(
        cp_sum_kernel,
        (shape((half, wide), BF), shape(back.shape, BF), shape(onward.shape, BF)),
        [ANY] + [VMEM] * (cps + 2),
        (query_g, own, *cp_got, back, onward),
    )
    last = lax.ppermute(back, "cp", downward)
    first = lax.ppermute(onward, "cp", upward)
    key_grad, value_grad = call(
        join_kernel,
        (shape((rows, feats), BF),) * 2,
        [VMEM] * 4,
        (key_g, value_g, last, first),
    )
    if floors != 4:
        at = (lax.axis_index("dp") % 2) * half
        whole = lax.dynamic_update_slice(
            jnp.zeros((shard, width), F32), part[:, :width].astype(F32), (at, 0)
        )
        weight_grad = lax.psum(whole, "dp")
        conv_grad = lax.psum(conv, ("cp", "dp"))[:KW]
    else:
        mine = call(
            z_sum_kernel,
            shape((half, wide), F32),
            [ANY] + [VMEM] * floors,
            (key_grad, part, *over_z(part)),
        )
        weight_grad, conv_grad = call(
            final_kernel,
            (shape((shard, width), F32), shape((KW, width), F32)),
            [VMEM] * 2,
            (mine, over_core(mine)),
        )
    return (
        query_g[None],
        key_grad[None],
        value_grad[None],
        stream_grad[None],
        weight_grad,
        conv_grad,
    )


def solution(mesh):
    rows_spec = P("dp", "cp", None)
    return jax.shard_map(
        body,
        mesh=mesh,
        in_specs=(rows_spec,) * 5 + (P("cp", None), P(), P("dp"), P("dp", None)),
        out_specs=(rows_spec,) * 4 + (P("cp", None), P()),
        check_vma=False,
    )
```

time: 77.5 us -> 50.2 us (0.65)
  starting transfers between devices: 37.5 us -> 17.7 us
  Pallas kernels: 22.2 us -> 12.6 us
  local copies, waits for them, and re-layouts: 0.04 us -> 1.9 us
    ppermute x31 -> x16, starting transfers between devices: 37.5 us -> 17.7 us  [the longest x6 7.04 us: over_cp(): lax.ppermute(array, 'cp', [(i, i ^ by) for i in range(cps)])]
    pallas_call x1, Pallas kernels: 12.1 us -> 1.86 us  [packed(): pl.pallas_call(pack_kernel, out_shape=outs, in_specs=[ANY] * 4, out_specs...]
    unnamed x20 -> x22, local copies, waits for them, and re-layouts: 0.04 us -> 1.9 us
    pallas_call x9 -> x10, Pallas kernels: 10.1 us -> 10.7 us  [call(): pl.pallas_call(kernel, out_shape=outs, in_specs=ins, out_specs=jax.tree.m...]
    ppermute x31 -> x16, waiting for transfers between devices: 15.9 us -> 16.4 us  [the longest x1 4.31 us: body(): first = lax.ppermute(onward, 'cp', upward)]
  transfers between devices with their start and end apart: 31 -> 16, of which waited for: 6 -> 8; matrix products, arithmetic and copies ran while one was open for 0% -> 0% of each run, Pallas kernels for 7% -> 19%
where the time goes in v2:
time: 50.2 us; the launch traced here: 50 us
  starting transfers between devices  17.7 us (35%)
  waiting for transfers between devices  16.4 us (33%)
  Pallas kernels  12.6 us (25%)
  local copies, waits for them, and re-layouts  1.9 us (4%)
  between operations  1.45 us (3%)
    pallas_call x10, Pallas kernels, call(): pl.pallas_call(kernel, out_shape=outs, in_specs=ins, out_specs=jax.tree.m...  10.7 us
    ppermute x6, starting transfers between devices, over_cp(): lax.ppermute(array, 'cp', [(i, i ^ by) for i in range(cps)])  7.04 us
    ppermute x3, starting transfers between devices, over_z(): lax.ppermute(array, 'dp', [(i, i ^ 2 * by) for i in range(dps)])  4.45 us
    ppermute x1, waiting for transfers between devices, body(): first = lax.ppermute(onward, 'cp', upward)  4.31 us
    ppermute x6, waiting for transfers between devices, over_cp(): lax.ppermute(array, 'cp', [(i, i ^ by) for i in range(cps)])  4.27 us
    ppermute x3, waiting for transfers between devices, over_z(): lax.ppermute(array, 'dp', [(i, i ^ 2 * by) for i in range(dps)])  3.31 us
    ppermute x3, waiting for transfers between devices, over_core(): return lax.ppermute(array, 'dp', [(i, i ^ 1) for i in range(dps)])  3.28 us
    ppermute x1, starting transfers between devices, body(): near = lax.ppermute(ahead, 'cp', upward)  2.99 us
  transfers between devices with their start and end apart: 16, of which 8 were waited for; matrix products, arithmetic and copies ran while one was open for 0% of the time, Pallas kernels for 19%

profile of v2, /device:TPU:0, one launch (start us, length us, event | category | flops | bytes accessed | tf_op | source)
XLA Modules:
  0.0 50.0 jit_solution(12747784229804763338)
XLA Ops:
  0.7 1.9 %shard_map.136 = (bf16[112,512]{1,0:T(8,128)(2,1)}, bf16[80,512]{1,0:T(8,128)(2,1)}, bf16[64,1024]{1,0:T(8,128)(2,1)}) custom-call(bf16[192,512]{1,0:T(8,128)(2,1)} %bitcast.13, bf16[192,512]{1,0:T(8,128)(2,1)} %bitcast.16, bf16[192,1024]{1,0:T(8,128)(2,1)} %bitcast.9, bf16[128,1024]{1,0:T(8,128)(2,1)} %w.3), custom_call_target="tpu_custom_call" | custom-call | tf_op jit(solution)/shard_map/pallas_call | solution.py:92
  2.5 3.0 %collective-permute-start = (bf16[112,512]{1,0:T(8,128)(2,1)}, bf16[112,512]{1,0:T(8,128)(2,1)S(1)}, u32[]{:S(2)}, u32[]{:S(2)}) collective-permute-start(bf16[112,512]{1,0:T(8,128)(2,1)} %get-tuple-element.31), channel_id=1, source_target_pairs={{0,8},{8,16},{16,24},{24,0},{1,9},{9,17},{17,25},{25,1},{2,10},{10... | collective-permute-start | bytes 344072 | tf_op jit(solution)/shard_map/ppermute | solution.py:387
  5.5 1.0 %collective-permute-start.1 = (bf16[80,512]{1,0:T(8,128)(2,1)}, bf16[80,512]{1,0:T(8,128)(2,1)S(1)}, u32[]{:S(2)}, u32[]{:S(2)}) collective-permute-start(bf16[80,512]{1,0:T(8,128)(2,1)} %get-tuple-element.32), channel_id=1, source_target_pairs={{0,24},{8,0},{16,8},{24,16},{1,25},{9,1},{17,9},{25,17},{2,26},{10... | collective-permute-start | bytes 245768 | tf_op jit(solution)/shard_map/ppermute | solution.py:388
  6.5 2.0 %collective-permute-start.5 = (bf16[64,1024]{1,0:T(8,128)(2,1)}, bf16[64,1024]{1,0:T(8,128)(2,1)S(1)}, u32[]{:S(2)}, u32[]{:S(2)}) collective-permute-start(bf16[64,1024]{1,0:T(8,128)(2,1)} %get-tuple-element.36), channel_id=1, source_target_pairs={{0,24},{8,16},{16,8},{24,0},{1,25},{9,17},{17,9},{25,1},{2,26},{10... | collective-permute-start | bytes 393224 | tf_op jit(solution)/shard_map/ppermute | solution.py:373
  9.0 1.0 %collective-permute-start.3 = (bf16[64,1024]{1,0:T(8,128)(2,1)}, bf16[64,1024]{1,0:T(8,128)(2,1)S(1)}, u32[]{:S(2)}, u32[]{:S(2)}) collective-permute-start(bf16[64,1024]{1,0:T(8,128)(2,1)} %get-tuple-element.36), channel_id=1, source_target_pairs={{0,8},{8,0},{16,24},{24,16},{1,9},{9,1},{17,25},{25,17},{2,10},{10... | collective-permute-start | bytes 393224 | tf_op jit(solution)/shard_map/ppermute | solution.py:373
  10.7 1.0 %shard_map.137.inner = bf16[192,1024]{1,0:T(8,128)(2,1)S(1)} custom-call(bf16[192,1024]{1,0:T(8,128)(2,1)S(1)} %bitcast.10, f32[7,1024]{1,0:T(8,128)S(1)} %copy-done.9, s32[1]{0:T(128)S(6)} %copy.15.lengths), custom_call_target="tpu_custom_call" | custom-call | tf_op jit(solution)/shard_map/pallas_call | solution.py:44
  11.7 1.2 %collective-permute-done.1.far = bf16[80,512]{1,0:T(8,128)(2,1)S(1)} collective-permute-done((bf16[80,512]{1,0:T(8,128)(2,1)}, bf16[80,512]{1,0:T(8,128)(2,1)S(1)}, u32[]{:S(2)}, u32[]{:S(2)}) %collective-permute-start.1) | collective-permute-done | bytes 81952 | tf_op jit(solution)/shard_map/ppermute | solution.py:388
  13.0 2.8 %shard_map.138 = (bf16[192,1024]{1,0:T(8,128)(2,1)}, bf16[4,64,1024]{2,1,0:T(8,128)(2,1)S(1)}, f32[4,64,1024]{2,1,0:T(8,128)S(1)}, bf16[192,512]{1,0:T(8,128)(2,1)S(1)}) custom-call(bf16[192,512]{1,0:T(8,128)(2,1)S(1)} %bitcast.19, bf16[192,512]{1,0:T(8,128)(2,1)S(1)} %bitcast.14, bf16[192,512]{1,0:T(8,128)(2,1)S(1)} %bitcast.17, ...), custom_call_target="tpu_custom_call" | custom-call | tf_op jit(solution)/shard_map/pallas_call | solution.py:44
  16.1 1.4 %collective-permute-done.3.refs_0_ = bf16[64,1024]{1,0:T(8,128)(2,1)S(1)} collective-permute-done((bf16[64,1024]{1,0:T(8,128)(2,1)}, bf16[64,1024]{1,0:T(8,128)(2,1)S(1)}, u32[]{:S(2)}, u32[]{:S(2)}) %collective-permute-start.3) | collective-permute-done | bytes 131104 | tf_op jit(solution)/shard_map/ppermute | solution.py:373
  17.6 1.7 %collective-permute-done.6.passed = bf16[3,64,1024]{2,1,0:T(8,128)(2,1)S(1)} collective-permute-done((bf16[3,64,1024]{2,1,0:T(8,128)(2,1)S(1)}, bf16[3,64,1024]{2,1,0:T(8,128)(2,1)S(1)}, u32[]{:S(2)}, u32[]{:S(2)}) %collective-permute-start.6) | collective-permute-done | bytes 393248 | tf_op jit(solution)/shard_map/ppermute | solution.py:384
  19.3 1.4 %shard_map.140 = (f32[8,1024]{1,0:T(8,128)S(1)}, bf16[512,1024]{1,0:T(8,128)(2,1)S(1)}) custom-call(bf16[192,512]{1,0:T(8,128)(2,1)S(1)} %get-tuple-element.35.after.att, bf16[128,1024]{1,0:T(8,128)(2,1)S(1)} %copy-done.3, bf16[3,64,1024]{2,1,0:T(8,128)(2,1)S(1)} %collective-permute-done.6.passed, bf16[192,1024]{1,0:T(8,128)(2,1)S(1)} %bitcast.21, ...), custom_call_target="tpu_custom_call" | custom-call | tf_op jit(solution)/shard_map/pallas_call | solution.py:44
  20.8 1.1 %collective-permute-start.7 = (bf16[64,1152]{1,0:T(8,128)(2,1)S(1)}, bf16[64,1152]{1,0:T(8,128)(2,1)S(1)}, u32[]{:S(2)}, u32[]{:S(2)}) collective-permute-start(bf16[64,1152]{1,0:T(8,128)(2,1)S(1)} %get-tuple-element.44), channel_id=1, source_target_pairs={{0,8},{8,0},{16,24},{24,16},{1,9},{9,1},{17,25},{25,17},{2,10},{10... | collective-permute-start | bytes 442376 | tf_op jit(solution)/shard_map/ppermute | solution.py:373
  21.8 1.1 %collective-permute-start.8 = (bf16[64,1152]{1,0:T(8,128)(2,1)S(1)}, bf16[64,1152]{1,0:T(8,128)(2,1)S(1)}, u32[]{:S(2)}, u32[]{:S(2)}) collective-permute-start(bf16[64,1152]{1,0:T(8,128)(2,1)S(1)} %get-tuple-element.45), channel_id=1, source_target_pairs={{0,16},{8,24},{16,0},{24,8},{1,17},{9,25},{17,1},{25,9},{2,18},{10... | collective-permute-start | bytes 442376 | tf_op jit(solution)/shard_map/ppermute | solution.py:373
  22.9 1.4 %collective-permute-start.9 = (bf16[64,1152]{1,0:T(8,128)(2,1)S(1)}, bf16[64,1152]{1,0:T(8,128)(2,1)S(1)}, u32[]{:S(2)}, u32[]{:S(2)}) collective-permute-start(bf16[64,1152]{1,0:T(8,128)(2,1)S(1)} %get-tuple-element.46), channel_id=1, source_target_pairs={{0,24},{8,16},{16,8},{24,0},{1,25},{9,17},{17,9},{25,1},{2,26},{10... | collective-permute-start | bytes 442376 | tf_op jit(solution)/shard_map/ppermute | solution.py:373
  24.3 3.7 %shard_map.142 = (bf16[192,512]{1,0:T(8,128)(2,1)}, f32[192,512]{1,0:T(8,128)S(1)}, f32[192,512]{1,0:T(8,128)S(1)}, bf16[96,512]{1,0:T(8,128)(2,1)S(1)}, bf16[64,512]{1,0:T(8,128)(2,1)S(1)}) custom-call(f32[64,1152]{1,0:T(8,128)S(1)} %get-tuple-element.38.after.own, bf16[192,512]{1,0:T(8,128)(2,1)S(1)} %bitcast.20, bf16[192,512]{1,0:T(8,128)(2,1)S(1)} %bitcast.15, ...), custom_call_target="tpu_custom_call" | custom-call | bytes 10485760 | tf_op jit(solution)/shard_map/pallas_call | solution.py:44
  28.0 2.6 %collective-permute-done.8.refs_1_ = bf16[64,1152]{1,0:T(8,128)(2,1)S(1)} collective-permute-done((bf16[64,1152]{1,0:T(8,128)(2,1)S(1)}, bf16[64,1152]{1,0:T(8,128)(2,1)S(1)}, u32[]{:S(2)}, u32[]{:S(2)}) %collective-permute-start.8) | collective-permute-done | bytes 147488 | tf_op jit(solution)/shard_map/ppermute | solution.py:373
  30.6 0.9 %copy-done.7 = bf16[192,512]{1,0:T(8,128)(2,1)S(1)} copy-done((bf16[192,512]{1,0:T(8,128)(2,1)S(1)}, bf16[192,512]{1,0:T(8,128)(2,1)}, u32[]{:S(2)}) %copy-start.7) | copy-done | bytes 196632
  31.6 3.7 %collective-permute-start.14 = (bf16[64,1152]{1,0:T(8,128)(2,1)S(1)}, bf16[64,1152]{1,0:T(8,128)(2,1)S(1)}, u32[]{:S(2)}, u32[]{:S(2)}) collective-permute-start(bf16[64,1152]{1,0:T(8,128)(2,1)S(1)} %get-tuple-element.53.refs_0_), channel_id=1, source_target_pairs={{0,6},{1,7},{2,4},{3,5},{4,2},{5,3},{6,0},{7,1},{8,14},{9,15},{10,... | collective-permute-start | bytes 442376 | tf_op jit(solution)/shard_map/ppermute | solution.py:379
  36.1 1.2 %collective-permute-start.10 = (bf16[96,512]{1,0:T(8,128)(2,1)S(1)}, bf16[96,512]{1,0:T(8,128)(2,1)S(1)}, u32[]{:S(2)}, u32[]{:S(2)}) collective-permute-start(bf16[96,512]{1,0:T(8,128)(2,1)S(1)} %get-tuple-element.49), channel_id=1, source_target_pairs={{0,24},{8,0},{16,8},{24,16},{1,25},{9,1},{17,9},{25,17},{2,26},{10... | collective-permute-start | bytes 294920 | tf_op jit(solution)/shard_map/ppermute | solution.py:456
  37.3 0.9 %collective-permute-start.11 = (bf16[64,512]{1,0:T(8,128)(2,1)S(1)}, bf16[64,512]{1,0:T(8,128)(2,1)S(1)}, u32[]{:S(2)}, u32[]{:S(2)}) collective-permute-start(bf16[64,512]{1,0:T(8,128)(2,1)S(1)} %get-tuple-element.50), channel_id=1, source_target_pairs={{0,8},{8,16},{16,24},{24,0},{1,9},{9,17},{17,25},{25,1},{2,10},{10... | collective-permute-start | bytes 196616 | tf_op jit(solution)/shard_map/ppermute | solution.py:457
  38.1 4.3 %collective-permute-done.11.first = bf16[64,512]{1,0:T(8,128)(2,1)S(1)} collective-permute-done((bf16[64,512]{1,0:T(8,128)(2,1)S(1)}, bf16[64,512]{1,0:T(8,128)(2,1)S(1)}, u32[]{:S(2)}, u32[]{:S(2)}) %collective-permute-start.11) | collective-permute-done | bytes 65568 | tf_op jit(solution)/shard_map/ppermute | solution.py:457
  43.2 3.3 %collective-permute-done.13.refs_2_ = bf16[64,1152]{1,0:T(8,128)(2,1)S(1)} collective-permute-done((bf16[64,1152]{1,0:T(8,128)(2,1)S(1)}, bf16[64,1152]{1,0:T(8,128)(2,1)S(1)}, u32[]{:S(2)}, u32[]{:S(2)}) %collective-permute-start.13) | collective-permute-done | bytes 147488 | tf_op jit(solution)/shard_map/ppermute | solution.py:379
  46.5 0.9 %copy-done.8 = bf16[192,512]{1,0:T(8,128)(2,1)S(1)} copy-done((bf16[192,512]{1,0:T(8,128)(2,1)S(1)}, bf16[192,512]{1,0:T(8,128)(2,1)}, u32[]{:S(2)}) %copy-start.8) | copy-done | bytes 196632
  47.6 1.6 %collective-permute-done.15.theirs = f32[64,1152]{1,0:T(8,128)S(1)} collective-permute-done((f32[64,1152]{1,0:T(8,128)S(1)}, f32[64,1152]{1,0:T(8,128)S(1)}, u32[]{:S(2)}, u32[]{:S(2)}) %collective-permute-start.15) | collective-permute-done | bytes 294944 | tf_op jit(solution)/shard_map/ppermute | solution.py:384
  (41 shorter events, 3.8 us)
Async XLA Ops:
  0.6 10.0 %copy-start = (bf16[1,192,1024]{2,1,0:T(8,128)(2,1)S(1)}, bf16[1,192,1024]{2,1,0:T(8,128)(2,1)}, u32[]{:S(2)}) copy-start(bf16[1,192,1024]{2,1,0:T(8,128)(2,1)} %param.13) | copy-start | bytes 1179652
  0.6 10.0 %copy-start.9 = (f32[7,1024]{1,0:T(8,128)S(1)}, f32[7,1024]{1,0:T(8,128)}, u32[]{:S(2)}) copy-start(f32[7,1024]{1,0:T(8,128)} %taps.3) | copy-start | bytes 86020
  2.5 10.5 %collective-permute-start = (bf16[112,512]{1,0:T(8,128)(2,1)}, bf16[112,512]{1,0:T(8,128)(2,1)S(1)}, u32[]{:S(2)}, u32[]{:S(2)}) collective-permute-start(bf16[112,512]{1,0:T(8,128)(2,1)} %get-tuple-element.31), channel_id=1, source_target_pairs={{0,8},{8,16},{16,24},{24,0},{1,9},{9,17},{17,25},{25,1},{2,10},{10... | collective-permute-start | bytes 344072 | tf_op jit(solution)/shard_map/ppermute | solution.py:387
  5.5 7.5 %collective-permute-start.1 = (bf16[80,512]{1,0:T(8,128)(2,1)}, bf16[80,512]{1,0:T(8,128)(2,1)S(1)}, u32[]{:S(2)}, u32[]{:S(2)}) collective-permute-start(bf16[80,512]{1,0:T(8,128)(2,1)} %get-tuple-element.32), channel_id=1, source_target_pairs={{0,24},{8,0},{16,8},{24,16},{1,25},{9,1},{17,9},{25,17},{2,26},{10... | collective-permute-start | bytes 245768 | tf_op jit(solution)/shard_map/ppermute | solution.py:388
  6.5 9.3 %collective-permute-start.5 = (bf16[64,1024]{1,0:T(8,128)(2,1)}, bf16[64,1024]{1,0:T(8,128)(2,1)S(1)}, u32[]{:S(2)}, u32[]{:S(2)}) collective-permute-start(bf16[64,1024]{1,0:T(8,128)(2,1)} %get-tuple-element.36), channel_id=1, source_target_pairs={{0,24},{8,16},{16,8},{24,0},{1,25},{9,17},{17,9},{25,1},{2,26},{10... | collective-permute-start | bytes 393224 | tf_op jit(solution)/shard_map/ppermute | solution.py:373
  8.5 7.6 %collective-permute-start.4 = (bf16[64,1024]{1,0:T(8,128)(2,1)}, bf16[64,1024]{1,0:T(8,128)(2,1)S(1)}, u32[]{:S(2)}, u32[]{:S(2)}) collective-permute-start(bf16[64,1024]{1,0:T(8,128)(2,1)} %get-tuple-element.36), channel_id=1, source_target_pairs={{0,16},{8,24},{16,0},{24,8},{1,17},{9,25},{17,1},{25,9},{2,18},{10... | collective-permute-start | bytes 393224 | tf_op jit(solution)/shard_map/ppermute | solution.py:373
  9.0 8.4 %collective-permute-start.3 = (bf16[64,1024]{1,0:T(8,128)(2,1)}, bf16[64,1024]{1,0:T(8,128)(2,1)S(1)}, u32[]{:S(2)}, u32[]{:S(2)}) collective-permute-start(bf16[64,1024]{1,0:T(8,128)(2,1)} %get-tuple-element.36), channel_id=1, source_target_pairs={{0,8},{8,0},{16,24},{24,16},{1,9},{9,1},{17,25},{25,17},{2,10},{10... | collective-permute-start | bytes 393224 | tf_op jit(solution)/shard_map/ppermute | solution.py:373
  10.7 2.3 %copy-start.1 = (bf16[1,192,512]{2,1,0:T(8,128)(2,1)S(1)}, bf16[1,192,512]{2,1,0:T(8,128)(2,1)}, u32[]{:S(2)}) copy-start(bf16[1,192,512]{2,1,0:T(8,128)(2,1)} %param.10) | copy-start | bytes 589828
  10.7 2.3 %copy-start.2 = (bf16[1,192,512]{2,1,0:T(8,128)(2,1)S(1)}, bf16[1,192,512]{2,1,0:T(8,128)(2,1)}, u32[]{:S(2)}) copy-start(bf16[1,192,512]{2,1,0:T(8,128)(2,1)} %param.11) | copy-start | bytes 589828
  10.7 2.3 %copy-start.4 = (bf16[1,192,512]{2,1,0:T(8,128)(2,1)S(1)}, bf16[1,192,512]{2,1,0:T(8,128)(2,1)}, u32[]{:S(2)}) copy-start(bf16[1,192,512]{2,1,0:T(8,128)(2,1)} %param.9) | copy-start | bytes 589828
  15.8 4.9 %collective-permute-start.2 = (bf16[4,64,1024]{2,1,0:T(8,128)(2,1)S(1)}, bf16[4,64,1024]{2,1,0:T(8,128)(2,1)S(1)}, u32[]{:S(2)}, u32[]{:S(2)}) collective-permute-start(bf16[4,64,1024]{2,1,0:T(8,128)(2,1)S(1)} %get-tuple-element.34), channel_id=1, source_target_pairs={{0,1},{1,0},{2,3},{3,2},{4,5},{5,4},{6,7},{7,6},{8,9},{9,8},{10,11... | collective-permute-start | bytes 1572872 | tf_op jit(solution)/shard_map/ppermute | solution.py:384
  17.4 1.8 %copy-start.3 = (bf16[128,1024]{1,0:T(8,128)(2,1)S(1)}, bf16[128,1024]{1,0:T(8,128)(2,1)}, u32[]{:S(2)}) copy-start(bf16[128,1024]{1,0:T(8,128)(2,1)} %w.3) | copy-start | bytes 786436
  17.4 1.8 %copy-start.5 = (bf16[1,192,1024]{2,1,0:T(8,128)(2,1)S(1)}, bf16[1,192,1024]{2,1,0:T(8,128)(2,1)}, u32[]{:S(2)}) copy-start(bf16[1,192,1024]{2,1,0:T(8,128)(2,1)} %param.12) | copy-start | bytes 1179652
  17.5 1.8 %collective-permute-start.6 = (bf16[3,64,1024]{2,1,0:T(8,128)(2,1)S(1)}, bf16[3,64,1024]{2,1,0:T(8,128)(2,1)S(1)}, u32[]{:S(2)}, u32[]{:S(2)}) collective-permute-start(bf16[3,64,1024]{2,1,0:T(8,128)(2,1)S(1)} %shard_map.139), channel_id=1, source_target_pairs={{0,1},{1,0},{2,3},{3,2},{4,5},{5,4},{6,7},{7,6},{8,9},{9,8},{10,11... | collective-permute-start | bytes 1179656 | tf_op jit(solution)/shard_map/ppermute | solution.py:384
  20.6 3.7 %copy-start.6 = (bf16[192,1024]{1,0:T(8,128)(2,1)S(1)}, bf16[192,1024]{1,0:T(8,128)(2,1)}, u32[]{:S(2)}) copy-start(bf16[192,1024]{1,0:T(8,128)(2,1)} %get-tuple-element.39.stream_grad) | copy-start | bytes 1179652
  20.8 7.2 %collective-permute-start.7 = (bf16[64,1152]{1,0:T(8,128)(2,1)S(1)}, bf16[64,1152]{1,0:T(8,128)(2,1)S(1)}, u32[]{:S(2)}, u32[]{:S(2)}) collective-permute-start(bf16[64,1152]{1,0:T(8,128)(2,1)S(1)} %get-tuple-element.44), channel_id=1, source_target_pairs={{0,8},{8,0},{16,24},{24,16},{1,9},{9,1},{17,25},{25,17},{2,10},{10... | collective-permute-start | bytes 442376 | tf_op jit(solution)/shard_map/ppermute | solution.py:373
  21.8 8.8 %collective-permute-start.8 = (bf16[64,1152]{1,0:T(8,128)(2,1)S(1)}, bf16[64,1152]{1,0:T(8,128)(2,1)S(1)}, u32[]{:S(2)}, u32[]{:S(2)}) collective-permute-start(bf16[64,1152]{1,0:T(8,128)(2,1)S(1)} %get-tuple-element.45), channel_id=1, source_target_pairs={{0,16},{8,24},{16,0},{24,8},{1,17},{9,25},{17,1},{25,9},{2,18},{10... | collective-permute-start | bytes 442376 | tf_op jit(solution)/shard_map/ppermute | solution.py:373
  22.9 7.7 %collective-permute-start.9 = (bf16[64,1152]{1,0:T(8,128)(2,1)S(1)}, bf16[64,1152]{1,0:T(8,128)(2,1)S(1)}, u32[]{:S(2)}, u32[]{:S(2)}) collective-permute-start(bf16[64,1152]{1,0:T(8,128)(2,1)S(1)} %get-tuple-element.46), channel_id=1, source_target_pairs={{0,24},{8,16},{16,8},{24,0},{1,25},{9,17},{17,9},{25,1},{2,26},{10... | collective-permute-start | bytes 442376 | tf_op jit(solution)/shard_map/ppermute | solution.py:373
  31.6 11.6 %collective-permute-start.14 = (bf16[64,1152]{1,0:T(8,128)(2,1)S(1)}, bf16[64,1152]{1,0:T(8,128)(2,1)S(1)}, u32[]{:S(2)}, u32[]{:S(2)}) collective-permute-start(bf16[64,1152]{1,0:T(8,128)(2,1)S(1)} %get-tuple-element.53.refs_0_), channel_id=1, source_target_pairs={{0,6},{1,7},{2,4},{3,5},{4,2},{5,3},{6,0},{7,1},{8,14},{9,15},{10,... | collective-permute-start | bytes 442376 | tf_op jit(solution)/shard_map/ppermute | solution.py:379
  35.3 11.2 %collective-permute-start.13 = (bf16[64,1152]{1,0:T(8,128)(2,1)S(1)}, bf16[64,1152]{1,0:T(8,128)(2,1)S(1)}, u32[]{:S(2)}, u32[]{:S(2)}) collective-permute-start(bf16[64,1152]{1,0:T(8,128)(2,1)S(1)} %get-tuple-element.53.refs_0_), channel_id=1, source_target_pairs={{0,4},{1,5},{2,6},{3,7},{4,0},{5,1},{6,2},{7,3},{8,12},{9,13},{10,... | collective-permute-start | bytes 442376 | tf_op jit(solution)/shard_map/ppermute | solution.py:379
  35.3 11.2 %collective-permute-start.12 = (bf16[64,1152]{1,0:T(8,128)(2,1)S(1)}, bf16[64,1152]{1,0:T(8,128)(2,1)S(1)}, u32[]{:S(2)}, u32[]{:S(2)}) collective-permute-start(bf16[64,1152]{1,0:T(8,128)(2,1)S(1)} %get-tuple-element.53.refs_0_), channel_id=1, source_target_pairs={{0,2},{1,3},{2,0},{3,1},{4,6},{5,7},{6,4},{7,5},{8,10},{9,11},{10,... | collective-permute-start | bytes 442376 | tf_op jit(solution)/shard_map/ppermute | solution.py:379
  36.1 6.3 %collective-permute-start.10 = (bf16[96,512]{1,0:T(8,128)(2,1)S(1)}, bf16[96,512]{1,0:T(8,128)(2,1)S(1)}, u32[]{:S(2)}, u32[]{:S(2)}) collective-permute-start(bf16[96,512]{1,0:T(8,128)(2,1)S(1)} %get-tuple-element.49), channel_id=1, source_target_pairs={{0,24},{8,0},{16,8},{24,16},{1,25},{9,1},{17,9},{25,17},{2,26},{10... | collective-permute-start | bytes 294920 | tf_op jit(solution)/shard_map/ppermute | solution.py:456
  37.3 5.2 %collective-permute-start.11 = (bf16[64,512]{1,0:T(8,128)(2,1)S(1)}, bf16[64,512]{1,0:T(8,128)(2,1)S(1)}, u32[]{:S(2)}, u32[]{:S(2)}) collective-permute-start(bf16[64,512]{1,0:T(8,128)(2,1)S(1)} %get-tuple-element.50), channel_id=1, source_target_pairs={{0,8},{8,16},{16,24},{24,0},{1,9},{9,17},{17,25},{25,1},{2,10},{10... | collective-permute-start | bytes 196616 | tf_op jit(solution)/shard_map/ppermute | solution.py:457
  47.5 1.6 %collective-permute-start.15 = (f32[64,1152]{1,0:T(8,128)S(1)}, f32[64,1152]{1,0:T(8,128)S(1)}, u32[]{:S(2)}, u32[]{:S(2)}) collective-permute-start(f32[64,1152]{1,0:T(8,128)S(1)} %shard_map.145.mine), channel_id=1, source_target_pairs={{0,1},{1,0},{2,3},{3,2},{4,5},{5,4},{6,7},{7,6},{8,9},{9,8},{10,11... | collective-permute-start | bytes 884744 | tf_op jit(solution)/shard_map/ppermute | solution.py:384
  (3 other events, 3.1 us)

commit v3 on v2

--- a/solution.py
+++ b/solution.py
@@ -24,7 +24,6 @@
 BF = jnp.bfloat16
 F32 = jnp.float32
 VMEM = pl.BlockSpec(memory_space=pltpu.VMEM)
-SMEM = pl.BlockSpec(memory_space=pltpu.SMEM)
 ANY = pl.BlockSpec(memory_space=pl.ANY)
 
 
@@ -56,46 +55,48 @@
     return jax.ShapeDtypeStruct(dims, kind)
 
 
-def pack_kernel(k, v, g, w, ahead, behind, w_half, edge, sems):
+def pack_kernel(k, v, g, ahead, behind, edge, first, sems):
     rows = k.shape[0]
     feats = k.shape[1]
-    half = w.shape[0] // 2
-    core = lax.rem(lax.axis_index("dp"), 2)
     pairs = [
         (k.at[pl.ds(rows - BACK, BACK)], ahead.at[pl.ds(0, BACK)]),
         (v.at[pl.ds(rows - BACK, BACK)], ahead.at[pl.ds(BACK, BACK)]),
-        (k.at[pl.ds(0, AHEAD)], behind.at[pl.ds(0, AHEAD)]),
-        (v.at[pl.ds(0, AHEAD)], behind.at[pl.ds(AHEAD, AHEAD)]),
+        (k.at[pl.ds(0, AHEAD)], first.at[0]),
+        (v.at[pl.ds(0, AHEAD)], first.at[1]),
         (g.at[pl.ds(rows - EDGE, EDGE)], edge.at[0]),
         (g.at[pl.ds(0, EDGE)], edge.at[1]),
-        (w.at[pl.ds(pl.multiple_of(core * half, half), half)], w_half),
     ]
     copies = [pltpu.make_async_copy(a, b, sems.at[i]) for i, (a, b) in enumerate(pairs)]
     for copy in copies:
         copy.start()
     for copy in copies:
         copy.wait()
-    last = edge[0].astype(F32)[8:]
-    first = edge[1].astype(F32)[:8]
-    for out, block in ((ahead, last), (behind, first)):
+    behind[0 : 2 * BLK] = jnp.concatenate(
+        [first[0].astype(F32)[:BLK], first[1].astype(F32)[:BLK]], 0
+    ).astype(BF)
+    for out, block in ((ahead, edge[0].astype(F32)[8:]), (behind, edge[1].astype(F32)[:8])):
         two = jnp.concatenate([block[:, :feats], block[:, feats:]], 0)
         out[out.shape[0] - EDGE :] = two.astype(BF)
 
 
-def packed(k, v, g, w):
+def packed(k, v, g):
     feats = k.shape[1]
     outs = (
-        shape((2 * BACK + EDGE, feats), BF),
-        shape((2 * AHEAD + EDGE, feats), BF),
-        shape((w.shape[0] // 2, w.shape[1]), BF),
+        pltpu.VMEM((2 * BACK + EDGE, feats), BF),
+        pltpu.VMEM((2 * BLK + EDGE, feats), BF),
     )
     return pl.pallas_call(
         pack_kernel,
         out_shape=outs,
-        in_specs=[ANY] * 4,
-        out_specs=(VMEM,) * 3,
-        scratch_shapes=[pltpu.VMEM((2, EDGE, g.shape[1]), BF), pltpu.SemaphoreType.DMA((7,))],
-    )(k, v, g, w)
+        in_specs=[ANY] * 3,
+        out_specs=(VMEM,) * 2,
+        scratch_shapes=[
+            pltpu.VMEM((2, EDGE, g.shape[1]), BF),
+            pltpu.VMEM((2, AHEAD, feats), BF),
+            pltpu.SemaphoreType.DMA((6,)),
+        ],
+        compiler_params=pltpu.CompilerParams(vmem_limit_bytes=40 * 1024 * 1024),
+    )(*[pltpu.with_memory_space_constraint(x, pltpu.HBM) for x in (k, v, g)])
 
 
 def head_of(dims):
@@ -122,7 +123,9 @@
     for at, ext, local in ((0, kx, k), (1, vx, v)):
         ext[0:BACK] = near[at * BACK : (at + 1) * BACK]
         ext[BACK : BACK + rows] = local[...]
-        ext[BACK + rows :] = far[at * AHEAD : (at + 1) * AHEAD]
+        after = far[0 : 2 * BLK].astype(F32)[at * BLK : (at + 1) * BLK]
+        zeros = jnp.zeros((AHEAD - BLK, after.shape[1]), F32)
+        ext[BACK + rows :] = jnp.concatenate([after, zeros], 0).astype(BF)
 
 
 def allowed_in(tile, base, length, back, ahead):
@@ -154,7 +157,7 @@
 def fill_rims(gx, at, near, far, base, rows, length):
     feats = near.shape[1]
     before = near[2 * BACK :].astype(F32)
-    after = far[2 * AHEAD :].astype(F32)
+    after = far[2 * BLK :].astype(F32)
     for part in range(2):
         cols = slice(part * feats, (part + 1) * feats)
         here = slice(part * 8, (part + 1) * 8)
@@ -175,13 +178,17 @@
         out[out_at : out_at + count, cols] = jnp.where(frame < length, total, 0.0).astype(BF)
 
 
-def inner_conv_kernel(g, taps, lengths, out, gx):
+def inner_conv_kernel(g, taps, w, lengths, offsets, out, w_half, gx):
     rows = g.shape[0]
     base = lax.axis_index("cp") * rows
+    half = w.shape[0] // 2
+    core = lax.rem(lax.axis_index("dp"), 2)
+    w_half[...] = w[pl.ds(pl.multiple_of(core * half, half), half)]
     gx[0:8] = jnp.zeros((8, gx.shape[1]), F32)
     gx[8 + rows :] = jnp.zeros((8, gx.shape[1]), F32)
-    gx[8 : 8 + rows] = masked(g[...], base, lengths[0])
-    convolve(out, 0, gx, 8, taps, base, rows, lengths[0])
+    length = lengths[...]
+    gx[8 : 8 + rows] = masked(g[...], base, length)
+    convolve(out, 0, gx, 8, taps, base, rows, length)
 
 
 def forward_kernel(
@@ -192,11 +199,11 @@
     place = lax.axis_index("cp")
     core = lax.rem(lax.axis_index("dp"), 2)
     base = place * rows
-    length = lengths[0]
+    length = lengths[...]
     fill_ext(kx, vx, k, v, near, far)
     for tile in range(rows // TILE):
         start = tile * TILE
-        allowed = allowed_in(tile, base, length, offsets[0, 0], offsets[0, 1])
+        allowed = allowed_in(tile, base, length, offsets[:, 0:1], offsets[:, 1:2])
         frame = base + start + lax.broadcasted_iota(jnp.int32, (TILE, FEATS), 0)
         for group in range(feats // FEATS):
             cols = slice(group * FEATS, (group + 1) * FEATS)
@@ -245,11 +252,10 @@
     return terms[0]
 
 
-def cp_sum_kernel(after, own, *refs):
-    got = refs[:-5]
-    back, onward, part, back_out, onward_out = refs[-5:]
-    total = tree_sum([own[...]] + [ref[...].astype(F32) for ref in got])
-    part[...] = total.astype(BF)
+def cp_sum_kernel(after, back, onward, *refs):
+    got = refs[:-3]
+    part, back_out, onward_out = refs[-3:]
+    part[...] = tree_sum([ref[...].astype(F32) for ref in got]).astype(BF)
     back_out[...] = back[...]
     onward_out[...] = onward[...]
 
@@ -258,7 +264,7 @@
     refs[-1][...] = tree_sum([ref[...].astype(F32) for ref in refs[:-1]])
 
 
-def final_kernel(mine, theirs, weight_grad, conv_grad):
+def final_kernel(after, mine, theirs, weight_grad, conv_grad):
     half = mine.shape[0]
     width = weight_grad.shape[1]
     core = lax.rem(lax.axis_index("dp"), 2)
@@ -283,7 +289,7 @@
     place = lax.axis_index("cp")
     core = lax.rem(lax.axis_index("dp"), 2)
     base = place * rows
-    length = lengths[0]
+    length = lengths[...]
     shard = w.shape[0]
     half = shard // 2
     wx[pl.ds(pl.multiple_of(place * shard, shard), shard)] = w[...]
@@ -309,18 +315,18 @@
 
 def backward_kernel(
     after, q, k, v, near, far, stream_grad, wx, lengths, offsets,
-    query_g, key_g, value_g, back, onward, kx, vx, kg, vg, ag,
+    query_g, key_g, value_g, back, onward, token, kx, vx, kg, vg, ag,
 ):
     rows, feats = q.shape
     base = lax.axis_index("cp") * rows
-    length = lengths[0]
+    length = lengths[...]
     ag[...] = nt(stream_grad[...], wx[...]).astype(BF)
     fill_ext(kx, vx, k, v, near, far)
     kg[...] = jnp.zeros_like(kg)
     vg[...] = jnp.zeros_like(vg)
     for tile in range(rows // TILE):
         start = tile * TILE
-        allowed = allowed_in(tile, base, length, offsets[0, 0], offsets[0, 1])
+        allowed = allowed_in(tile, base, length, offsets[:, 0:1], offsets[:, 1:2])
         span = slice(start, start + REACH)
         for group in range(feats // FEATS):
             cols = slice(group * FEATS, (group + 1) * FEATS)
@@ -339,19 +345,22 @@
     value_g[...] = vg[BACK : BACK + rows]
     for at, ext in ((0, kg), (1, vg)):
         back[at * BACK : (at + 1) * BACK] = ext[0:BACK].astype(BF)
-        onward[at * AHEAD : (at + 1) * AHEAD] = ext[BACK + rows :].astype(BF)
-
-
-def join_kernel(key_g, value_g, last, first, key_out, value_out):
+    span = slice(BACK + rows, BACK + rows + BLK)
+    onward[...] = jnp.concatenate([kg[span], vg[span]], 0).astype(BF)
+    token[...] = jnp.zeros_like(token)
+
+
+def join_kernel(key_g, value_g, last, first, key_out, value_out, token):
     rows = key_g.shape[0]
     for at, grad, out in ((0, key_g, key_out), (1, value_g, value_out)):
-        out[0:AHEAD] = (
-            grad[0:AHEAD] + first[at * AHEAD : (at + 1) * AHEAD].astype(F32)
-        ).astype(BF)
+        before = first[...].astype(F32)[at * BLK : (at + 1) * BLK]
+        zeros = jnp.zeros((AHEAD - BLK, before.shape[1]), F32)
+        out[0:AHEAD] = (grad[0:AHEAD] + jnp.concatenate([before, zeros], 0)).astype(BF)
         out[AHEAD : rows - BACK] = grad[AHEAD : rows - BACK].astype(BF)
         out[rows - BACK :] = (
             grad[rows - BACK :] + last[at * BACK : (at + 1) * BACK].astype(F32)
         ).astype(BF)
+    token[...] = jnp.zeros_like(token)
 
 
 def body(
@@ -364,6 +373,7 @@
     q, k, v, g, stream = queries[0], key_rows[0], value_rows[0], out_grad[0], stream_in[0]
     shard = out_weight.shape[0]
     half = shard // 2
+    lengths = lengths.reshape(1, 1)
     ext = rows + BACK + AHEAD
     upward = [(i, (i + 1) % cps) for i in range(cps)]
     downward = [(i, (i - 1) % cps) for i in range(cps)]
@@ -383,17 +393,17 @@
     def over_core(array):
         return lax.ppermute(array, "dp", [(i, i ^ 1) for i in range(dps)])
 
-    ahead, behind, w_half = packed(k, v, g, out_weight)
+    ahead, behind = packed(k, v, g)
     near = lax.ppermute(ahead, "cp", upward)
     far = lax.ppermute(behind, "cp", downward)
+    inner, w_half = call(
+        inner_conv_kernel,
+        (shape((rows, width), BF), shape((half, width), BF)),
+        [VMEM] * 5,
+        (g, conv_weight, out_weight, lengths, offsets),
+        [pltpu.VMEM((rows + 16, width), F32)],
+    )
     w_got = over_cp([w_half] * (cps - 1))
-    inner = call(
-        inner_conv_kernel,
-        shape((rows, width), BF),
-        [VMEM] * 2 + [SMEM],
-        (g, conv_weight, lengths),
-        [pltpu.VMEM((rows + 16, width), F32)],
-    )
     ext_scratch = [pltpu.VMEM((ext, feats), BF)] * 2
     stream_grad, send, keep, att = call(
         forward_kernel,
@@ -403,7 +413,7 @@
             shape((cps, half, width), F32),
             shape((rows, feats), BF),
         ),
-        [VMEM] * 8 + [SMEM] * 2,
+        [VMEM] * 10,
         (q, k, v, near, far, g, conv_weight, inner, lengths, offsets),
         ext_scratch + [pltpu.VMEM((64, width), F32), pltpu.VMEM((feats, rows), BF)],
     )
@@ -419,7 +429,7 @@
     conv, wx = call(
         conv_kernel,
         (shape((8, width), F32), shape((feats, width), BF)),
-        [VMEM] * 7 + [SMEM] + [VMEM] * (cps - 1),
+        [VMEM] * (7 + cps),
         (att, out_weight, passed, stream, g, near, far, lengths, *w_got),
         [pltpu.VMEM((rows + 16, width), F32), pltpu.VMEM((rows, width), F32)],
     )
@@ -431,16 +441,18 @@
         (keep, core_got, conv),
     )
     cp_got = over_cp(pieces)
-    query_g, key_g, value_g, back, onward = call(
+    token = shape((8, 128), F32)
+    query_g, key_g, value_g, back, onward, bwd_done = call(
         backward_kernel,
         (
             shape((rows, feats), BF),
             shape((rows, feats), F32),
             shape((rows, feats), F32),
             shape((2 * BACK, feats), BF),
-            shape((2 * AHEAD, feats), BF),
+            shape((2 * BLK, feats), BF),
+            token,
         ),
-        [ANY] + [VMEM] * 7 + [SMEM] * 2,
+        [ANY] + [VMEM] * 9,
         (own, q, k, v, near, far, stream_grad, wx, lengths, offsets),
         ext_scratch
         + [pltpu.VMEM((ext, feats), F32)] * 2
@@ -450,14 +462,14 @@
     part, back, onward = call(
         cp_sum_kernel,
         (shape((half, wide), BF), shape(back.shape, BF), shape(onward.shape, BF)),
-        [ANY] + [VMEM] * (cps + 2),
-        (query_g, own, *cp_got, back, onward),
+        [VMEM] * (cps + 3),
+        (bwd_done, back, onward, own, *cp_got),
     )
     last = lax.ppermute(back, "cp", downward)
     first = lax.ppermute(onward, "cp", upward)
-    key_grad, value_grad = call(
+    key_grad, value_grad, join_done = call(
         join_kernel,
-        (shape((rows, feats), BF),) * 2,
+        (shape((rows, feats), BF),) * 2 + (token,),
         [VMEM] * 4,
         (key_g, value_g, last, first),
     )
@@ -472,14 +484,14 @@
         mine = call(
             z_sum_kernel,
             shape((half, wide), F32),
-            [ANY] + [VMEM] * floors,
-            (key_grad, part, *over_z(part)),
+            [VMEM] * (floors + 1),
+            (join_done, part, *over_z(part)),
         )
         weight_grad, conv_grad = call(
             final_kernel,
             (shape((shard, width), F32), shape((KW, width), F32)),
-            [VMEM] * 2,
-            (mine, over_core(mine)),
+            [VMEM] * 3,
+            (join_done, mine, over_core(mine)),
         )
     return (
         query_g[None],

time: 50.2 us -> 48.1 us (0.958)
  Pallas kernels: 12.6 us -> 11.2 us
  local copies, waits for them, and re-layouts: 1.9 us -> 0.65 us
    unnamed x22 -> x18, local copies, waits for them, and re-layouts: 1.9 us -> 0.65 us
    ppermute x1, waiting for transfers between devices: 1.24 us -> 0.01 us  [body(): far = lax.ppermute(behind, 'cp', downward)]
    ppermute x6, waiting for transfers between devices: 4.27 us -> 5.34 us  [over_cp(): lax.ppermute(array, 'cp', [(i, i ^ by) for i in range(cps)])]
    pallas_call x1, Pallas kernels: 1.86 us -> 0.97 us  [packed(): pl.pallas_call(pack_kernel, out_shape=outs, in_specs=[ANY] * 3, out_specs...]
    pallas_call x10, Pallas kernels: 10.7 us -> 10.2 us  [call(): pl.pallas_call(kernel, out_shape=outs, in_specs=ins, out_specs=jax.tree.m...]
    ppermute x1, starting transfers between devices: 1.17 us -> 1.7 us  [body(): last = lax.ppermute(back, 'cp', downward)]
    ppermute x1, starting transfers between devices: 0.85 us -> 0.33 us  [body(): first = lax.ppermute(onward, 'cp', upward)]
  transfers between devices with their start and end apart: 16 -> 16, of which waited for: 8 -> 10; matrix products, arithmetic and copies ran while one was open for 0% -> 0% of each run, Pallas kernels for 19% -> 19%
where the time goes in v3:
time: 48.1 us; the launch traced here: 47.9 us
  starting transfers between devices  17.7 us (37%)
  waiting for transfers between devices  16.9 us (35%)
  Pallas kernels  11.2 us (23%)
  between operations  1.45 us (3%)
  local copies, waits for them, and re-layouts  0.65 us (1%)
    pallas_call x10, Pallas kernels, call(): pl.pallas_call(kernel, out_shape=outs, in_specs=ins, out_specs=jax.tree.m...  10.2 us
    ppermute x6, starting transfers between devices, over_cp(): lax.ppermute(array, 'cp', [(i, i ^ by) for i in range(cps)])  7.11 us
    ppermute x6, waiting for transfers between devices, over_cp(): lax.ppermute(array, 'cp', [(i, i ^ by) for i in range(cps)])  5.34 us
    ppermute x1, waiting for transfers between devices, body(): first = lax.ppermute(onward, 'cp', upward)  4.66 us
    ppermute x3, starting transfers between devices, over_z(): lax.ppermute(array, 'dp', [(i, i ^ 2 * by) for i in range(dps)])  4.45 us
    ppermute x3, waiting for transfers between devices, over_z(): lax.ppermute(array, 'dp', [(i, i ^ 2 * by) for i in range(dps)])  3.63 us
    ppermute x3, waiting for transfers between devices, over_core(): return lax.ppermute(array, 'dp', [(i, i ^ 1) for i in range(dps)])  3.28 us
    ppermute x1, starting transfers between devices, body(): near = lax.ppermute(ahead, 'cp', upward)  2.99 us
  transfers between devices with their start and end apart: 16, of which 10 were waited for; matrix products, arithmetic and copies ran while one was open for 0% of the time, Pallas kernels for 19%

profile of v3, /device:TPU:0, one launch (start us, length us, event | category | flops | bytes accessed | tf_op | source)
XLA Modules:
  0.0 47.9 jit_solution(12149835344889618720)
XLA Ops:
  0.7 1.0 %shard_map.136 = (bf16[112,512]{1,0:T(8,128)(2,1)S(1)}, bf16[64,512]{1,0:T(8,128)(2,1)S(1)}) custom-call(bf16[192,512]{1,0:T(8,128)(2,1)} %bitcast.18, bf16[192,512]{1,0:T(8,128)(2,1)} %bitcast.21, bf16[192,1024]{1,0:T(8,128)(2,1)} %bitcast.14), custom_call_target="tpu_custom_call" | custom-call | tf_op jit(solution)/shard_map/pallas_call | solution.py:88
  1.6 3.0 %collective-permute-start = (bf16[112,512]{1,0:T(8,128)(2,1)S(1)}, bf16[112,512]{1,0:T(8,128)(2,1)S(1)}, u32[]{:S(2)}, u32[]{:S(2)}) collective-permute-start(bf16[112,512]{1,0:T(8,128)(2,1)S(1)} %get-tuple-element.34), channel_id=1, source_target_pairs={{0,8},{8,16},{16,24},{24,0},{1,9},{9,17},{17,25},{25,1},{2,10},{10... | collective-permute-start | bytes 344072 | tf_op jit(solution)/shard_map/ppermute | solution.py:397
  4.6 1.0 %collective-permute-start.1 = (bf16[64,512]{1,0:T(8,128)(2,1)S(1)}, bf16[64,512]{1,0:T(8,128)(2,1)S(1)}, u32[]{:S(2)}, u32[]{:S(2)}) collective-permute-start(bf16[64,512]{1,0:T(8,128)(2,1)S(1)} %get-tuple-element.35), channel_id=1, source_target_pairs={{0,24},{8,0},{16,8},{24,16},{1,25},{9,1},{17,9},{25,17},{2,26},{10... | collective-permute-start | bytes 196616 | tf_op jit(solution)/shard_map/ppermute | solution.py:398
  6.4 0.6 %copy-done.8 = s32[1,2]{1,0:T(1,128)S(1)} copy-done((s32[1,2]{1,0:T(1,128)S(1)}, s32[1,2]{1,0:T(1,128)}, u32[]{:S(2)}) %copy-start.8) | copy-done | bytes 32
  7.0 1.0 %shard_map.137 = (bf16[192,1024]{1,0:T(8,128)(2,1)S(1)}, bf16[64,1024]{1,0:T(8,128)(2,1)S(1)}) custom-call(bf16[192,1024]{1,0:T(8,128)(2,1)S(1)} %bitcast.15, f32[7,1024]{1,0:T(8,128)S(1)} %copy-done.7, bf16[128,1024]{1,0:T(8,128)(2,1)S(1)} %copy-done.3, s32[1,1]{1,0:T(1,128)} %bitcast.10.lengths, s32[1,2]{1,0:T(1,128)S(1)} %copy-done.8), custom_call_target="tpu_custom_call" | custom-call | tf_op jit(solution)/shard_map/pallas_call | solution.py:43
  8.0 2.0 %collective-permute-start.5 = (bf16[64,1024]{1,0:T(8,128)(2,1)S(1)}, bf16[64,1024]{1,0:T(8,128)(2,1)S(1)}, u32[]{:S(2)}, u32[]{:S(2)}) collective-permute-start(bf16[64,1024]{1,0:T(8,128)(2,1)S(1)} %get-tuple-element.40), channel_id=1, source_target_pairs={{0,24},{8,16},{16,8},{24,0},{1,25},{9,17},{17,9},{25,1},{2,26},{10... | collective-permute-start | bytes 393224 | tf_op jit(solution)/shard_map/ppermute | solution.py:383
  10.6 1.0 %collective-permute-start.3 = (bf16[64,1024]{1,0:T(8,128)(2,1)S(1)}, bf16[64,1024]{1,0:T(8,128)(2,1)S(1)}, u32[]{:S(2)}, u32[]{:S(2)}) collective-permute-start(bf16[64,1024]{1,0:T(8,128)(2,1)S(1)} %get-tuple-element.40), channel_id=1, source_target_pairs={{0,8},{8,0},{16,24},{24,16},{1,9},{9,1},{17,25},{25,17},{2,10},{10... | collective-permute-start | bytes 393224 | tf_op jit(solution)/shard_map/ppermute | solution.py:383
  11.6 2.8 %shard_map.138 = (bf16[192,1024]{1,0:T(8,128)(2,1)}, bf16[4,64,1024]{2,1,0:T(8,128)(2,1)S(1)}, f32[4,64,1024]{2,1,0:T(8,128)S(1)}, bf16[192,512]{1,0:T(8,128)(2,1)S(1)}) custom-call(bf16[192,512]{1,0:T(8,128)(2,1)S(1)} %bitcast.24, bf16[192,512]{1,0:T(8,128)(2,1)S(1)} %bitcast.19, bf16[192,512]{1,0:T(8,128)(2,1)S(1)} %bitcast.22, ...), custom_call_target="tpu_custom_call" | custom-call | tf_op jit(solution)/shard_map/pallas_call | solution.py:43
  14.4 0.7 %collective-permute-done.5.refs_2_ = bf16[64,1024]{1,0:T(8,128)(2,1)S(1)} collective-permute-done((bf16[64,1024]{1,0:T(8,128)(2,1)S(1)}, bf16[64,1024]{1,0:T(8,128)(2,1)S(1)}, u32[]{:S(2)}, u32[]{:S(2)}) %collective-permute-start.5) | collective-permute-done | bytes 131104 | tf_op jit(solution)/shard_map/ppermute | solution.py:383
  15.1 1.7 %collective-permute-done.4.refs_1_ = bf16[64,1024]{1,0:T(8,128)(2,1)S(1)} collective-permute-done((bf16[64,1024]{1,0:T(8,128)(2,1)S(1)}, bf16[64,1024]{1,0:T(8,128)(2,1)S(1)}, u32[]{:S(2)}, u32[]{:S(2)}) %collective-permute-start.4) | collective-permute-done | bytes 131104 | tf_op jit(solution)/shard_map/ppermute | solution.py:383
  17.1 1.7 %collective-permute-done.6.passed = bf16[3,64,1024]{2,1,0:T(8,128)(2,1)S(1)} collective-permute-done((bf16[3,64,1024]{2,1,0:T(8,128)(2,1)S(1)}, bf16[3,64,1024]{2,1,0:T(8,128)(2,1)S(1)}, u32[]{:S(2)}, u32[]{:S(2)}) %collective-permute-start.6) | collective-permute-done | bytes 393248 | tf_op jit(solution)/shard_map/ppermute | solution.py:394
  18.8 1.4 %shard_map.140 = (f32[8,1024]{1,0:T(8,128)S(1)}, bf16[512,1024]{1,0:T(8,128)(2,1)S(1)}) custom-call(bf16[192,512]{1,0:T(8,128)(2,1)S(1)} %get-tuple-element.39.after.att, bf16[128,1024]{1,0:T(8,128)(2,1)S(1)} %copy-done.3, bf16[3,64,1024]{2,1,0:T(8,128)(2,1)S(1)} %collective-permute-done.6.passed, bf16[192,1024]{1,0:T(8,128)(2,1)S(1)} %bitcast.26, ...), custom_call_target="tpu_custom_call" | custom-call | tf_op jit(solution)/shard_map/pallas_call | solution.py:43
  20.9 1.5 %collective-permute-start.8 = (bf16[64,1152]{1,0:T(8,128)(2,1)S(1)}, bf16[64,1152]{1,0:T(8,128)(2,1)S(1)}, u32[]{:S(2)}, u32[]{:S(2)}) collective-permute-start(bf16[64,1152]{1,0:T(8,128)(2,1)S(1)} %get-tuple-element.52), channel_id=1, source_target_pairs={{0,16},{8,24},{16,0},{24,8},{1,17},{9,25},{17,1},{25,9},{2,18},{10... | collective-permute-start | bytes 442376 | tf_op jit(solution)/shard_map/ppermute | solution.py:383
  22.4 1.5 %collective-permute-start.9 = (bf16[64,1152]{1,0:T(8,128)(2,1)S(1)}, bf16[64,1152]{1,0:T(8,128)(2,1)S(1)}, u32[]{:S(2)}, u32[]{:S(2)}) collective-permute-start(bf16[64,1152]{1,0:T(8,128)(2,1)S(1)} %get-tuple-element.53), channel_id=1, source_target_pairs={{0,24},{8,16},{16,8},{24,0},{1,25},{9,17},{17,9},{25,1},{2,26},{10... | collective-permute-start | bytes 442376 | tf_op jit(solution)/shard_map/ppermute | solution.py:383
  23.9 3.1 %shard_map.142 = (bf16[192,512]{1,0:T(8,128)(2,1)}, f32[192,512]{1,0:T(8,128)S(1)}, f32[192,512]{1,0:T(8,128)S(1)}, bf16[96,512]{1,0:T(8,128)(2,1)S(1)}, bf16[48...) custom-call(f32[64,1152]{1,0:T(8,128)S(1)} %get-tuple-element.42.after.refs_0_, bf16[192,512]{1,0:T(8,128)(2,1)S(1)} %bitcast.25, ...), custom_call_target="tpu_custom_call" | custom-call | bytes 10485760 | tf_op jit(solution)/shard_map/pallas_call | solution.py:43
  27.4 2.3 %collective-permute-done.9.refs_3_ = bf16[64,1152]{1,0:T(8,128)(2,1)S(1)} collective-permute-done((bf16[64,1152]{1,0:T(8,128)(2,1)S(1)}, bf16[64,1152]{1,0:T(8,128)(2,1)S(1)}, u32[]{:S(2)}, u32[]{:S(2)}) %collective-permute-start.9) | collective-permute-done | bytes 147488 | tf_op jit(solution)/shard_map/ppermute | solution.py:383
  29.8 3.7 %collective-permute-start.14 = (bf16[64,1152]{1,0:T(8,128)(2,1)S(1)}, bf16[64,1152]{1,0:T(8,128)(2,1)S(1)}, u32[]{:S(2)}, u32[]{:S(2)}) collective-permute-start(bf16[64,1152]{1,0:T(8,128)(2,1)S(1)} %get-tuple-element.59.refs_0_), channel_id=1, source_target_pairs={{0,6},{1,7},{2,4},{3,5},{4,2},{5,3},{6,0},{7,1},{8,14},{9,15},{10,... | collective-permute-start | bytes 442376 | tf_op jit(solution)/shard_map/ppermute | solution.py:389
  33.5 0.8 %collective-permute-start.12 = (bf16[64,1152]{1,0:T(8,128)(2,1)S(1)}, bf16[64,1152]{1,0:T(8,128)(2,1)S(1)}, u32[]{:S(2)}, u32[]{:S(2)}) collective-permute-start(bf16[64,1152]{1,0:T(8,128)(2,1)S(1)} %get-tuple-element.59.refs_0_), channel_id=1, source_target_pairs={{0,2},{1,3},{2,0},{3,1},{4,6},{5,7},{6,4},{7,5},{8,10},{9,11},{10,... | collective-permute-start | bytes 442376 | tf_op jit(solution)/shard_map/ppermute | solution.py:389
  34.3 1.7 %collective-permute-start.10 = (bf16[96,512]{1,0:T(8,128)(2,1)S(1)}, bf16[96,512]{1,0:T(8,128)(2,1)S(1)}, u32[]{:S(2)}, u32[]{:S(2)}) collective-permute-start(bf16[96,512]{1,0:T(8,128)(2,1)S(1)} %get-tuple-element.54), channel_id=1, source_target_pairs={{0,24},{8,0},{16,8},{24,16},{1,25},{9,1},{17,9},{25,17},{2,26},{10... | collective-permute-start | bytes 294920 | tf_op jit(solution)/shard_map/ppermute | solution.py:468
  36.3 4.7 %collective-permute-done.11.first = bf16[48,512]{1,0:T(8,128)(2,1)S(1)} collective-permute-done((bf16[48,512]{1,0:T(8,128)(2,1)S(1)}, bf16[48,512]{1,0:T(8,128)(2,1)S(1)}, u32[]{:S(2)}, u32[]{:S(2)}) %collective-permute-start.11) | collective-permute-done | bytes 49184 | tf_op jit(solution)/shard_map/ppermute | solution.py:469
  40.9 0.8 %shard_map.144 = (bf16[192,512]{1,0:T(8,128)(2,1)}, bf16[192,512]{1,0:T(8,128)(2,1)}, f32[8,128]{1,0:T(8,128)S(1)}) custom-call(f32[192,512]{1,0:T(8,128)S(1)} %get-tuple-element.46.key_g, f32[192,512]{1,0:T(8,128)S(1)} %get-tuple-element.47.value_g, bf16[96,512]{1,0:T(8,128)(2,1)S(1)} %collective-permute-done.10.last, ...), custom_call_target="tpu_custom_call" | custom-call | tf_op jit(solution)/shard_map/pallas_call | solution.py:43
  41.7 3.6 %collective-permute-done.13.refs_2_ = bf16[64,1152]{1,0:T(8,128)(2,1)S(1)} collective-permute-done((bf16[64,1152]{1,0:T(8,128)(2,1)S(1)}, bf16[64,1152]{1,0:T(8,128)(2,1)S(1)}, u32[]{:S(2)}, u32[]{:S(2)}) %collective-permute-start.13) | collective-permute-done | bytes 147488 | tf_op jit(solution)/shard_map/ppermute | solution.py:389
  45.5 1.6 %collective-permute-done.15.theirs = f32[64,1152]{1,0:T(8,128)S(1)} collective-permute-done((f32[64,1152]{1,0:T(8,128)S(1)}, f32[64,1152]{1,0:T(8,128)S(1)}, u32[]{:S(2)}, u32[]{:S(2)}) %collective-permute-start.15) | collective-permute-done | bytes 294944 | tf_op jit(solution)/shard_map/ppermute | solution.py:394
  47.1 0.8 %shard_map.146 = (f32[128,1024]{1,0:T(8,128)}, f32[7,1024]{1,0:T(8,128)}) custom-call(f32[8,128]{1,0:T(8,128)S(1)} %get-tuple-element.58.after, f32[64,1152]{1,0:T(8,128)S(1)} %shard_map.145.mine, f32[64,1152]{1,0:T(8,128)S(1)} %collective-permute-done.15.theirs), custom_call_target="tpu_custom_call" | custom-call | tf_op jit(solution)/shard_map/pallas_call | solution.py:43
  (37 shorter events, 2.6 us)
Async XLA Ops:
  0.6 5.7 %copy-start = (bf16[1,192,1024]{2,1,0:T(8,128)(2,1)S(1)}, bf16[1,192,1024]{2,1,0:T(8,128)(2,1)}, u32[]{:S(2)}) copy-start(bf16[1,192,1024]{2,1,0:T(8,128)(2,1)} %param.13) | copy-start | bytes 1179652
  0.6 5.7 %copy-start.3 = (bf16[128,1024]{1,0:T(8,128)(2,1)S(1)}, bf16[128,1024]{1,0:T(8,128)(2,1)}, u32[]{:S(2)}) copy-start(bf16[128,1024]{1,0:T(8,128)(2,1)} %w.3) | copy-start | bytes 786436
  0.7 5.7 %copy-start.7 = (f32[7,1024]{1,0:T(8,128)S(1)}, f32[7,1024]{1,0:T(8,128)}, u32[]{:S(2)}) copy-start(f32[7,1024]{1,0:T(8,128)} %taps.3) | copy-start | bytes 86020
  1.6 9.9 %collective-permute-start = (bf16[112,512]{1,0:T(8,128)(2,1)S(1)}, bf16[112,512]{1,0:T(8,128)(2,1)S(1)}, u32[]{:S(2)}, u32[]{:S(2)}) collective-permute-start(bf16[112,512]{1,0:T(8,128)(2,1)S(1)} %get-tuple-element.34), channel_id=1, source_target_pairs={{0,8},{8,16},{16,24},{24,0},{1,9},{9,17},{17,25},{25,1},{2,10},{10... | collective-permute-start | bytes 344072 | tf_op jit(solution)/shard_map/ppermute | solution.py:397
  4.6 7.0 %collective-permute-start.1 = (bf16[64,512]{1,0:T(8,128)(2,1)S(1)}, bf16[64,512]{1,0:T(8,128)(2,1)S(1)}, u32[]{:S(2)}, u32[]{:S(2)}) collective-permute-start(bf16[64,512]{1,0:T(8,128)(2,1)S(1)} %get-tuple-element.35), channel_id=1, source_target_pairs={{0,24},{8,0},{16,8},{24,16},{1,25},{9,1},{17,9},{25,17},{2,26},{10... | collective-permute-start | bytes 196616 | tf_op jit(solution)/shard_map/ppermute | solution.py:398
  7.0 4.6 %copy-start.1 = (bf16[1,192,512]{2,1,0:T(8,128)(2,1)S(1)}, bf16[1,192,512]{2,1,0:T(8,128)(2,1)}, u32[]{:S(2)}) copy-start(bf16[1,192,512]{2,1,0:T(8,128)(2,1)} %param.10) | copy-start | bytes 589828
  7.0 4.6 %copy-start.2 = (bf16[1,192,512]{2,1,0:T(8,128)(2,1)S(1)}, bf16[1,192,512]{2,1,0:T(8,128)(2,1)}, u32[]{:S(2)}) copy-start(bf16[1,192,512]{2,1,0:T(8,128)(2,1)} %param.11) | copy-start | bytes 589828
  7.0 4.6 %copy-start.4 = (bf16[1,192,512]{2,1,0:T(8,128)(2,1)S(1)}, bf16[1,192,512]{2,1,0:T(8,128)(2,1)}, u32[]{:S(2)}) copy-start(bf16[1,192,512]{2,1,0:T(8,128)(2,1)} %param.9) | copy-start | bytes 589828
  8.0 7.1 %collective-permute-start.5 = (bf16[64,1024]{1,0:T(8,128)(2,1)S(1)}, bf16[64,1024]{1,0:T(8,128)(2,1)S(1)}, u32[]{:S(2)}, u32[]{:S(2)}) collective-permute-start(bf16[64,1024]{1,0:T(8,128)(2,1)S(1)} %get-tuple-element.40), channel_id=1, source_target_pairs={{0,24},{8,16},{16,8},{24,0},{1,25},{9,17},{17,9},{25,1},{2,26},{10... | collective-permute-start | bytes 393224 | tf_op jit(solution)/shard_map/ppermute | solution.py:383
  10.1 6.7 %collective-permute-start.4 = (bf16[64,1024]{1,0:T(8,128)(2,1)S(1)}, bf16[64,1024]{1,0:T(8,128)(2,1)S(1)}, u32[]{:S(2)}, u32[]{:S(2)}) collective-permute-start(bf16[64,1024]{1,0:T(8,128)(2,1)S(1)} %get-tuple-element.40), channel_id=1, source_target_pairs={{0,16},{8,24},{16,0},{24,8},{1,17},{9,25},{17,1},{25,9},{2,18},{10... | collective-permute-start | bytes 393224 | tf_op jit(solution)/shard_map/ppermute | solution.py:383
  10.6 6.4 %collective-permute-start.3 = (bf16[64,1024]{1,0:T(8,128)(2,1)S(1)}, bf16[64,1024]{1,0:T(8,128)(2,1)S(1)}, u32[]{:S(2)}, u32[]{:S(2)}) collective-permute-start(bf16[64,1024]{1,0:T(8,128)(2,1)S(1)} %get-tuple-element.40), channel_id=1, source_target_pairs={{0,8},{8,0},{16,24},{24,16},{1,9},{9,1},{17,25},{25,17},{2,10},{10... | collective-permute-start | bytes 393224 | tf_op jit(solution)/shard_map/ppermute | solution.py:383
  14.4 5.8 %collective-permute-start.2 = (bf16[4,64,1024]{2,1,0:T(8,128)(2,1)S(1)}, bf16[4,64,1024]{2,1,0:T(8,128)(2,1)S(1)}, u32[]{:S(2)}, u32[]{:S(2)}) collective-permute-start(bf16[4,64,1024]{2,1,0:T(8,128)(2,1)S(1)} %get-tuple-element.38), channel_id=1, source_target_pairs={{0,1},{1,0},{2,3},{3,2},{4,5},{5,4},{6,7},{7,6},{8,9},{9,8},{10,11... | collective-permute-start | bytes 1572872 | tf_op jit(solution)/shard_map/ppermute | solution.py:394
  17.0 1.8 %copy-start.5 = (bf16[1,192,1024]{2,1,0:T(8,128)(2,1)S(1)}, bf16[1,192,1024]{2,1,0:T(8,128)(2,1)}, u32[]{:S(2)}) copy-start(bf16[1,192,1024]{2,1,0:T(8,128)(2,1)} %param.12) | copy-start | bytes 1179652
  17.0 1.8 %collective-permute-start.6 = (bf16[3,64,1024]{2,1,0:T(8,128)(2,1)S(1)}, bf16[3,64,1024]{2,1,0:T(8,128)(2,1)S(1)}, u32[]{:S(2)}, u32[]{:S(2)}) collective-permute-start(bf16[3,64,1024]{2,1,0:T(8,128)(2,1)S(1)} %shard_map.139), channel_id=1, source_target_pairs={{0,1},{1,0},{2,3},{3,2},{4,5},{5,4},{6,7},{7,6},{8,9},{9,8},{10,11... | collective-permute-start | bytes 1179656 | tf_op jit(solution)/shard_map/ppermute | solution.py:394
  20.2 3.7 %copy-start.6 = (bf16[192,1024]{1,0:T(8,128)(2,1)S(1)}, bf16[192,1024]{1,0:T(8,128)(2,1)}, u32[]{:S(2)}) copy-start(bf16[192,1024]{1,0:T(8,128)(2,1)} %get-tuple-element.43.stream_grad) | copy-start | bytes 1179652
  20.3 6.8 %collective-permute-start.7 = (bf16[64,1152]{1,0:T(8,128)(2,1)S(1)}, bf16[64,1152]{1,0:T(8,128)(2,1)S(1)}, u32[]{:S(2)}, u32[]{:S(2)}) collective-permute-start(bf16[64,1152]{1,0:T(8,128)(2,1)S(1)} %get-tuple-element.51), channel_id=1, source_target_pairs={{0,8},{8,0},{16,24},{24,16},{1,9},{9,1},{17,25},{25,17},{2,10},{10... | collective-permute-start | bytes 442376 | tf_op jit(solution)/shard_map/ppermute | solution.py:383
  20.9 6.4 %collective-permute-start.8 = (bf16[64,1152]{1,0:T(8,128)(2,1)S(1)}, bf16[64,1152]{1,0:T(8,128)(2,1)S(1)}, u32[]{:S(2)}, u32[]{:S(2)}) collective-permute-start(bf16[64,1152]{1,0:T(8,128)(2,1)S(1)} %get-tuple-element.52), channel_id=1, source_target_pairs={{0,16},{8,24},{16,0},{24,8},{1,17},{9,25},{17,1},{25,9},{2,18},{10... | collective-permute-start | bytes 442376 | tf_op jit(solution)/shard_map/ppermute | solution.py:383
  22.4 7.3 %collective-permute-start.9 = (bf16[64,1152]{1,0:T(8,128)(2,1)S(1)}, bf16[64,1152]{1,0:T(8,128)(2,1)S(1)}, u32[]{:S(2)}, u32[]{:S(2)}) collective-permute-start(bf16[64,1152]{1,0:T(8,128)(2,1)S(1)} %get-tuple-element.53), channel_id=1, source_target_pairs={{0,24},{8,16},{16,8},{24,0},{1,25},{9,17},{17,9},{25,1},{2,26},{10... | collective-permute-start | bytes 442376 | tf_op jit(solution)/shard_map/ppermute | solution.py:383
  29.8 11.9 %collective-permute-start.14 = (bf16[64,1152]{1,0:T(8,128)(2,1)S(1)}, bf16[64,1152]{1,0:T(8,128)(2,1)S(1)}, u32[]{:S(2)}, u32[]{:S(2)}) collective-permute-start(bf16[64,1152]{1,0:T(8,128)(2,1)S(1)} %get-tuple-element.59.refs_0_), channel_id=1, source_target_pairs={{0,6},{1,7},{2,4},{3,5},{4,2},{5,3},{6,0},{7,1},{8,14},{9,15},{10,... | collective-permute-start | bytes 442376 | tf_op jit(solution)/shard_map/ppermute | solution.py:389
  33.5 11.9 %collective-permute-start.13 = (bf16[64,1152]{1,0:T(8,128)(2,1)S(1)}, bf16[64,1152]{1,0:T(8,128)(2,1)S(1)}, u32[]{:S(2)}, u32[]{:S(2)}) collective-permute-start(bf16[64,1152]{1,0:T(8,128)(2,1)S(1)} %get-tuple-element.59.refs_0_), channel_id=1, source_target_pairs={{0,4},{1,5},{2,6},{3,7},{4,0},{5,1},{6,2},{7,3},{8,12},{9,13},{10,... | collective-permute-start | bytes 442376 | tf_op jit(solution)/shard_map/ppermute | solution.py:389
  33.5 11.9 %collective-permute-start.12 = (bf16[64,1152]{1,0:T(8,128)(2,1)S(1)}, bf16[64,1152]{1,0:T(8,128)(2,1)S(1)}, u32[]{:S(2)}, u32[]{:S(2)}) collective-permute-start(bf16[64,1152]{1,0:T(8,128)(2,1)S(1)} %get-tuple-element.59.refs_0_), channel_id=1, source_target_pairs={{0,2},{1,3},{2,0},{3,1},{4,6},{5,7},{6,4},{7,5},{8,10},{9,11},{10,... | collective-permute-start | bytes 442376 | tf_op jit(solution)/shard_map/ppermute | solution.py:389
  34.3 6.7 %collective-permute-start.10 = (bf16[96,512]{1,0:T(8,128)(2,1)S(1)}, bf16[96,512]{1,0:T(8,128)(2,1)S(1)}, u32[]{:S(2)}, u32[]{:S(2)}) collective-permute-start(bf16[96,512]{1,0:T(8,128)(2,1)S(1)} %get-tuple-element.54), channel_id=1, source_target_pairs={{0,24},{8,0},{16,8},{24,16},{1,25},{9,1},{17,9},{25,17},{2,26},{10... | collective-permute-start | bytes 294920 | tf_op jit(solution)/shard_map/ppermute | solution.py:468
  36.0 5.0 %collective-permute-start.11 = (bf16[48,512]{1,0:T(8,128)(2,1)S(1)}, bf16[48,512]{1,0:T(8,128)(2,1)S(1)}, u32[]{:S(2)}, u32[]{:S(2)}) collective-permute-start(bf16[48,512]{1,0:T(8,128)(2,1)S(1)} %get-tuple-element.55), channel_id=1, source_target_pairs={{0,8},{8,16},{16,24},{24,0},{1,9},{9,17},{17,25},{25,1},{2,10},{10... | collective-permute-start | bytes 147464 | tf_op jit(solution)/shard_map/ppermute | solution.py:469
  45.4 1.6 %collective-permute-start.15 = (f32[64,1152]{1,0:T(8,128)S(1)}, f32[64,1152]{1,0:T(8,128)S(1)}, u32[]{:S(2)}, u32[]{:S(2)}) collective-permute-start(f32[64,1152]{1,0:T(8,128)S(1)} %shard_map.145.mine), channel_id=1, source_target_pairs={{0,1},{1,0},{2,3},{3,2},{4,5},{5,4},{6,7},{7,6},{8,9},{9,8},{10,11... | collective-permute-start | bytes 884744 | tf_op jit(solution)/shard_map/ppermute | solution.py:394
  (1 other events, 0.7 us)

commit v4 on v3

--- a/solution.py
+++ b/solution.py
@@ -55,9 +55,16 @@
     return jax.ShapeDtypeStruct(dims, kind)
 
 
-def pack_kernel(k, v, g, ahead, behind, edge, first, sems):
+def half_cols(side, width):
+    return pl.ds(pl.multiple_of(side * (width // 2), width // 2), width // 2)
+
+
+def pack_kernel(
+    k, v, g, w, lengths, offsets, ahead, behind, facts, w_half, edge, first, length, pair, sems,
+):
     rows = k.shape[0]
     feats = k.shape[1]
+    core = lax.rem(lax.axis_index("dp"), 2)
     pairs = [
         (k.at[pl.ds(rows - BACK, BACK)], ahead.at[pl.ds(0, BACK)]),
         (v.at[pl.ds(rows - BACK, BACK)], ahead.at[pl.ds(BACK, BACK)]),
@@ -65,12 +72,17 @@
         (v.at[pl.ds(0, AHEAD)], first.at[1]),
         (g.at[pl.ds(rows - EDGE, EDGE)], edge.at[0]),
         (g.at[pl.ds(0, EDGE)], edge.at[1]),
+        (w.at[:, half_cols(core, w.shape[1])], w_half),
+        (lengths, length),
+        (offsets, pair),
     ]
     copies = [pltpu.make_async_copy(a, b, sems.at[i]) for i, (a, b) in enumerate(pairs)]
     for copy in copies:
         copy.start()
     for copy in copies:
         copy.wait()
+    for row, value in enumerate((length[0], pair[0, 0], pair[0, 1])):
+        facts[row : row + 1] = jnp.full((1, facts.shape[1]), value, jnp.int32)
     behind[0 : 2 * BLK] = jnp.concatenate(
         [first[0].astype(F32)[:BLK], first[1].astype(F32)[:BLK]], 0
     ).astype(BF)
@@ -79,24 +91,28 @@
         out[out.shape[0] - EDGE :] = two.astype(BF)
 
 
-def packed(k, v, g):
-    feats = k.shape[1]
+def packed(*args):
+    feats, width = args[0].shape[1], args[2].shape[1]
     outs = (
         pltpu.VMEM((2 * BACK + EDGE, feats), BF),
         pltpu.VMEM((2 * BLK + EDGE, feats), BF),
+        pltpu.VMEM((8, 128), jnp.int32),
+        pltpu.VMEM((args[3].shape[0], width // 2), BF),
     )
     return pl.pallas_call(
         pack_kernel,
         out_shape=outs,
-        in_specs=[ANY] * 3,
-        out_specs=(VMEM,) * 2,
+        in_specs=[ANY] * 6,
+        out_specs=(VMEM,) * 4,
         scratch_shapes=[
-            pltpu.VMEM((2, EDGE, g.shape[1]), BF),
+            pltpu.VMEM((2, EDGE, width), BF),
             pltpu.VMEM((2, AHEAD, feats), BF),
-            pltpu.SemaphoreType.DMA((6,)),
+            pltpu.SMEM((1,), jnp.int32),
+            pltpu.SMEM((1, 2), jnp.int32),
+            pltpu.SemaphoreType.DMA((9,)),
         ],
         compiler_params=pltpu.CompilerParams(vmem_limit_bytes=40 * 1024 * 1024),
-    )(*[pltpu.with_memory_space_constraint(x, pltpu.HBM) for x in (k, v, g)])
+    )(*[x if x.ndim == 1 else pltpu.with_memory_space_constraint(x, pltpu.HBM) for x in args])
 
 
 def head_of(dims):
@@ -165,6 +181,15 @@
         gx[at : at + 8, cols] = masked(after[here], base + rows, length)
 
 
+def fill_half(gx, side, g, near, far, base, length):
+    rows = g.shape[0]
+    before = near[2 * BACK :].astype(F32)
+    after = far[2 * BLK :].astype(F32)
+    gx[0:8] = masked(jnp.where(side == 0, before[:8], before[8:]), base - 8, length)
+    gx[8 : 8 + rows] = masked(g[:, half_cols(side, g.shape[1])], base, length)
+    gx[8 + rows :] = masked(jnp.where(side == 0, after[:8], after[8:]), base + rows, length)
+
+
 def convolve(out, out_at, gx, gx_at, taps, start, count, length):
     width = out.shape[1]
     step = 128
@@ -178,32 +203,26 @@
         out[out_at : out_at + count, cols] = jnp.where(frame < length, total, 0.0).astype(BF)
 
 
-def inner_conv_kernel(g, taps, w, lengths, offsets, out, w_half, gx):
+def inner_conv_kernel(g, taps, facts, out, gx):
     rows = g.shape[0]
     base = lax.axis_index("cp") * rows
-    half = w.shape[0] // 2
-    core = lax.rem(lax.axis_index("dp"), 2)
-    w_half[...] = w[pl.ds(pl.multiple_of(core * half, half), half)]
     gx[0:8] = jnp.zeros((8, gx.shape[1]), F32)
     gx[8 + rows :] = jnp.zeros((8, gx.shape[1]), F32)
-    length = lengths[...]
+    length = facts[0:1, 0:1]
     gx[8 : 8 + rows] = masked(g[...], base, length)
     convolve(out, 0, gx, 8, taps, base, rows, length)
 
 
-def forward_kernel(
-    q, k, v, near, far, g, taps, inner, lengths, offsets,
-    stream_grad, send, keep, att_out, kx, vx, gx, att_t,
-):
+def forward_kernel(q, k, v, near, far, g, stream, facts, att_out, send, kx, vx, half_gx):
     rows, feats = q.shape
-    place = lax.axis_index("cp")
-    core = lax.rem(lax.axis_index("dp"), 2)
-    base = place * rows
-    length = lengths[...]
+    width = g.shape[1]
+    core = lax.rem(lax.axis_index("dp"), 2)
+    base = lax.axis_index("cp") * rows
+    length = facts[0:1, 0:1]
     fill_ext(kx, vx, k, v, near, far)
     for tile in range(rows // TILE):
         start = tile * TILE
-        allowed = allowed_in(tile, base, length, offsets[:, 0:1], offsets[:, 1:2])
+        allowed = allowed_in(tile, base, length, facts[1:2, 0:1], facts[2:3, 0:1])
         frame = base + start + lax.broadcasted_iota(jnp.int32, (TILE, FEATS), 0)
         for group in range(feats // FEATS):
             cols = slice(group * FEATS, (group + 1) * FEATS)
@@ -212,38 +231,53 @@
             product = tn(probs.astype(BF), vx[start : start + REACH, cols])
             attended = jnp.where(frame < length, unstacked(product), 0.0).astype(BF)
             att_out[start : start + TILE, cols] = attended
-    att_t[...] = att_out[...].astype(F32).T.astype(BF)
+            send[start : start + TILE, cols] = attended
+    send[rows : 2 * rows] = masked(stream[:, half_cols(1 - core, width)], base, length).astype(BF)
+    fill_half(half_gx, 1 - core, g, near, far, base, length)
+    send[2 * rows :] = half_gx[...].astype(BF)
+
+
+def weights_kernel(att, near, far, g, taps, inner, facts, stream_grad, send, keep, gx, att_t):
+    rows = att.shape[0]
+    parts, half, width = keep.shape
+    core = lax.rem(lax.axis_index("dp"), 2)
+    base = lax.axis_index("cp") * rows
+    length = facts[0:1, 0:1]
+    turned = att[...].astype(F32).T.astype(BF)
+    for part in range(parts):
+        for side in range(2):
+            at = jnp.where(core == side, parts * half, 0) + part * half
+            att_t[pl.ds(pl.multiple_of(at, half), half)] = turned[
+                (2 * part + side) * half : (2 * part + side + 1) * half
+            ]
     fill_rims(gx, 56, near, far, base, rows, length)
     gx[8:32] = masked(g[0:32].astype(F32)[:24], base, length)
     gx[32:56] = masked(g[rows - 32 :].astype(F32)[8:], base + rows - 24, length)
     stream_grad[EDGE : rows - EDGE] = inner[EDGE : rows - EDGE]
     convolve(stream_grad, 0, gx, 8, taps, base, EDGE, length)
     convolve(stream_grad, rows - EDGE, gx, 40, taps, base + rows - EDGE, EDGE, length)
-    half = send.shape[1]
-    for part in range(send.shape[0]):
-        there = pl.multiple_of(2 * half * part + half * (1 - core), half)
-        here = pl.multiple_of(2 * half * part + half * core, half)
-        send[part] = nn(att_t[pl.ds(there, half)], stream_grad[...]).astype(BF)
-        keep[part] = nn(att_t[pl.ds(here, half)], stream_grad[...])
-
-
-def folded(conv, half):
-    extra = 8 * conv.shape[1] // half
-    return jnp.concatenate(
-        [conv[:, at : at + extra] for at in range(0, conv.shape[1], extra)], 0
-    )
+    product = nn(att_t[...], stream_grad[...])
+    for part in range(parts):
+        send[part] = product[part * half : (part + 1) * half].astype(BF)
+        keep[part] = product[(parts + part) * half : (parts + part + 1) * half]
+
+
+def packed_grads(rows, conv):
+    cut = conv.shape[1] // 2
+    blocks = [rows[at : at + 16] for at in range(0, rows.shape[0], 16)]
+    return jnp.concatenate(blocks + [jnp.concatenate([conv[:, :cut], conv[:, cut:]], 0)], 1)
 
 
 def split_kernel(keep, got, conv, own, *pieces):
     place = lax.axis_index("cp")
-    half, width = keep.shape[1:]
-    tail = folded(conv[...], half).astype(BF)
-    own[:, :width] = keep[place] + got[place].astype(F32)
-    own[:, width:] = tail.astype(F32)
-    for by, piece in enumerate(pieces, 1):
+    parts, half, width = keep.shape
+    for by in range(parts):
         at = lax.bitwise_xor(place, by)
-        piece[:, :width] = (keep[at] + got[at].astype(F32)).astype(BF)
-        piece[:, width:] = tail
+        block = packed_grads(keep[at] + got[at].astype(F32), conv[...].astype(BF).astype(F32))
+        if by == 0:
+            own[...] = block
+        else:
+            pieces[by - 1][...] = block.astype(BF)
 
 
 def tree_sum(terms):
@@ -265,16 +299,18 @@
 
 
 def final_kernel(after, mine, theirs, weight_grad, conv_grad):
-    half = mine.shape[0]
     width = weight_grad.shape[1]
-    core = lax.rem(lax.axis_index("dp"), 2)
-    weight_grad[pl.ds(pl.multiple_of(core * half, half), half)] = mine[:, :width]
-    weight_grad[pl.ds(pl.multiple_of((1 - core) * half, half), half)] = theirs[:, :width]
-    extra = mine.shape[1] - width
-    total = mine[:, width:] + theirs[:, width:]
-    for at in range(0, half, 8):
-        cols = slice(at // 8 * extra, (at // 8 + 1) * extra)
-        conv_grad[:, cols] = total[at : at + KW]
+    half = weight_grad.shape[0] // 2
+    cut = width // 4
+    core = lax.rem(lax.axis_index("dp"), 2)
+    for side, grads in ((core, mine), (1 - core, theirs)):
+        for at in range(0, half, 16):
+            block = grads[:, at // 16 * width : (at // 16 + 1) * width]
+            weight_grad[pl.ds(pl.multiple_of(side * half + at, 16), 16)] = block
+        conv = grads[:, half // 16 * width :]
+        for part in range(2):
+            cols = pl.ds(pl.multiple_of((2 * side + part) * cut, cut), cut)
+            conv_grad[:, cols] = conv[8 * part : 8 * part + KW]
 
 
 def weight_stack_kernel(after, *refs):
@@ -282,51 +318,65 @@
         refs[-1][k] = ref[...]
 
 
-def conv_kernel(att, w, passed, stream, g, near, far, lengths, *refs):
-    got = refs[:-4]
-    conv, wx, gx, mixed = refs[-4:]
+def own_columns_kernel(after, w, *refs):
+    wx = refs[-1]
+    shard, width = w.shape
+    place = lax.axis_index("cp")
+    core = lax.rem(lax.axis_index("dp"), 2)
+    wx[pl.ds(pl.multiple_of(place * shard, shard), shard)] = w[:, half_cols(core, width)]
+    for by, ref in enumerate(refs[:-1], 1):
+        at = lax.bitwise_xor(place, by) * shard
+        wx[pl.ds(pl.multiple_of(at, shard), shard)] = ref[...]
+
+
+def conv_kernel(att, wx, stream, g, near, far, facts, other, conv, gx, mixed):
     rows, width = g.shape
+    core = lax.rem(lax.axis_index("dp"), 2)
+    base = lax.axis_index("cp") * rows
+    length = facts[0:1, 0:1]
+    cols = half_cols(core, width)
+    fill_half(gx.at[0], core, g, near, far, base, length)
+    gx[1] = other[2 * rows :].astype(F32)
+    mixed[0] = masked(stream[:, cols], base, length) + nn(att[...], wx[...])
+    mixed[1] = other[rows : 2 * rows].astype(F32) + nn(other[0:rows], wx[...])
+    conv[KW:] = jnp.zeros((8 - KW, conv.shape[1]), F32)
+    step = 128
+    for at in range(0, width // 2, step):
+        here = slice(at, at + step)
+        blocks = [mixed[0, :, here], mixed[1, :, here]]
+        for tap in range(KW):
+            first = 8 + HALF - tap
+            conv[tap : tap + 1, here] = jnp.sum(
+                blocks[0] * gx[0, first : first + rows, here]
+                + blocks[1] * gx[1, first : first + rows, here],
+                axis=0,
+                keepdims=True,
+            )
+
+
+def backward_kernel(
+    after, q, k, v, near, far, stream_grad, facts, w, passed, *refs
+):
+    got = refs[:-12]
+    query_g, key_g, value_g, back, onward, token, kx, vx, kg, vg, ag, wx = refs[-12:]
+    rows, feats = q.shape
     place = lax.axis_index("cp")
     core = lax.rem(lax.axis_index("dp"), 2)
-    base = place * rows
-    length = lengths[...]
-    shard = w.shape[0]
-    half = shard // 2
+    shard, width = w.shape
     wx[pl.ds(pl.multiple_of(place * shard, shard), shard)] = w[...]
     for by, ref in enumerate(got, 1):
-        at = lax.bitwise_xor(place, by) * shard
-        wx[pl.ds(pl.multiple_of(at + core * half, half), half)] = ref[...]
-        wx[pl.ds(pl.multiple_of(at + (1 - core) * half, half), half)] = passed[by - 1]
-    fill_rims(gx, 8 + rows, near, far, base, rows, length)
-    gx[8 : 8 + rows] = masked(g[...], base, length)
-    total = stream[...].astype(F32) + nn(att[...], wx[...])
-    mixed[...] = masked(total, base, length)
-    conv[KW:] = jnp.zeros((8 - KW, width), F32)
-    step = 128
-    for at in range(0, width, step):
-        cols = slice(at, at + step)
-        block = mixed[:, cols]
-        for tap in range(KW):
-            top = 8 + HALF - tap
-            conv[tap : tap + 1, cols] = jnp.sum(
-                block * gx[top : top + rows, cols], axis=0, keepdims=True
-            )
-
-
-def backward_kernel(
-    after, q, k, v, near, far, stream_grad, wx, lengths, offsets,
-    query_g, key_g, value_g, back, onward, token, kx, vx, kg, vg, ag,
-):
-    rows, feats = q.shape
+        at = pl.ds(pl.multiple_of(lax.bitwise_xor(place, by) * shard, shard), shard)
+        wx[at, half_cols(core, width)] = ref[...]
+        wx[at, half_cols(1 - core, width)] = passed[by - 1]
     base = lax.axis_index("cp") * rows
-    length = lengths[...]
+    length = facts[0:1, 0:1]
     ag[...] = nt(stream_grad[...], wx[...]).astype(BF)
     fill_ext(kx, vx, k, v, near, far)
     kg[...] = jnp.zeros_like(kg)
     vg[...] = jnp.zeros_like(vg)
     for tile in range(rows // TILE):
         start = tile * TILE
-        allowed = allowed_in(tile, base, length, offsets[:, 0:1], offsets[:, 1:2])
+        allowed = allowed_in(tile, base, length, facts[1:2, 0:1], facts[2:3, 0:1])
         span = slice(start, start + REACH)
         for group in range(feats // FEATS):
             cols = slice(group * FEATS, (group + 1) * FEATS)
@@ -373,75 +423,94 @@
     q, k, v, g, stream = queries[0], key_rows[0], value_rows[0], out_grad[0], stream_in[0]
     shard = out_weight.shape[0]
     half = shard // 2
-    lengths = lengths.reshape(1, 1)
     ext = rows + BACK + AHEAD
     upward = [(i, (i + 1) % cps) for i in range(cps)]
     downward = [(i, (i - 1) % cps) for i in range(cps)]
 
     def over_cp(arrays):
-        return [
-            lax.ppermute(array, "cp", [(i, i ^ by) for i in range(cps)])
-            for by, array in enumerate(arrays, 1)
+        got = [
+            lax.ppermute(arrays[by - 1], "cp", [(i, i ^ by) for i in range(cps)])
+            for by in range(cps - 1, 0, -1)
         ]
+        return got[::-1]
 
     def over_z(array):
-        return [
+        got = [
             lax.ppermute(array, "dp", [(i, i ^ (2 * by)) for i in range(dps)])
-            for by in range(1, floors)
+            for by in range(floors - 1, 0, -1)
         ]
+        return got[::-1]
 
     def over_core(array):
         return lax.ppermute(array, "dp", [(i, i ^ 1) for i in range(dps)])
 
-    ahead, behind = packed(k, v, g)
+    ahead, behind, facts, w_half = packed(k, v, g, out_weight, lengths, offsets)
     near = lax.ppermute(ahead, "cp", upward)
     far = lax.ppermute(behind, "cp", downward)
-    inner, w_half = call(
+    inner = call(
         inner_conv_kernel,
-        (shape((rows, width), BF), shape((half, width), BF)),
-        [VMEM] * 5,
-        (g, conv_weight, out_weight, lengths, offsets),
+        shape((rows, width), BF),
+        [VMEM] * 3,
+        (g, conv_weight, facts),
         [pltpu.VMEM((rows + 16, width), F32)],
     )
     w_got = over_cp([w_half] * (cps - 1))
     ext_scratch = [pltpu.VMEM((ext, feats), BF)] * 2
-    stream_grad, send, keep, att = call(
+    att, conv_send = call(
         forward_kernel,
+        (shape((rows, feats), BF), shape((3 * rows + 16, width // 2), BF)),
+        [VMEM] * 8,
+        (q, k, v, near, far, g, stream, facts),
+        ext_scratch + [pltpu.VMEM((rows + 16, width // 2), F32)],
+        flops=2**32,
+    )
+    conv_got = over_core(conv_send)
+    stream_grad, send, keep = call(
+        weights_kernel,
         (
             shape((rows, width), BF),
             shape((cps, half, width), BF),
             shape((cps, half, width), F32),
-            shape((rows, feats), BF),
         ),
-        [VMEM] * 10,
-        (q, k, v, near, far, g, conv_weight, inner, lengths, offsets),
-        ext_scratch + [pltpu.VMEM((64, width), F32), pltpu.VMEM((feats, rows), BF)],
+        [VMEM] * 7,
+        (att, near, far, g, conv_weight, inner, facts),
+        [pltpu.VMEM((64, width), F32), pltpu.VMEM((feats, rows), BF)],
     )
     core_got = over_core(send)
+    w_cols = call(
+        own_columns_kernel,
+        shape((feats, width // 2), BF),
+        [ANY] + [VMEM] * cps,
+        (send, out_weight, *w_got),
+        flops=2**34,
+    )
+    conv = call(
+        conv_kernel,
+        shape((8, width // 2), F32),
+        [VMEM] * 8,
+        (att, w_cols, stream, g, near, far, facts, conv_got),
+        [
+            pltpu.VMEM((2, rows + 16, width // 2), F32),
+            pltpu.VMEM((2, rows, width // 2), F32),
+        ],
+    )
+    wide = half // 16 * width + width // 4
+    own, *pieces = call(
+        split_kernel,
+        (shape((16, wide), F32),) + (shape((16, wide), BF),) * (cps - 1),
+        [VMEM] * 3,
+        (keep, core_got, conv),
+    )
+    cp_got = over_cp(pieces)
+    token = shape((8, 128), F32)
     passed = over_core(
         call(
             weight_stack_kernel,
-            shape((cps - 1, half, width), BF),
+            shape((cps - 1, shard, width // 2), BF),
             [ANY] + [VMEM] * (cps - 1),
-            (att, *w_got),
+            (own, *w_got),
         )
     )
-    conv, wx = call(
-        conv_kernel,
-        (shape((8, width), F32), shape((feats, width), BF)),
-        [VMEM] * (7 + cps),
-        (att, out_weight, passed, stream, g, near, far, lengths, *w_got),
-        [pltpu.VMEM((rows + 16, width), F32), pltpu.VMEM((rows, width), F32)],
-    )
-    wide = width + 8 * width // half
-    own, *pieces = call(
-        split_kernel,
-        (shape((half, wide), F32),) + (shape((half, wide), BF),) * (cps - 1),
-        [VMEM] * 3,
-        (keep, core_got, conv),
-    )
-    cp_got = over_cp(pieces)
-    token = shape((8, 128), F32)
     query_g, key_g, value_g, back, onward, bwd_done = call(
         backward_kernel,
         (
@@ -452,16 +521,16 @@
             shape((2 * BLK, feats), BF),
             token,
         ),
-        [ANY] + [VMEM] * 9,
-        (own, q, k, v, near, far, stream_grad, wx, lengths, offsets),
+        [ANY] + [VMEM] * (8 + cps),
+        (own, q, k, v, near, far, stream_grad, facts, out_weight, passed, *w_got),
         ext_scratch
         + [pltpu.VMEM((ext, feats), F32)] * 2
-        + [pltpu.VMEM((rows, feats), BF)],
+        + [pltpu.VMEM((rows, feats), BF), pltpu.VMEM((feats, width), BF)],
         moved=10 * 2**20,
     )
     part, back, onward = call(
         cp_sum_kernel,
-        (shape((half, wide), BF), shape(back.shape, BF), shape(onward.shape, BF)),
+        (shape((16, wide), BF), shape(back.shape, BF), shape(onward.shape, BF)),
         [VMEM] * (cps + 3),
         (bwd_done, back, onward, own, *cp_got),
     )
@@ -474,16 +543,21 @@
         (key_g, value_g, last, first),
     )
     if floors != 4:
-        at = (lax.axis_index("dp") % 2) * half
-        whole = lax.dynamic_update_slice(
-            jnp.zeros((shard, width), F32), part[:, :width].astype(F32), (at, 0)
+        core = lax.axis_index("dp") % 2
+        blocks = [part[:, at * width : (at + 1) * width] for at in range(half // 16)]
+        summed = jnp.concatenate(blocks, 0).astype(F32)
+        weights = lax.dynamic_update_slice(
+            jnp.zeros((shard, width), F32), summed, (core * half, 0)
         )
-        weight_grad = lax.psum(whole, "dp")
-        conv_grad = lax.psum(conv, ("cp", "dp"))[:KW]
+        taps = lax.dynamic_update_slice(
+            jnp.zeros((8, width), F32), conv, (0, core * (width // 2))
+        )
+        weight_grad = lax.psum(weights, "dp")
+        conv_grad = lax.psum(taps, ("cp", "dp"))[:KW]
     else:
         mine = call(
             z_sum_kernel,
-            shape((half, wide), F32),
+            shape((16, wide), F32),
             [VMEM] * (floors + 1),
             (join_done, part, *over_z(part)),
         )

time: 48.1 us -> 45.3 us (0.942)
  waiting for transfers between devices: 16.9 us -> 14.3 us
  local copies, waits for them, and re-layouts: 0.65 us -> 0.04 us
  starting transfers between devices: 17.7 us -> 18.2 us
    ppermute x3 -> x4, waiting for transfers between devices: 3.28 us -> 1.55 us  [over_core(): return lax.ppermute(array, 'dp', [(i, i ^ 1) for i in range(dps)])]
    ppermute x1, waiting for transfers between devices: 0.01 us -> 1.35 us  [body(): far = lax.ppermute(behind, 'cp', downward)]
    ppermute x6, waiting for transfers between devices: 5.34 us -> 4.37 us  [over_cp(): lax.ppermute(arrays[by - 1], 'cp', [(i, i ^ by) for i in range(cps)])]
    ppermute x3, waiting for transfers between devices: 3.63 us -> 2.9 us  [over_z(): lax.ppermute(array, 'dp', [(i, i ^ 2 * by) for i in range(dps)])]
    unnamed x18 -> x16, local copies, waits for them, and re-layouts: 0.65 us -> 0.04 us
    ppermute x3 -> x4, starting transfers between devices: 0.14 us -> 0.7 us  [over_core(): return lax.ppermute(array, 'dp', [(i, i ^ 1) for i in range(dps)])]
    ppermute x1, waiting for transfers between devices: 4.66 us -> 4.14 us  [body(): first = lax.ppermute(onward, 'cp', upward)]
    ppermute x1, starting transfers between devices: 1.7 us -> 1.17 us  [body(): last = lax.ppermute(back, 'cp', downward)]
  transfers between devices with their start and end apart: 16 -> 17, of which waited for: 10 -> 7; matrix products, arithmetic and copies ran while one was open for 0% -> 0% of each run, Pallas kernels for 19% -> 19%
where the time goes in v4:
time: 45.3 us; the launch traced here: 45.1 us
  starting transfers between devices  18.2 us (40%)
  waiting for transfers between devices  14.3 us (32%)
  Pallas kernels  11.1 us (25%)
  between operations  1.47 us (3%)
    pallas_call x12, Pallas kernels, call(): pl.pallas_call(kernel, out_shape=outs, in_specs=ins, out_specs=jax.tree.m...  9.91 us
    ppermute x6, starting transfers between devices, over_cp(): lax.ppermute(arrays[by - 1], 'cp', [(i, i ^ by) for i in range(cps)])  7.04 us
    ppermute x3, starting transfers between devices, over_z(): lax.ppermute(array, 'dp', [(i, i ^ 2 * by) for i in range(dps)])  4.45 us
    ppermute x6, waiting for transfers between devices, over_cp(): lax.ppermute(arrays[by - 1], 'cp', [(i, i ^ by) for i in range(cps)])  4.37 us
    ppermute x1, waiting for transfers between devices, body(): first = lax.ppermute(onward, 'cp', upward)  4.14 us
    ppermute x1, starting transfers between devices, body(): near = lax.ppermute(ahead, 'cp', upward)  2.99 us
    ppermute x3, waiting for transfers between devices, over_z(): lax.ppermute(array, 'dp', [(i, i ^ 2 * by) for i in range(dps)])  2.9 us
    ppermute x4, waiting for transfers between devices, over_core(): return lax.ppermute(array, 'dp', [(i, i ^ 1) for i in range(dps)])  1.55 us
  transfers between devices with their start and end apart: 17, of which 7 were waited for; matrix products, arithmetic and copies ran while one was open for 0% of the time, Pallas kernels for 19%

profile of v4, /device:TPU:0, one launch (start us, length us, event | category | flops | bytes accessed | tf_op | source)
XLA Modules:
  0.0 45.1 jit_solution(16006721476695604079)
XLA Ops:
  1.3 1.2 %shard_map.136 = (bf16[112,512]{1,0:T(8,128)(2,1)S(1)}, bf16[64,512]{1,0:T(8,128)(2,1)S(1)}, s32[8,128]{1,0:T(8,128)S(1)}, bf16[128,512]{1,0:T(8,128)(2,1)S(1)}) custom-call(bf16[192,512]{1,0:T(8,128)(2,1)} %bitcast.14, bf16[192,512]{1,0:T(8,128)(2,1)} %bitcast.17, bf16[192,1024]{1,0:T(8,128)(2,1)} %bitcast.9, bf16[128,1024]{1,0:T(8,128)(2,1)} %w.5, ...), custom_call_target="tpu_custom_call" | custom-call | tf_op jit(solution)/shard_map/pallas_call | solution.py:102
  2.5 3.0 %collective-permute-start = (bf16[112,512]{1,0:T(8,128)(2,1)S(1)}, bf16[112,512]{1,0:T(8,128)(2,1)S(1)}, u32[]{:S(2)}, u32[]{:S(2)}) collective-permute-start(bf16[112,512]{1,0:T(8,128)(2,1)S(1)} %get-tuple-element.33), channel_id=1, source_target_pairs={{0,8},{8,16},{16,24},{24,0},{1,9},{9,17},{17,25},{25,1},{2,10},{10... | collective-permute-start | bytes 344072 | tf_op jit(solution)/shard_map/ppermute | solution.py:448
  5.5 1.0 %collective-permute-start.1 = (bf16[64,512]{1,0:T(8,128)(2,1)S(1)}, bf16[64,512]{1,0:T(8,128)(2,1)S(1)}, u32[]{:S(2)}, u32[]{:S(2)}) collective-permute-start(bf16[64,512]{1,0:T(8,128)(2,1)S(1)} %get-tuple-element.34), channel_id=1, source_target_pairs={{0,24},{8,0},{16,8},{24,16},{1,25},{9,1},{17,9},{25,17},{2,26},{10... | collective-permute-start | bytes 196616 | tf_op jit(solution)/shard_map/ppermute | solution.py:449
  6.5 2.0 %collective-permute-start.5 = (bf16[128,512]{1,0:T(8,128)(2,1)S(1)}, bf16[128,512]{1,0:T(8,128)(2,1)S(1)}, u32[]{:S(2)}, u32[]{:S(2)}) collective-permute-start(bf16[128,512]{1,0:T(8,128)(2,1)S(1)} %get-tuple-element.39), channel_id=1, source_target_pairs={{0,24},{8,16},{16,8},{24,0},{1,25},{9,17},{17,9},{25,1},{2,26},{10... | collective-permute-start | bytes 393224 | tf_op jit(solution)/shard_map/ppermute | solution.py:432
  9.0 1.0 %collective-permute-start.3 = (bf16[128,512]{1,0:T(8,128)(2,1)S(1)}, bf16[128,512]{1,0:T(8,128)(2,1)S(1)}, u32[]{:S(2)}, u32[]{:S(2)}) collective-permute-start(bf16[128,512]{1,0:T(8,128)(2,1)S(1)} %get-tuple-element.39), channel_id=1, source_target_pairs={{0,8},{8,0},{16,24},{24,16},{1,9},{9,1},{17,25},{25,17},{2,10},{10... | collective-permute-start | bytes 393224 | tf_op jit(solution)/shard_map/ppermute | solution.py:432
  10.0 1.0 %shard_map.138.inner = bf16[192,1024]{1,0:T(8,128)(2,1)S(1)} custom-call(bf16[192,1024]{1,0:T(8,128)(2,1)S(1)} %bitcast.10, f32[7,1024]{1,0:T(8,128)S(1)} %copy-done.7, s32[8,128]{1,0:T(8,128)S(1)} %get-tuple-element.35.facts), custom_call_target="tpu_custom_call" | custom-call | tf_op jit(solution)/shard_map/pallas_call | solution.py:43
  11.0 1.3 %collective-permute-done.1.far = bf16[64,512]{1,0:T(8,128)(2,1)S(1)} collective-permute-done((bf16[64,512]{1,0:T(8,128)(2,1)S(1)}, bf16[64,512]{1,0:T(8,128)(2,1)S(1)}, u32[]{:S(2)}, u32[]{:S(2)}) %collective-permute-start.1) | collective-permute-done | bytes 65568 | tf_op jit(solution)/shard_map/ppermute | solution.py:449
  12.4 1.5 %shard_map.137 = (bf16[192,512]{1,0:T(8,128)(2,1)S(1)}, bf16[592,512]{1,0:T(8,128)(2,1)S(1)}) custom-call(bf16[192,512]{1,0:T(8,128)(2,1)S(1)} %bitcast.23, bf16[192,512]{1,0:T(8,128)(2,1)S(1)} %bitcast.15, bf16[192,512]{1,0:T(8,128)(2,1)S(1)} %bitcast.18, bf16[112,512]{1,0:T(8,128)(2,1)S(1)} %collective-permute-done.near, ...), custom_call_target="tpu_custom_call" | custom-call | flops 4294967296 | tf_op jit(solution)/shard_map/pallas_call | solution.py:43
  14.0 1.1 %shard_map.139 = (bf16[192,1024]{1,0:T(8,128)(2,1)}, bf16[4,64,1024]{2,1,0:T(8,128)(2,1)S(1)}, f32[4,64,1024]{2,1,0:T(8,128)S(1)}) custom-call(bf16[192,512]{1,0:T(8,128)(2,1)S(1)} %get-tuple-element.36.att, bf16[112,512]{1,0:T(8,128)(2,1)S(1)} %collective-permute-done.near, bf16[64,512]{1,0:T(8,128)(2,1)S(1)} %collective-permute-done.1.far, ...), custom_call_target="tpu_custom_call" | custom-call | tf_op jit(solution)/shard_map/pallas_call | solution.py:43
  15.9 1.0 %collective-permute-done.3.refs_0_ = bf16[128,512]{1,0:T(8,128)(2,1)S(1)} collective-permute-done((bf16[128,512]{1,0:T(8,128)(2,1)S(1)}, bf16[128,512]{1,0:T(8,128)(2,1)S(1)}, u32[]{:S(2)}, u32[]{:S(2)}) %collective-permute-start.3) | collective-permute-done | bytes 131104 | tf_op jit(solution)/shard_map/ppermute | solution.py:432
  16.9 1.2 %shard_map.141.conv = f32[8,512]{1,0:T(8,128)S(1)} custom-call(bf16[192,512]{1,0:T(8,128)(2,1)S(1)} %get-tuple-element.36.att, bf16[512,512]{1,0:T(8,128)(2,1)S(1)} %shard_map.140.wx, bf16[192,1024]{1,0:T(8,128)(2,1)S(1)} %bitcast.21, bf16[192,1024]{1,0:T(8,128)(2,1)S(1)} %bitcast.13, bf16[112,512]{1,0:T(8,128)(2,1)S(1)} %collective-permute-done.near, ...), custom_call_target="tpu_custom_call" | custom-call | tf_op jit(solution)/shard_map/pallas_call | solution.py:43
  18.4 1.1 %collective-permute-start.8 = (bf16[16,4352]{1,0:T(8,128)(2,1)S(1)}, bf16[16,4352]{1,0:T(8,128)(2,1)S(1)}, u32[]{:S(2)}, u32[]{:S(2)}) collective-permute-start(bf16[16,4352]{1,0:T(8,128)(2,1)S(1)} %get-tuple-element.49), channel_id=1, source_target_pairs={{0,8},{8,0},{16,24},{24,16},{1,9},{9,1},{17,25},{25,17},{2,10},{10... | collective-permute-start | bytes 417800 | tf_op jit(solution)/shard_map/ppermute | solution.py:432
  19.5 1.1 %collective-permute-start.9 = (bf16[16,4352]{1,0:T(8,128)(2,1)S(1)}, bf16[16,4352]{1,0:T(8,128)(2,1)S(1)}, u32[]{:S(2)}, u32[]{:S(2)}) collective-permute-start(bf16[16,4352]{1,0:T(8,128)(2,1)S(1)} %get-tuple-element.50), channel_id=1, source_target_pairs={{0,16},{8,24},{16,0},{24,8},{1,17},{9,25},{17,1},{25,9},{2,18},{10... | collective-permute-start | bytes 417800 | tf_op jit(solution)/shard_map/ppermute | solution.py:432
  20.6 1.4 %collective-permute-start.10 = (bf16[16,4352]{1,0:T(8,128)(2,1)S(1)}, bf16[16,4352]{1,0:T(8,128)(2,1)S(1)}, u32[]{:S(2)}, u32[]{:S(2)}) collective-permute-start(bf16[16,4352]{1,0:T(8,128)(2,1)S(1)} %get-tuple-element.51), channel_id=1, source_target_pairs={{0,24},{8,16},{16,8},{24,0},{1,25},{9,17},{17,9},{25,1},{2,26},{10... | collective-permute-start | bytes 417800 | tf_op jit(solution)/shard_map/ppermute | solution.py:432
  22.0 3.2 %shard_map.144 = (bf16[192,512]{1,0:T(8,128)(2,1)}, f32[192,512]{1,0:T(8,128)S(1)}, f32[192,512]{1,0:T(8,128)S(1)}, bf16[96,512]{1,0:T(8,128)(2,1)S(1)}, bf16[48...) custom-call(f32[16,4352]{1,0:T(8,128)S(1)} %get-tuple-element.41.after.refs_0_, bf16[192,512]{1,0:T(8,128)(2,1)S(1)} %bitcast.24, ...), custom_call_target="tpu_custom_call" | custom-call | bytes 10485760 | tf_op jit(solution)/shard_map/pallas_call | solution.py:43
  25.2 3.1 %collective-permute-done.9.refs_2_ = bf16[16,4352]{1,0:T(8,128)(2,1)S(1)} collective-permute-done((bf16[16,4352]{1,0:T(8,128)(2,1)S(1)}, bf16[16,4352]{1,0:T(8,128)(2,1)S(1)}, u32[]{:S(2)}, u32[]{:S(2)}) %collective-permute-start.9) | collective-permute-done | bytes 139296 | tf_op jit(solution)/shard_map/ppermute | solution.py:432
  28.3 3.7 %collective-permute-start.15 = (bf16[16,4352]{1,0:T(8,128)(2,1)S(1)}, bf16[16,4352]{1,0:T(8,128)(2,1)S(1)}, u32[]{:S(2)}, u32[]{:S(2)}) collective-permute-start(bf16[16,4352]{1,0:T(8,128)(2,1)S(1)} %get-tuple-element.57.refs_0_), channel_id=1, source_target_pairs={{0,6},{1,7},{2,4},{3,5},{4,2},{5,3},{6,0},{7,1},{8,14},{9,15},{10,... | collective-permute-start | bytes 417800 | tf_op jit(solution)/shard_map/ppermute | solution.py:439
  32.7 1.2 %collective-permute-start.11 = (bf16[96,512]{1,0:T(8,128)(2,1)S(1)}, bf16[96,512]{1,0:T(8,128)(2,1)S(1)}, u32[]{:S(2)}, u32[]{:S(2)}) collective-permute-start(bf16[96,512]{1,0:T(8,128)(2,1)S(1)} %get-tuple-element.52), channel_id=1, source_target_pairs={{0,24},{8,0},{16,8},{24,16},{1,25},{9,1},{17,9},{25,17},{2,26},{10... | collective-permute-start | bytes 294920 | tf_op jit(solution)/shard_map/ppermute | solution.py:537
  33.9 0.9 %collective-permute-start.12 = (bf16[48,512]{1,0:T(8,128)(2,1)S(1)}, bf16[48,512]{1,0:T(8,128)(2,1)S(1)}, u32[]{:S(2)}, u32[]{:S(2)}) collective-permute-start(bf16[48,512]{1,0:T(8,128)(2,1)S(1)} %get-tuple-element.53), channel_id=1, source_target_pairs={{0,8},{8,16},{16,24},{24,0},{1,9},{9,17},{17,25},{25,1},{2,10},{10... | collective-permute-start | bytes 147464 | tf_op jit(solution)/shard_map/ppermute | solution.py:538
  34.8 4.1 %collective-permute-done.12.first = bf16[48,512]{1,0:T(8,128)(2,1)S(1)} collective-permute-done((bf16[48,512]{1,0:T(8,128)(2,1)S(1)}, bf16[48,512]{1,0:T(8,128)(2,1)S(1)}, u32[]{:S(2)}, u32[]{:S(2)}) %collective-permute-start.12) | collective-permute-done | bytes 49184 | tf_op jit(solution)/shard_map/ppermute | solution.py:538
  38.9 0.8 %shard_map.146 = (bf16[192,512]{1,0:T(8,128)(2,1)}, bf16[192,512]{1,0:T(8,128)(2,1)}, f32[8,128]{1,0:T(8,128)S(1)}) custom-call(f32[192,512]{1,0:T(8,128)S(1)} %get-tuple-element.44.key_g, f32[192,512]{1,0:T(8,128)S(1)} %get-tuple-element.45.value_g, bf16[96,512]{1,0:T(8,128)(2,1)S(1)} %collective-permute-done.11.last, ...), custom_call_target="tpu_custom_call" | custom-call | tf_op jit(solution)/shard_map/pallas_call | solution.py:43
  39.7 2.9 %collective-permute-done.14.refs_2_ = bf16[16,4352]{1,0:T(8,128)(2,1)S(1)} collective-permute-done((bf16[16,4352]{1,0:T(8,128)(2,1)S(1)}, bf16[16,4352]{1,0:T(8,128)(2,1)S(1)}, u32[]{:S(2)}, u32[]{:S(2)}) %collective-permute-start.14) | collective-permute-done | bytes 139296 | tf_op jit(solution)/shard_map/ppermute | solution.py:439
  42.8 1.5 %collective-permute-done.16.theirs = f32[16,4352]{1,0:T(8,128)S(1)} collective-permute-done((f32[16,4352]{1,0:T(8,128)S(1)}, f32[16,4352]{1,0:T(8,128)S(1)}, u32[]{:S(2)}, u32[]{:S(2)}) %collective-permute-start.16) | collective-permute-done | bytes 278560 | tf_op jit(solution)/shard_map/ppermute | solution.py:445
  44.3 0.8 %shard_map.148 = (f32[128,1024]{1,0:T(8,128)}, f32[7,1024]{1,0:T(8,128)}) custom-call(f32[8,128]{1,0:T(8,128)S(1)} %get-tuple-element.56.after, f32[16,4352]{1,0:T(8,128)S(1)} %shard_map.147.mine, f32[16,4352]{1,0:T(8,128)S(1)} %collective-permute-done.16.theirs), custom_call_target="tpu_custom_call" | custom-call | tf_op jit(solution)/shard_map/pallas_call | solution.py:43
  (39 shorter events, 2.7 us)
Async XLA Ops:
  1.3 8.7 %copy-start = (bf16[1,192,1024]{2,1,0:T(8,128)(2,1)S(1)}, bf16[1,192,1024]{2,1,0:T(8,128)(2,1)}, u32[]{:S(2)}) copy-start(bf16[1,192,1024]{2,1,0:T(8,128)(2,1)} %param.13) | copy-start | bytes 1179652
  1.3 8.7 %copy-start.7 = (f32[7,1024]{1,0:T(8,128)S(1)}, f32[7,1024]{1,0:T(8,128)}, u32[]{:S(2)}) copy-start(f32[7,1024]{1,0:T(8,128)} %taps.3) | copy-start | bytes 86020
  1.3 11.1 %copy-start.6 = (bf16[1,192,512]{2,1,0:T(8,128)(2,1)S(1)}, bf16[1,192,512]{2,1,0:T(8,128)(2,1)}, u32[]{:S(2)}) copy-start(bf16[1,192,512]{2,1,0:T(8,128)(2,1)} %param.9) | copy-start | bytes 589828
  2.5 9.9 %collective-permute-start = (bf16[112,512]{1,0:T(8,128)(2,1)S(1)}, bf16[112,512]{1,0:T(8,128)(2,1)S(1)}, u32[]{:S(2)}, u32[]{:S(2)}) collective-permute-start(bf16[112,512]{1,0:T(8,128)(2,1)S(1)} %get-tuple-element.33), channel_id=1, source_target_pairs={{0,8},{8,16},{16,24},{24,0},{1,9},{9,17},{17,25},{25,1},{2,10},{10... | collective-permute-start | bytes 344072 | tf_op jit(solution)/shard_map/ppermute | solution.py:448
  5.5 6.9 %collective-permute-start.1 = (bf16[64,512]{1,0:T(8,128)(2,1)S(1)}, bf16[64,512]{1,0:T(8,128)(2,1)S(1)}, u32[]{:S(2)}, u32[]{:S(2)}) collective-permute-start(bf16[64,512]{1,0:T(8,128)(2,1)S(1)} %get-tuple-element.34), channel_id=1, source_target_pairs={{0,24},{8,0},{16,8},{24,16},{1,25},{9,1},{17,9},{25,17},{2,26},{10... | collective-permute-start | bytes 196616 | tf_op jit(solution)/shard_map/ppermute | solution.py:449
  6.5 9.0 %collective-permute-start.5 = (bf16[128,512]{1,0:T(8,128)(2,1)S(1)}, bf16[128,512]{1,0:T(8,128)(2,1)S(1)}, u32[]{:S(2)}, u32[]{:S(2)}) collective-permute-start(bf16[128,512]{1,0:T(8,128)(2,1)S(1)} %get-tuple-element.39), channel_id=1, source_target_pairs={{0,24},{8,16},{16,8},{24,0},{1,25},{9,17},{17,9},{25,1},{2,26},{10... | collective-permute-start | bytes 393224 | tf_op jit(solution)/shard_map/ppermute | solution.py:432
  8.5 7.4 %collective-permute-start.4 = (bf16[128,512]{1,0:T(8,128)(2,1)S(1)}, bf16[128,512]{1,0:T(8,128)(2,1)S(1)}, u32[]{:S(2)}, u32[]{:S(2)}) collective-permute-start(bf16[128,512]{1,0:T(8,128)(2,1)S(1)} %get-tuple-element.39), channel_id=1, source_target_pairs={{0,16},{8,24},{16,0},{24,8},{1,17},{9,25},{17,1},{25,9},{2,18},{10... | collective-permute-start | bytes 393224 | tf_op jit(solution)/shard_map/ppermute | solution.py:432
  9.0 7.9 %collective-permute-start.3 = (bf16[128,512]{1,0:T(8,128)(2,1)S(1)}, bf16[128,512]{1,0:T(8,128)(2,1)S(1)}, u32[]{:S(2)}, u32[]{:S(2)}) collective-permute-start(bf16[128,512]{1,0:T(8,128)(2,1)S(1)} %get-tuple-element.39), channel_id=1, source_target_pairs={{0,8},{8,0},{16,24},{24,16},{1,9},{9,1},{17,25},{25,17},{2,10},{10... | collective-permute-start | bytes 393224 | tf_op jit(solution)/shard_map/ppermute | solution.py:432
  10.0 2.4 %copy-start.3 = (bf16[1,192,512]{2,1,0:T(8,128)(2,1)S(1)}, bf16[1,192,512]{2,1,0:T(8,128)(2,1)}, u32[]{:S(2)}) copy-start(bf16[1,192,512]{2,1,0:T(8,128)(2,1)} %param.11) | copy-start | bytes 589828
  10.0 2.4 %copy-start.4 = (bf16[1,192,1024]{2,1,0:T(8,128)(2,1)S(1)}, bf16[1,192,1024]{2,1,0:T(8,128)(2,1)}, u32[]{:S(2)}) copy-start(bf16[1,192,1024]{2,1,0:T(8,128)(2,1)} %param.12) | copy-start | bytes 1179652
  13.9 3.0 %collective-permute-start.6 = (bf16[592,512]{1,0:T(8,128)(2,1)S(1)}, bf16[592,512]{1,0:T(8,128)(2,1)S(1)}, u32[]{:S(2)}, u32[]{:S(2)}) collective-permute-start(bf16[592,512]{1,0:T(8,128)(2,1)S(1)} %get-tuple-element.40), channel_id=1, source_target_pairs={{0,1},{1,0},{2,3},{3,2},{4,5},{5,4},{6,7},{7,6},{8,9},{9,8},{10,11... | collective-permute-start | bytes 1818632 | tf_op jit(solution)/shard_map/ppermute | solution.py:445
  14.0 2.9 %copy-start.1 = (bf16[128,1024]{1,0:T(8,128)(2,1)S(1)}, bf16[128,1024]{1,0:T(8,128)(2,1)}, u32[]{:S(2)}) copy-start(bf16[128,1024]{1,0:T(8,128)(2,1)} %w.5) | copy-start | bytes 786436
  15.1 3.1 %collective-permute-start.2 = (bf16[4,64,1024]{2,1,0:T(8,128)(2,1)S(1)}, bf16[4,64,1024]{2,1,0:T(8,128)(2,1)S(1)}, u32[]{:S(2)}, u32[]{:S(2)}) collective-permute-start(bf16[4,64,1024]{2,1,0:T(8,128)(2,1)S(1)} %get-tuple-element.38.after), channel_id=1, source_target_pairs={{0,1},{1,0},{2,3},{3,2},{4,5},{5,4},{6,7},{7,6},{8,9},{9,8},{10,11... | collective-permute-start | bytes 1572872 | tf_op jit(solution)/shard_map/ppermute | solution.py:445
  18.3 3.7 %copy-start.5 = (bf16[192,1024]{1,0:T(8,128)(2,1)S(1)}, bf16[192,1024]{1,0:T(8,128)(2,1)}, u32[]{:S(2)}) copy-start(bf16[192,1024]{1,0:T(8,128)(2,1)} %get-tuple-element.42.stream_grad) | copy-start | bytes 1179652
  18.3 3.6 %collective-permute-start.7 = (bf16[3,128,512]{2,1,0:T(8,128)(2,1)S(1)}, bf16[3,128,512]{2,1,0:T(8,128)(2,1)S(1)}, u32[]{:S(2)}, u32[]{:S(2)}) collective-permute-start(bf16[3,128,512]{2,1,0:T(8,128)(2,1)S(1)} %shard_map.143), channel_id=1, source_target_pairs={{0,1},{1,0},{2,3},{3,2},{4,5},{5,4},{6,7},{7,6},{8,9},{9,8},{10,11... | collective-permute-start | bytes 1179656 | tf_op jit(solution)/shard_map/ppermute | solution.py:445
  18.4 6.7 %collective-permute-start.8 = (bf16[16,4352]{1,0:T(8,128)(2,1)S(1)}, bf16[16,4352]{1,0:T(8,128)(2,1)S(1)}, u32[]{:S(2)}, u32[]{:S(2)}) collective-permute-start(bf16[16,4352]{1,0:T(8,128)(2,1)S(1)} %get-tuple-element.49), channel_id=1, source_target_pairs={{0,8},{8,0},{16,24},{24,16},{1,9},{9,1},{17,25},{25,17},{2,10},{10... | collective-permute-start | bytes 417800 | tf_op jit(solution)/shard_map/ppermute | solution.py:432
  19.5 8.7 %collective-permute-start.9 = (bf16[16,4352]{1,0:T(8,128)(2,1)S(1)}, bf16[16,4352]{1,0:T(8,128)(2,1)S(1)}, u32[]{:S(2)}, u32[]{:S(2)}) collective-permute-start(bf16[16,4352]{1,0:T(8,128)(2,1)S(1)} %get-tuple-element.50), channel_id=1, source_target_pairs={{0,16},{8,24},{16,0},{24,8},{1,17},{9,25},{17,1},{25,9},{2,18},{10... | collective-permute-start | bytes 417800 | tf_op jit(solution)/shard_map/ppermute | solution.py:432
  20.6 7.6 %collective-permute-start.10 = (bf16[16,4352]{1,0:T(8,128)(2,1)S(1)}, bf16[16,4352]{1,0:T(8,128)(2,1)S(1)}, u32[]{:S(2)}, u32[]{:S(2)}) collective-permute-start(bf16[16,4352]{1,0:T(8,128)(2,1)S(1)} %get-tuple-element.51), channel_id=1, source_target_pairs={{0,24},{8,16},{16,8},{24,0},{1,25},{9,17},{17,9},{25,1},{2,26},{10... | collective-permute-start | bytes 417800 | tf_op jit(solution)/shard_map/ppermute | solution.py:432
  28.3 11.4 %collective-permute-start.15 = (bf16[16,4352]{1,0:T(8,128)(2,1)S(1)}, bf16[16,4352]{1,0:T(8,128)(2,1)S(1)}, u32[]{:S(2)}, u32[]{:S(2)}) collective-permute-start(bf16[16,4352]{1,0:T(8,128)(2,1)S(1)} %get-tuple-element.57.refs_0_), channel_id=1, source_target_pairs={{0,6},{1,7},{2,4},{3,5},{4,2},{5,3},{6,0},{7,1},{8,14},{9,15},{10,... | collective-permute-start | bytes 417800 | tf_op jit(solution)/shard_map/ppermute | solution.py:439
  32.0 10.6 %collective-permute-start.14 = (bf16[16,4352]{1,0:T(8,128)(2,1)S(1)}, bf16[16,4352]{1,0:T(8,128)(2,1)S(1)}, u32[]{:S(2)}, u32[]{:S(2)}) collective-permute-start(bf16[16,4352]{1,0:T(8,128)(2,1)S(1)} %get-tuple-element.57.refs_0_), channel_id=1, source_target_pairs={{0,4},{1,5},{2,6},{3,7},{4,0},{5,1},{6,2},{7,3},{8,12},{9,13},{10,... | collective-permute-start | bytes 417800 | tf_op jit(solution)/shard_map/ppermute | solution.py:439
  32.0 10.6 %collective-permute-start.13 = (bf16[16,4352]{1,0:T(8,128)(2,1)S(1)}, bf16[16,4352]{1,0:T(8,128)(2,1)S(1)}, u32[]{:S(2)}, u32[]{:S(2)}) collective-permute-start(bf16[16,4352]{1,0:T(8,128)(2,1)S(1)} %get-tuple-element.57.refs_0_), channel_id=1, source_target_pairs={{0,2},{1,3},{2,0},{3,1},{4,6},{5,7},{6,4},{7,5},{8,10},{9,11},{10,... | collective-permute-start | bytes 417800 | tf_op jit(solution)/shard_map/ppermute | solution.py:439
  32.7 6.2 %collective-permute-start.11 = (bf16[96,512]{1,0:T(8,128)(2,1)S(1)}, bf16[96,512]{1,0:T(8,128)(2,1)S(1)}, u32[]{:S(2)}, u32[]{:S(2)}) collective-permute-start(bf16[96,512]{1,0:T(8,128)(2,1)S(1)} %get-tuple-element.52), channel_id=1, source_target_pairs={{0,24},{8,0},{16,8},{24,16},{1,25},{9,1},{17,9},{25,17},{2,26},{10... | collective-permute-start | bytes 294920 | tf_op jit(solution)/shard_map/ppermute | solution.py:537
  33.9 5.0 %collective-permute-start.12 = (bf16[48,512]{1,0:T(8,128)(2,1)S(1)}, bf16[48,512]{1,0:T(8,128)(2,1)S(1)}, u32[]{:S(2)}, u32[]{:S(2)}) collective-permute-start(bf16[48,512]{1,0:T(8,128)(2,1)S(1)} %get-tuple-element.53), channel_id=1, source_target_pairs={{0,8},{8,16},{16,24},{24,0},{1,9},{9,17},{17,25},{25,1},{2,10},{10... | collective-permute-start | bytes 147464 | tf_op jit(solution)/shard_map/ppermute | solution.py:538
  42.7 1.6 %collective-permute-start.16 = (f32[16,4352]{1,0:T(8,128)S(1)}, f32[16,4352]{1,0:T(8,128)S(1)}, u32[]{:S(2)}, u32[]{:S(2)}) collective-permute-start(f32[16,4352]{1,0:T(8,128)S(1)} %shard_map.147.mine), channel_id=1, source_target_pairs={{0,1},{1,0},{2,3},{3,2},{4,5},{5,4},{6,7},{7,6},{8,9},{9,8},{10,11... | collective-permute-start | bytes 835592 | tf_op jit(solution)/shard_map/ppermute | solution.py:445
  (1 other events, 2.4 us)

commit v5 on v4

--- a/solution.py
+++ b/solution.py
@@ -21,6 +21,9 @@
 FEATS = GROUP * HSZ
 LANES = GROUP * TILE
 NEG = -1e30
+W_ORDER = (1, 2, 3)
+CP_ORDER = (1, 2, 3)
+Z_ORDER = (3, 1, 2)
 BF = jnp.bfloat16
 F32 = jnp.float32
 VMEM = pl.BlockSpec(memory_space=pltpu.VMEM)
@@ -60,7 +63,7 @@
 
 
 def pack_kernel(
-    k, v, g, w, lengths, offsets, ahead, behind, facts, w_half, edge, first, length, pair, sems,
+    k, v, g, w, ahead, behind, w_half, edge, first, sems,
 ):
     rows = k.shape[0]
     feats = k.shape[1]
@@ -73,16 +76,12 @@
         (g.at[pl.ds(rows - EDGE, EDGE)], edge.at[0]),
         (g.at[pl.ds(0, EDGE)], edge.at[1]),
         (w.at[:, half_cols(core, w.shape[1])], w_half),
-        (lengths, length),
-        (offsets, pair),
     ]
     copies = [pltpu.make_async_copy(a, b, sems.at[i]) for i, (a, b) in enumerate(pairs)]
     for copy in copies:
         copy.start()
     for copy in copies:
         copy.wait()
-    for row, value in enumerate((length[0], pair[0, 0], pair[0, 1])):
-        facts[row : row + 1] = jnp.full((1, facts.shape[1]), value, jnp.int32)
     behind[0 : 2 * BLK] = jnp.concatenate(
         [first[0].astype(F32)[:BLK], first[1].astype(F32)[:BLK]], 0
     ).astype(BF)
@@ -96,23 +95,20 @@
     outs = (
         pltpu.VMEM((2 * BACK + EDGE, feats), BF),
         pltpu.VMEM((2 * BLK + EDGE, feats), BF),
-        pltpu.VMEM((8, 128), jnp.int32),
         pltpu.VMEM((args[3].shape[0], width // 2), BF),
     )
     return pl.pallas_call(
         pack_kernel,
         out_shape=outs,
-        in_specs=[ANY] * 6,
-        out_specs=(VMEM,) * 4,
+        in_specs=[ANY] * 4,
+        out_specs=(VMEM,) * 3,
         scratch_shapes=[
             pltpu.VMEM((2, EDGE, width), BF),
             pltpu.VMEM((2, AHEAD, feats), BF),
-            pltpu.SMEM((1,), jnp.int32),
-            pltpu.SMEM((1, 2), jnp.int32),
-            pltpu.SemaphoreType.DMA((9,)),
+            pltpu.SemaphoreType.DMA((7,)),
         ],
         compiler_params=pltpu.CompilerParams(vmem_limit_bytes=40 * 1024 * 1024),
-    )(*[x if x.ndim == 1 else pltpu.with_memory_space_constraint(x, pltpu.HBM) for x in args])
+    )(*[pltpu.with_memory_space_constraint(x, pltpu.HBM) for x in args])
 
 
 def head_of(dims):
@@ -203,7 +199,10 @@
         out[out_at : out_at + count, cols] = jnp.where(frame < length, total, 0.0).astype(BF)
 
 
-def inner_conv_kernel(g, taps, facts, out, gx):
+def inner_conv_kernel(g, taps, lengths, offsets, out, facts, gx, pair, sem):
+    copy = pltpu.make_async_copy(offsets, pair, sem)
+    copy.start()
+    facts[0:1] = jnp.full((1, facts.shape[1]), lengths[0], jnp.int32)
     rows = g.shape[0]
     base = lax.axis_index("cp") * rows
     gx[0:8] = jnp.zeros((8, gx.shape[1]), F32)
@@ -211,6 +210,9 @@
     length = facts[0:1, 0:1]
     gx[8 : 8 + rows] = masked(g[...], base, length)
     convolve(out, 0, gx, 8, taps, base, rows, length)
+    copy.wait()
+    for row in range(2):
+        facts[row + 1 : row + 2] = jnp.full((1, facts.shape[1]), pair[0, row], jnp.int32)
 
 
 def forward_kernel(q, k, v, near, far, g, stream, facts, att_out, send, kx, vx, half_gx):
@@ -280,6 +282,10 @@
             pieces[by - 1][...] = block.astype(BF)
 
 
+def ordered(arrays, order):
+    return [arrays[by - 1] for by in order] if len(arrays) == len(order) else arrays
+
+
 def tree_sum(terms):
     while len(terms) > 1:
         terms = [a + b for a, b in zip(terms[::2], terms[1::2])]
@@ -318,13 +324,13 @@
         refs[-1][k] = ref[...]
 
 
-def own_columns_kernel(after, w, *refs):
+def own_columns_kernel(order, after, w, *refs):
     wx = refs[-1]
     shard, width = w.shape
     place = lax.axis_index("cp")
     core = lax.rem(lax.axis_index("dp"), 2)
     wx[pl.ds(pl.multiple_of(place * shard, shard), shard)] = w[:, half_cols(core, width)]
-    for by, ref in enumerate(refs[:-1], 1):
+    for by, ref in zip(order, refs[:-1]):
         at = lax.bitwise_xor(place, by) * shard
         wx[pl.ds(pl.multiple_of(at, shard), shard)] = ref[...]
 
@@ -427,12 +433,12 @@
     upward = [(i, (i + 1) % cps) for i in range(cps)]
     downward = [(i, (i - 1) % cps) for i in range(cps)]
 
-    def over_cp(arrays):
+    def over_cp(arrays, order):
         got = [
             lax.ppermute(arrays[by - 1], "cp", [(i, i ^ by) for i in range(cps)])
-            for by in range(cps - 1, 0, -1)
+            for by in order
         ]
-        return got[::-1]
+        return [got[order.index(by)] for by in range(1, cps)]
 
     def over_z(array):
         got = [
@@ -444,17 +450,22 @@
     def over_core(array):
         return lax.ppermute(array, "dp", [(i, i ^ 1) for i in range(dps)])
 
-    ahead, behind, facts, w_half = packed(k, v, g, out_weight, lengths, offsets)
+    ahead, behind, w_half = packed(k, v, g, out_weight)
     near = lax.ppermute(ahead, "cp", upward)
     far = lax.ppermute(behind, "cp", downward)
-    inner = call(
+    inner, facts = call(
         inner_conv_kernel,
-        shape((rows, width), BF),
-        [VMEM] * 3,
-        (g, conv_weight, facts),
-        [pltpu.VMEM((rows + 16, width), F32)],
-    )
-    w_got = over_cp([w_half] * (cps - 1))
+        (shape((rows, width), BF), shape((8, 128), jnp.int32)),
+        [VMEM] * 2 + [pl.BlockSpec(memory_space=pltpu.SMEM), ANY],
+        (g, conv_weight, lengths, pltpu.with_memory_space_constraint(offsets, pltpu.HBM)),
+        [
+            pltpu.VMEM((rows + 16, width), F32),
+            pltpu.SMEM((1, 2), jnp.int32),
+            pltpu.SemaphoreType.DMA,
+        ],
+    )
+    falling, rising = list(range(cps - 1, 0, -1)), list(range(1, cps))
+    w_got = over_cp([w_half] * (cps - 1), falling)
     ext_scratch = [pltpu.VMEM((ext, feats), BF)] * 2
     att, conv_send = call(
         forward_kernel,
@@ -477,11 +488,12 @@
         [pltpu.VMEM((64, width), F32), pltpu.VMEM((feats, rows), BF)],
     )
     core_got = over_core(send)
+    w_order = W_ORDER if cps == 4 else tuple(range(1, cps))
     w_cols = call(
-        own_columns_kernel,
+        functools.partial(own_columns_kernel, w_order),
         shape((feats, width // 2), BF),
         [ANY] + [VMEM] * cps,
-        (send, out_weight, *w_got),
+        (send, out_weight, *ordered(w_got, w_order)),
         flops=2**34,
     )
     conv = call(
@@ -501,7 +513,7 @@
         [VMEM] * 3,
         (keep, core_got, conv),
     )
-    cp_got = over_cp(pieces)
+    cp_got = over_cp(pieces, rising)
     token = shape((8, 128), F32)
     passed = over_core(
         call(
@@ -532,7 +544,7 @@
         cp_sum_kernel,
         (shape((16, wide), BF), shape(back.shape, BF), shape(onward.shape, BF)),
         [VMEM] * (cps + 3),
-        (bwd_done, back, onward, own, *cp_got),
+        (bwd_done, back, onward, own, *ordered(cp_got, CP_ORDER)),
     )
     last = lax.ppermute(back, "cp", downward)
     first = lax.ppermute(onward, "cp", upward)
@@ -559,7 +571,7 @@
             z_sum_kernel,
             shape((16, wide), F32),
             [VMEM] * (floors + 1),
-            (join_done, part, *over_z(part)),
+            (join_done, part, *ordered(over_z(part), Z_ORDER)),
         )
         weight_grad, conv_grad = call(
             final_kernel,

time: 45.3 us -> 43.7 us (0.965)
  the two profiles are of different devices: /device:TPU:0 before, /device:TPU:19 now
where the time goes in v5:
time: 43.7 us; the launch traced here: 43.5 us
  starting transfers between devices  16.3 us (37%)
  waiting for transfers between devices  14.6 us (33%)
  Pallas kernels  11.1 us (25%)
  between operations  1.45 us (3%)
    pallas_call x12, Pallas kernels, call(): pl.pallas_call(kernel, out_shape=outs, in_specs=ins, out_specs=jax.tree.m...  9.94 us
    ppermute x3, waiting for transfers between devices, over_z(): lax.ppermute(array, 'dp', [(i, i ^ 2 * by) for i in range(dps)])  7.34 us
    ppermute x6, starting transfers between devices, over_cp(): lax.ppermute(arrays[by - 1], 'cp', [(i, i ^ by) for i in range(cps)])  5.31 us
    ppermute x4, starting transfers between devices, over_core(): return lax.ppermute(array, 'dp', [(i, i ^ 1) for i in range(dps)])  4.44 us
    ppermute x6, waiting for transfers between devices, over_cp(): lax.ppermute(arrays[by - 1], 'cp', [(i, i ^ by) for i in range(cps)])  3.11 us
    ppermute x3, starting transfers between devices, over_z(): lax.ppermute(array, 'dp', [(i, i ^ 2 * by) for i in range(dps)])  2.71 us
    ppermute x1, starting transfers between devices, body(): first = lax.ppermute(onward, 'cp', upward)  2.36 us
    ppermute x1, waiting for transfers between devices, body(): first = lax.ppermute(onward, 'cp', upward)  2.24 us
  transfers between devices with their start and end apart: 17, of which 9 were waited for; matrix products, arithmetic and copies ran while one was open for 0% of the time, Pallas kernels for 20%

profile of v5, /device:TPU:19, one launch (start us, length us, event | category | flops | bytes accessed | tf_op | source)
XLA Modules:
  0.0 43.5 jit_solution(3439263472674154653)
XLA Ops:
  0.7 1.2 %shard_map.136 = (bf16[112,512]{1,0:T(8,128)(2,1)S(1)}, bf16[64,512]{1,0:T(8,128)(2,1)S(1)}, bf16[128,512]{1,0:T(8,128)(2,1)S(1)}) custom-call(bf16[192,512]{1,0:T(8,128)(2,1)} %bitcast.14, bf16[192,512]{1,0:T(8,128)(2,1)} %bitcast.17, bf16[192,1024]{1,0:T(8,128)(2,1)} %bitcast.9, bf16[128,1024]{1,0:T(8,128)(2,1)} %w.5), custom_call_target="tpu_custom_call" | custom-call | tf_op jit(solution)/shard_map/pallas_call | solution.py:100
  1.8 1.3 %collective-permute-start = (bf16[112,512]{1,0:T(8,128)(2,1)S(1)}, bf16[112,512]{1,0:T(8,128)(2,1)S(1)}, u32[]{:S(2)}, u32[]{:S(2)}) collective-permute-start(bf16[112,512]{1,0:T(8,128)(2,1)S(1)} %get-tuple-element.34), channel_id=1, source_target_pairs={{0,8},{8,16},{16,24},{24,0},{1,9},{9,17},{17,25},{25,1},{2,10},{10... | collective-permute-start | bytes 344072 | tf_op jit(solution)/shard_map/ppermute | solution.py:454
  3.4 2.1 %collective-permute-start.5 = (bf16[128,512]{1,0:T(8,128)(2,1)S(1)}, bf16[128,512]{1,0:T(8,128)(2,1)S(1)}, u32[]{:S(2)}, u32[]{:S(2)}) collective-permute-start(bf16[128,512]{1,0:T(8,128)(2,1)S(1)} %get-tuple-element.41), channel_id=1, source_target_pairs={{0,24},{8,16},{16,8},{24,0},{1,25},{9,17},{17,9},{25,1},{2,26},{10... | collective-permute-start | bytes 393224 | tf_op jit(solution)/shard_map/ppermute | solution.py:438
  5.7 0.3 collective-permute-start.3
  6.7 1.0 %shard_map.137 = (bf16[192,1024]{1,0:T(8,128)(2,1)S(1)}, s32[8,128]{1,0:T(8,128)S(1)}) custom-call(bf16[192,1024]{1,0:T(8,128)(2,1)S(1)} %bitcast.10, f32[7,1024]{1,0:T(8,128)S(1)} %copy-done.7, s32[1]{0:T(128)S(6)} %copy.15.lengths, s32[1,2]{1,0:T(1,128)} %offsets.1), custom_call_target="tpu_custom_call" | custom-call | tf_op jit(solution)/shard_map/pallas_call | solution.py:46
  8.0 1.5 %shard_map.138 = (bf16[192,512]{1,0:T(8,128)(2,1)S(1)}, bf16[592,512]{1,0:T(8,128)(2,1)S(1)}) custom-call(bf16[192,512]{1,0:T(8,128)(2,1)S(1)} %bitcast.23, bf16[192,512]{1,0:T(8,128)(2,1)S(1)} %bitcast.15, bf16[192,512]{1,0:T(8,128)(2,1)S(1)} %bitcast.18, bf16[112,512]{1,0:T(8,128)(2,1)S(1)} %collective-permute-done.near, ...), custom_call_target="tpu_custom_call" | custom-call | flops 4294967296 | tf_op jit(solution)/shard_map/pallas_call | solution.py:46
  9.5 3.2 %collective-permute-start.6 = (bf16[592,512]{1,0:T(8,128)(2,1)S(1)}, bf16[592,512]{1,0:T(8,128)(2,1)S(1)}, u32[]{:S(2)}, u32[]{:S(2)}) collective-permute-start(bf16[592,512]{1,0:T(8,128)(2,1)S(1)} %get-tuple-element.42), channel_id=1, source_target_pairs={{0,1},{1,0},{2,3},{3,2},{4,5},{5,4},{6,7},{7,6},{8,9},{9,8},{10,11... | collective-permute-start | bytes 1818632 | tf_op jit(solution)/shard_map/ppermute | solution.py:451
  12.7 1.1 %shard_map.139 = (bf16[192,1024]{1,0:T(8,128)(2,1)}, bf16[4,64,1024]{2,1,0:T(8,128)(2,1)S(1)}, f32[4,64,1024]{2,1,0:T(8,128)S(1)}) custom-call(bf16[192,512]{1,0:T(8,128)(2,1)S(1)} %get-tuple-element.37.att, bf16[112,512]{1,0:T(8,128)(2,1)S(1)} %collective-permute-done.near, bf16[64,512]{1,0:T(8,128)(2,1)S(1)} %collective-permute-done.1.far, ...), custom_call_target="tpu_custom_call" | custom-call | tf_op jit(solution)/shard_map/pallas_call | solution.py:46
  14.0 0.4 collective-permute-done.6.other
  14.3 1.2 %shard_map.141.conv = f32[8,512]{1,0:T(8,128)S(1)} custom-call(bf16[192,512]{1,0:T(8,128)(2,1)S(1)} %get-tuple-element.37.att, bf16[512,512]{1,0:T(8,128)(2,1)S(1)} %shard_map.140.wx, bf16[192,1024]{1,0:T(8,128)(2,1)S(1)} %bitcast.21, bf16[192,1024]{1,0:T(8,128)(2,1)S(1)} %bitcast.13, bf16[112,512]{1,0:T(8,128)(2,1)S(1)} %collective-permute-done.near, ...), custom_call_target="tpu_custom_call" | custom-call | tf_op jit(solution)/shard_map/pallas_call | solution.py:46
  15.8 0.7 %collective-permute-start.7 = (bf16[3,128,512]{2,1,0:T(8,128)(2,1)S(1)}, bf16[3,128,512]{2,1,0:T(8,128)(2,1)S(1)}, u32[]{:S(2)}, u32[]{:S(2)}) collective-permute-start(bf16[3,128,512]{2,1,0:T(8,128)(2,1)S(1)} %shard_map.143), channel_id=1, source_target_pairs={{0,1},{1,0},{2,3},{3,2},{4,5},{5,4},{6,7},{7,6},{8,9},{9,8},{10,11... | collective-permute-start | bytes 1179656 | tf_op jit(solution)/shard_map/ppermute | solution.py:451
  16.5 0.8 %collective-permute-start.8 = (bf16[16,4352]{1,0:T(8,128)(2,1)S(1)}, bf16[16,4352]{1,0:T(8,128)(2,1)S(1)}, u32[]{:S(2)}, u32[]{:S(2)}) collective-permute-start(bf16[16,4352]{1,0:T(8,128)(2,1)S(1)} %get-tuple-element.51), channel_id=1, source_target_pairs={{0,8},{8,0},{16,24},{24,16},{1,9},{9,1},{17,25},{25,17},{2,10},{10... | collective-permute-start | bytes 417800 | tf_op jit(solution)/shard_map/ppermute | solution.py:438
  17.5 1.7 %collective-permute-start.10 = (bf16[16,4352]{1,0:T(8,128)(2,1)S(1)}, bf16[16,4352]{1,0:T(8,128)(2,1)S(1)}, u32[]{:S(2)}, u32[]{:S(2)}) collective-permute-start(bf16[16,4352]{1,0:T(8,128)(2,1)S(1)} %get-tuple-element.53), channel_id=1, source_target_pairs={{0,24},{8,16},{16,8},{24,0},{1,25},{9,17},{17,9},{25,1},{2,26},{10... | collective-permute-start | bytes 417800 | tf_op jit(solution)/shard_map/ppermute | solution.py:438
  19.1 3.2 %shard_map.144 = (bf16[192,512]{1,0:T(8,128)(2,1)}, f32[192,512]{1,0:T(8,128)S(1)}, f32[192,512]{1,0:T(8,128)S(1)}, bf16[96,512]{1,0:T(8,128)(2,1)S(1)}, bf16[48...) custom-call(f32[16,4352]{1,0:T(8,128)S(1)} %get-tuple-element.43.after.refs_0_, bf16[192,512]{1,0:T(8,128)(2,1)S(1)} %bitcast.24, ...), custom_call_target="tpu_custom_call" | custom-call | bytes 10485760 | tf_op jit(solution)/shard_map/pallas_call | solution.py:46
  22.3 3.0 %collective-permute-done.10.refs_3_ = bf16[16,4352]{1,0:T(8,128)(2,1)S(1)} collective-permute-done((bf16[16,4352]{1,0:T(8,128)(2,1)S(1)}, bf16[16,4352]{1,0:T(8,128)(2,1)S(1)}, u32[]{:S(2)}, u32[]{:S(2)}) %collective-permute-start.10) | collective-permute-done | bytes 139296 | tf_op jit(solution)/shard_map/ppermute | solution.py:438
  25.5 1.3 %collective-permute-start.14 = (bf16[16,4352]{1,0:T(8,128)(2,1)S(1)}, bf16[16,4352]{1,0:T(8,128)(2,1)S(1)}, u32[]{:S(2)}, u32[]{:S(2)}) collective-permute-start(bf16[16,4352]{1,0:T(8,128)(2,1)S(1)} %get-tuple-element.59.refs_0_), channel_id=1, source_target_pairs={{0,2},{1,3},{2,0},{3,1},{4,6},{5,7},{6,4},{7,5},{8,10},{9,11},{10,... | collective-permute-start | bytes 417800 | tf_op jit(solution)/shard_map/ppermute | solution.py:445
  26.8 1.3 %collective-permute-start.13 = (bf16[16,4352]{1,0:T(8,128)(2,1)S(1)}, bf16[16,4352]{1,0:T(8,128)(2,1)S(1)}, u32[]{:S(2)}, u32[]{:S(2)}) collective-permute-start(bf16[16,4352]{1,0:T(8,128)(2,1)S(1)} %get-tuple-element.59.refs_0_), channel_id=1, source_target_pairs={{0,6},{1,7},{2,4},{3,5},{4,2},{5,3},{6,0},{7,1},{8,14},{9,15},{10,... | collective-permute-start | bytes 417800 | tf_op jit(solution)/shard_map/ppermute | solution.py:445
  28.1 2.4 %collective-permute-start.12 = (bf16[48,512]{1,0:T(8,128)(2,1)S(1)}, bf16[48,512]{1,0:T(8,128)(2,1)S(1)}, u32[]{:S(2)}, u32[]{:S(2)}) collective-permute-start(bf16[48,512]{1,0:T(8,128)(2,1)S(1)} %get-tuple-element.55), channel_id=1, source_target_pairs={{0,8},{8,16},{16,24},{24,0},{1,9},{9,17},{17,25},{25,1},{2,10},{10... | collective-permute-start | bytes 147464 | tf_op jit(solution)/shard_map/ppermute | solution.py:550
  30.4 2.2 %collective-permute-done.12.first = bf16[48,512]{1,0:T(8,128)(2,1)S(1)} collective-permute-done((bf16[48,512]{1,0:T(8,128)(2,1)S(1)}, bf16[48,512]{1,0:T(8,128)(2,1)S(1)}, u32[]{:S(2)}, u32[]{:S(2)}) %collective-permute-start.12) | collective-permute-done | bytes 49184 | tf_op jit(solution)/shard_map/ppermute | solution.py:550
  32.7 0.8 %shard_map.146 = (bf16[192,512]{1,0:T(8,128)(2,1)}, bf16[192,512]{1,0:T(8,128)(2,1)}, f32[8,128]{1,0:T(8,128)S(1)}) custom-call(f32[192,512]{1,0:T(8,128)S(1)} %get-tuple-element.46.key_g, f32[192,512]{1,0:T(8,128)S(1)} %get-tuple-element.47.value_g, bf16[96,512]{1,0:T(8,128)(2,1)S(1)} %collective-permute-done.11.last, ...), custom_call_target="tpu_custom_call" | custom-call | tf_op jit(solution)/shard_map/pallas_call | solution.py:46
  33.5 7.3 %collective-permute-done.13.refs_1_ = bf16[16,4352]{1,0:T(8,128)(2,1)S(1)} collective-permute-done((bf16[16,4352]{1,0:T(8,128)(2,1)S(1)}, bf16[16,4352]{1,0:T(8,128)(2,1)S(1)}, u32[]{:S(2)}, u32[]{:S(2)}) %collective-permute-start.13) | collective-permute-done | bytes 139296 | tf_op jit(solution)/shard_map/ppermute | solution.py:445
  41.0 0.6 %collective-permute-start.16 = (f32[16,4352]{1,0:T(8,128)S(1)}, f32[16,4352]{1,0:T(8,128)S(1)}, u32[]{:S(2)}, u32[]{:S(2)}) collective-permute-start(f32[16,4352]{1,0:T(8,128)S(1)} %shard_map.147.mine), channel_id=1, source_target_pairs={{0,1},{1,0},{2,3},{3,2},{4,5},{5,4},{6,7},{7,6},{8,9},{9,8},{10,11... | collective-permute-start | bytes 835592 | tf_op jit(solution)/shard_map/ppermute | solution.py:451
  41.5 1.2 %collective-permute-done.16.theirs = f32[16,4352]{1,0:T(8,128)S(1)} collective-permute-done((f32[16,4352]{1,0:T(8,128)S(1)}, f32[16,4352]{1,0:T(8,128)S(1)}, u32[]{:S(2)}, u32[]{:S(2)}) %collective-permute-start.16) | collective-permute-done | bytes 278560 | tf_op jit(solution)/shard_map/ppermute | solution.py:451
  42.7 0.8 %shard_map.148 = (f32[128,1024]{1,0:T(8,128)}, f32[7,1024]{1,0:T(8,128)}) custom-call(f32[8,128]{1,0:T(8,128)S(1)} %get-tuple-element.58.after, f32[16,4352]{1,0:T(8,128)S(1)} %shard_map.147.mine, f32[16,4352]{1,0:T(8,128)S(1)} %collective-permute-done.16.theirs), custom_call_target="tpu_custom_call" | custom-call | tf_op jit(solution)/shard_map/pallas_call | solution.py:46
  (39 shorter events, 1.7 us)
Async XLA Ops:
  0.6 6.0 %copy-start = (bf16[1,192,1024]{2,1,0:T(8,128)(2,1)S(1)}, bf16[1,192,1024]{2,1,0:T(8,128)(2,1)}, u32[]{:S(2)}) copy-start(bf16[1,192,1024]{2,1,0:T(8,128)(2,1)} %param.13) | copy-start | bytes 1179652
  0.6 6.0 %copy-start.7 = (f32[7,1024]{1,0:T(8,128)S(1)}, f32[7,1024]{1,0:T(8,128)}, u32[]{:S(2)}) copy-start(f32[7,1024]{1,0:T(8,128)} %taps.3) | copy-start | bytes 86020
  0.7 7.3 %copy-start.4 = (bf16[1,192,1024]{2,1,0:T(8,128)(2,1)S(1)}, bf16[1,192,1024]{2,1,0:T(8,128)(2,1)}, u32[]{:S(2)}) copy-start(bf16[1,192,1024]{2,1,0:T(8,128)(2,1)} %param.12) | copy-start | bytes 1179652
  0.7 7.3 %copy-start.6 = (bf16[1,192,512]{2,1,0:T(8,128)(2,1)S(1)}, bf16[1,192,512]{2,1,0:T(8,128)(2,1)}, u32[]{:S(2)}) copy-start(bf16[1,192,512]{2,1,0:T(8,128)(2,1)} %param.9) | copy-start | bytes 589828
  1.8 6.1 %collective-permute-start = (bf16[112,512]{1,0:T(8,128)(2,1)S(1)}, bf16[112,512]{1,0:T(8,128)(2,1)S(1)}, u32[]{:S(2)}, u32[]{:S(2)}) collective-permute-start(bf16[112,512]{1,0:T(8,128)(2,1)S(1)} %get-tuple-element.34), channel_id=1, source_target_pairs={{0,8},{8,16},{16,24},{24,0},{1,9},{9,17},{17,25},{25,1},{2,10},{10... | collective-permute-start | bytes 344072 | tf_op jit(solution)/shard_map/ppermute | solution.py:454
  3.1 4.9 %collective-permute-start.1 = (bf16[64,512]{1,0:T(8,128)(2,1)S(1)}, bf16[64,512]{1,0:T(8,128)(2,1)S(1)}, u32[]{:S(2)}, u32[]{:S(2)}) collective-permute-start(bf16[64,512]{1,0:T(8,128)(2,1)S(1)} %get-tuple-element.35), channel_id=1, source_target_pairs={{0,24},{8,0},{16,8},{24,16},{1,25},{9,1},{17,9},{25,17},{2,26},{10... | collective-permute-start | bytes 196616 | tf_op jit(solution)/shard_map/ppermute | solution.py:455
  3.4 10.4 %collective-permute-start.5 = (bf16[128,512]{1,0:T(8,128)(2,1)S(1)}, bf16[128,512]{1,0:T(8,128)(2,1)S(1)}, u32[]{:S(2)}, u32[]{:S(2)}) collective-permute-start(bf16[128,512]{1,0:T(8,128)(2,1)S(1)} %get-tuple-element.41), channel_id=1, source_target_pairs={{0,24},{8,16},{16,8},{24,0},{1,25},{9,17},{17,9},{25,1},{2,26},{10... | collective-permute-start | bytes 393224 | tf_op jit(solution)/shard_map/ppermute | solution.py:438
  5.5 8.4 %collective-permute-start.4 = (bf16[128,512]{1,0:T(8,128)(2,1)S(1)}, bf16[128,512]{1,0:T(8,128)(2,1)S(1)}, u32[]{:S(2)}, u32[]{:S(2)}) collective-permute-start(bf16[128,512]{1,0:T(8,128)(2,1)S(1)} %get-tuple-element.41), channel_id=1, source_target_pairs={{0,16},{8,24},{16,0},{24,8},{1,17},{9,25},{17,1},{25,9},{2,18},{10... | collective-permute-start | bytes 393224 | tf_op jit(solution)/shard_map/ppermute | solution.py:438
  5.7 8.2 %collective-permute-start.3 = (bf16[128,512]{1,0:T(8,128)(2,1)S(1)}, bf16[128,512]{1,0:T(8,128)(2,1)S(1)}, u32[]{:S(2)}, u32[]{:S(2)}) collective-permute-start(bf16[128,512]{1,0:T(8,128)(2,1)S(1)} %get-tuple-element.41), channel_id=1, source_target_pairs={{0,8},{8,0},{16,24},{24,16},{1,9},{9,1},{17,25},{25,17},{2,10},{10... | collective-permute-start | bytes 393224 | tf_op jit(solution)/shard_map/ppermute | solution.py:438
  6.7 1.3 %copy-start.2 = (bf16[1,192,512]{2,1,0:T(8,128)(2,1)S(1)}, bf16[1,192,512]{2,1,0:T(8,128)(2,1)}, u32[]{:S(2)}) copy-start(bf16[1,192,512]{2,1,0:T(8,128)(2,1)} %param.10) | copy-start | bytes 589828
  6.7 1.3 %copy-start.3 = (bf16[1,192,512]{2,1,0:T(8,128)(2,1)S(1)}, bf16[1,192,512]{2,1,0:T(8,128)(2,1)}, u32[]{:S(2)}) copy-start(bf16[1,192,512]{2,1,0:T(8,128)(2,1)} %param.11) | copy-start | bytes 589828
  9.5 4.8 %collective-permute-start.6 = (bf16[592,512]{1,0:T(8,128)(2,1)S(1)}, bf16[592,512]{1,0:T(8,128)(2,1)S(1)}, u32[]{:S(2)}, u32[]{:S(2)}) collective-permute-start(bf16[592,512]{1,0:T(8,128)(2,1)S(1)} %get-tuple-element.42), channel_id=1, source_target_pairs={{0,1},{1,0},{2,3},{3,2},{4,5},{5,4},{6,7},{7,6},{8,9},{9,8},{10,11... | collective-permute-start | bytes 1818632 | tf_op jit(solution)/shard_map/ppermute | solution.py:451
  13.7 1.9 %collective-permute-start.2 = (bf16[4,64,1024]{2,1,0:T(8,128)(2,1)S(1)}, bf16[4,64,1024]{2,1,0:T(8,128)(2,1)S(1)}, u32[]{:S(2)}, u32[]{:S(2)}) collective-permute-start(bf16[4,64,1024]{2,1,0:T(8,128)(2,1)S(1)} %get-tuple-element.40.after), channel_id=1, source_target_pairs={{0,1},{1,0},{2,3},{3,2},{4,5},{5,4},{6,7},{7,6},{8,9},{9,8},{10,11... | collective-permute-start | bytes 1572872 | tf_op jit(solution)/shard_map/ppermute | solution.py:451
  15.7 3.4 %copy-start.5 = (bf16[192,1024]{1,0:T(8,128)(2,1)S(1)}, bf16[192,1024]{1,0:T(8,128)(2,1)}, u32[]{:S(2)}) copy-start(bf16[192,1024]{1,0:T(8,128)(2,1)} %get-tuple-element.44.stream_grad) | copy-start | bytes 1179652
  15.8 3.4 %collective-permute-start.7 = (bf16[3,128,512]{2,1,0:T(8,128)(2,1)S(1)}, bf16[3,128,512]{2,1,0:T(8,128)(2,1)S(1)}, u32[]{:S(2)}, u32[]{:S(2)}) collective-permute-start(bf16[3,128,512]{2,1,0:T(8,128)(2,1)S(1)} %shard_map.143), channel_id=1, source_target_pairs={{0,1},{1,0},{2,3},{3,2},{4,5},{5,4},{6,7},{7,6},{8,9},{9,8},{10,11... | collective-permute-start | bytes 1179656 | tf_op jit(solution)/shard_map/ppermute | solution.py:451
  16.5 5.8 %collective-permute-start.8 = (bf16[16,4352]{1,0:T(8,128)(2,1)S(1)}, bf16[16,4352]{1,0:T(8,128)(2,1)S(1)}, u32[]{:S(2)}, u32[]{:S(2)}) collective-permute-start(bf16[16,4352]{1,0:T(8,128)(2,1)S(1)} %get-tuple-element.51), channel_id=1, source_target_pairs={{0,8},{8,0},{16,24},{24,16},{1,9},{9,1},{17,25},{25,17},{2,10},{10... | collective-permute-start | bytes 417800 | tf_op jit(solution)/shard_map/ppermute | solution.py:438
  17.2 5.1 %collective-permute-start.9 = (bf16[16,4352]{1,0:T(8,128)(2,1)S(1)}, bf16[16,4352]{1,0:T(8,128)(2,1)S(1)}, u32[]{:S(2)}, u32[]{:S(2)}) collective-permute-start(bf16[16,4352]{1,0:T(8,128)(2,1)S(1)} %get-tuple-element.52), channel_id=1, source_target_pairs={{0,16},{8,24},{16,0},{24,8},{1,17},{9,25},{17,1},{25,9},{2,18},{10... | collective-permute-start | bytes 417800 | tf_op jit(solution)/shard_map/ppermute | solution.py:438
  17.5 7.8 %collective-permute-start.10 = (bf16[16,4352]{1,0:T(8,128)(2,1)S(1)}, bf16[16,4352]{1,0:T(8,128)(2,1)S(1)}, u32[]{:S(2)}, u32[]{:S(2)}) collective-permute-start(bf16[16,4352]{1,0:T(8,128)(2,1)S(1)} %get-tuple-element.53), channel_id=1, source_target_pairs={{0,24},{8,16},{16,8},{24,0},{1,25},{9,17},{17,9},{25,1},{2,26},{10... | collective-permute-start | bytes 417800 | tf_op jit(solution)/shard_map/ppermute | solution.py:438
  25.4 8.2 %collective-permute-start.15 = (bf16[16,4352]{1,0:T(8,128)(2,1)S(1)}, bf16[16,4352]{1,0:T(8,128)(2,1)S(1)}, u32[]{:S(2)}, u32[]{:S(2)}) collective-permute-start(bf16[16,4352]{1,0:T(8,128)(2,1)S(1)} %get-tuple-element.59.refs_0_), channel_id=1, source_target_pairs={{0,4},{1,5},{2,6},{3,7},{4,0},{5,1},{6,2},{7,3},{8,12},{9,13},{10,... | collective-permute-start | bytes 417800 | tf_op jit(solution)/shard_map/ppermute | solution.py:445
  25.5 8.1 %collective-permute-start.14 = (bf16[16,4352]{1,0:T(8,128)(2,1)S(1)}, bf16[16,4352]{1,0:T(8,128)(2,1)S(1)}, u32[]{:S(2)}, u32[]{:S(2)}) collective-permute-start(bf16[16,4352]{1,0:T(8,128)(2,1)S(1)} %get-tuple-element.59.refs_0_), channel_id=1, source_target_pairs={{0,2},{1,3},{2,0},{3,1},{4,6},{5,7},{6,4},{7,5},{8,10},{9,11},{10,... | collective-permute-start | bytes 417800 | tf_op jit(solution)/shard_map/ppermute | solution.py:445
  26.8 14.1 %collective-permute-start.13 = (bf16[16,4352]{1,0:T(8,128)(2,1)S(1)}, bf16[16,4352]{1,0:T(8,128)(2,1)S(1)}, u32[]{:S(2)}, u32[]{:S(2)}) collective-permute-start(bf16[16,4352]{1,0:T(8,128)(2,1)S(1)} %get-tuple-element.59.refs_0_), channel_id=1, source_target_pairs={{0,6},{1,7},{2,4},{3,5},{4,2},{5,3},{6,0},{7,1},{8,14},{9,15},{10,... | collective-permute-start | bytes 417800 | tf_op jit(solution)/shard_map/ppermute | solution.py:445
  28.1 4.7 %collective-permute-start.11 = (bf16[96,512]{1,0:T(8,128)(2,1)S(1)}, bf16[96,512]{1,0:T(8,128)(2,1)S(1)}, u32[]{:S(2)}, u32[]{:S(2)}) collective-permute-start(bf16[96,512]{1,0:T(8,128)(2,1)S(1)} %get-tuple-element.54), channel_id=1, source_target_pairs={{0,24},{8,0},{16,8},{24,16},{1,25},{9,1},{17,9},{25,17},{2,26},{10... | collective-permute-start | bytes 294920 | tf_op jit(solution)/shard_map/ppermute | solution.py:549
  28.1 4.6 %collective-permute-start.12 = (bf16[48,512]{1,0:T(8,128)(2,1)S(1)}, bf16[48,512]{1,0:T(8,128)(2,1)S(1)}, u32[]{:S(2)}, u32[]{:S(2)}) collective-permute-start(bf16[48,512]{1,0:T(8,128)(2,1)S(1)} %get-tuple-element.55), channel_id=1, source_target_pairs={{0,8},{8,16},{16,24},{24,0},{1,9},{9,17},{17,25},{25,1},{2,10},{10... | collective-permute-start | bytes 147464 | tf_op jit(solution)/shard_map/ppermute | solution.py:550
  41.0 1.7 %collective-permute-start.16 = (f32[16,4352]{1,0:T(8,128)S(1)}, f32[16,4352]{1,0:T(8,128)S(1)}, u32[]{:S(2)}, u32[]{:S(2)}) collective-permute-start(f32[16,4352]{1,0:T(8,128)S(1)} %shard_map.147.mine), channel_id=1, source_target_pairs={{0,1},{1,0},{2,3},{3,2},{4,5},{5,4},{6,7},{7,6},{8,9},{9,8},{10,11... | collective-permute-start | bytes 835592 | tf_op jit(solution)/shard_map/ppermute | solution.py:451
  (1 other events, 1.2 us)

commit v6 on v5

--- a/solution.py
+++ b/solution.py
@@ -20,6 +20,7 @@
 GROUP = 4
 FEATS = GROUP * HSZ
 LANES = GROUP * TILE
+LANE = 128
 NEG = -1e30
 W_ORDER = (1, 2, 3)
 CP_ORDER = (1, 2, 3)
@@ -166,36 +167,38 @@
     return jnp.where((frame >= 0) & (frame < length), block.astype(F32), 0.0)
 
 
-def fill_rims(gx, at, near, far, base, rows, length):
-    feats = near.shape[1]
+def put(gx, at, block):
+    for chunk in range(gx.shape[0]):
+        gx[chunk, at : at + block.shape[0]] = block[:, chunk * LANE : (chunk + 1) * LANE]
+
+
+def rims(near, far, base, rows, length):
     before = near[2 * BACK :].astype(F32)
     after = far[2 * BLK :].astype(F32)
-    for part in range(2):
-        cols = slice(part * feats, (part + 1) * feats)
-        here = slice(part * 8, (part + 1) * 8)
-        gx[0:8, cols] = masked(before[here], base - 8, length)
-        gx[at : at + 8, cols] = masked(after[here], base + rows, length)
+    return (
+        masked(jnp.concatenate([before[:8], before[8:]], 1), base - 8, length),
+        masked(jnp.concatenate([after[:8], after[8:]], 1), base + rows, length),
+    )
 
 
 def fill_half(gx, side, g, near, far, base, length):
     rows = g.shape[0]
     before = near[2 * BACK :].astype(F32)
     after = far[2 * BLK :].astype(F32)
-    gx[0:8] = masked(jnp.where(side == 0, before[:8], before[8:]), base - 8, length)
-    gx[8 : 8 + rows] = masked(g[:, half_cols(side, g.shape[1])], base, length)
-    gx[8 + rows :] = masked(jnp.where(side == 0, after[:8], after[8:]), base + rows, length)
+    put(gx, 0, masked(jnp.where(side == 0, before[:8], before[8:]), base - 8, length))
+    put(gx, 8, masked(g[:, half_cols(side, g.shape[1])], base, length))
+    put(gx, 8 + rows, masked(jnp.where(side == 0, after[:8], after[8:]), base + rows, length))
 
 
 def convolve(out, out_at, gx, gx_at, taps, start, count, length):
-    width = out.shape[1]
-    step = 128
-    frame = start + lax.broadcasted_iota(jnp.int32, (count, step), 0)
-    for at in range(0, width, step):
-        cols = slice(at, at + step)
-        total = taps[0:1, cols] * gx[gx_at + HALF : gx_at + HALF + count, cols]
+    frame = start + lax.broadcasted_iota(jnp.int32, (count, LANE), 0)
+    for chunk in range(gx.shape[0]):
+        cols = slice(chunk * LANE, (chunk + 1) * LANE)
+        first = gx_at + HALF
+        total = taps[0:1, cols] * gx[chunk, first : first + count]
         for tap in range(1, KW):
-            top = gx_at + HALF - tap
-            total = total + taps[tap : tap + 1, cols] * gx[top : top + count, cols]
+            first = gx_at + HALF - tap
+            total = total + taps[tap : tap + 1, cols] * gx[chunk, first : first + count]
         out[out_at : out_at + count, cols] = jnp.where(frame < length, total, 0.0).astype(BF)
 
 
@@ -205,10 +208,10 @@
     facts[0:1] = jnp.full((1, facts.shape[1]), lengths[0], jnp.int32)
     rows = g.shape[0]
     base = lax.axis_index("cp") * rows
-    gx[0:8] = jnp.zeros((8, gx.shape[1]), F32)
-    gx[8 + rows :] = jnp.zeros((8, gx.shape[1]), F32)
+    gx[:, 0:8] = jnp.zeros((gx.shape[0], 8, LANE), F32)
+    gx[:, 8 + rows :] = jnp.zeros((gx.shape[0], 8, LANE), F32)
     length = facts[0:1, 0:1]
-    gx[8 : 8 + rows] = masked(g[...], base, length)
+    put(gx, 8, masked(g[...], base, length))
     convolve(out, 0, gx, 8, taps, base, rows, length)
     copy.wait()
     for row in range(2):
@@ -236,7 +239,8 @@
             send[start : start + TILE, cols] = attended
     send[rows : 2 * rows] = masked(stream[:, half_cols(1 - core, width)], base, length).astype(BF)
     fill_half(half_gx, 1 - core, g, near, far, base, length)
-    send[2 * rows :] = half_gx[...].astype(BF)
+    for chunk in range(half_gx.shape[0]):
+        send[2 * rows :, chunk * LANE : (chunk + 1) * LANE] = half_gx[chunk].astype(BF)
 
 
 def weights_kernel(att, near, far, g, taps, inner, facts, stream_grad, send, keep, gx, att_t):
@@ -252,9 +256,11 @@
             att_t[pl.ds(pl.multiple_of(at, half), half)] = turned[
                 (2 * part + side) * half : (2 * part + side + 1) * half
             ]
-    fill_rims(gx, 56, near, far, base, rows, length)
-    gx[8:32] = masked(g[0:32].astype(F32)[:24], base, length)
-    gx[32:56] = masked(g[rows - 32 :].astype(F32)[8:], base + rows - 24, length)
+    before, after = rims(near, far, base, rows, length)
+    put(gx, 0, before)
+    put(gx, 8, masked(g[0:32].astype(F32)[:24], base, length))
+    put(gx, 32, masked(g[rows - 32 :].astype(F32)[8:], base + rows - 24, length))
+    put(gx, 56, after)
     stream_grad[EDGE : rows - EDGE] = inner[EDGE : rows - EDGE]
     convolve(stream_grad, 0, gx, 8, taps, base, EDGE, length)
     convolve(stream_grad, rows - EDGE, gx, 40, taps, base + rows - EDGE, EDGE, length)
@@ -342,19 +348,18 @@
     length = facts[0:1, 0:1]
     cols = half_cols(core, width)
     fill_half(gx.at[0], core, g, near, far, base, length)
-    gx[1] = other[2 * rows :].astype(F32)
+    put(gx.at[1], 0, other[2 * rows :].astype(F32))
     mixed[0] = masked(stream[:, cols], base, length) + nn(att[...], wx[...])
     mixed[1] = other[rows : 2 * rows].astype(F32) + nn(other[0:rows], wx[...])
     conv[KW:] = jnp.zeros((8 - KW, conv.shape[1]), F32)
-    step = 128
-    for at in range(0, width // 2, step):
-        here = slice(at, at + step)
+    for chunk in range(gx.shape[1]):
+        here = slice(chunk * LANE, (chunk + 1) * LANE)
         blocks = [mixed[0, :, here], mixed[1, :, here]]
         for tap in range(KW):
             first = 8 + HALF - tap
             conv[tap : tap + 1, here] = jnp.sum(
-                blocks[0] * gx[0, first : first + rows, here]
-                + blocks[1] * gx[1, first : first + rows, here],
+                blocks[0] * gx[0, chunk, first : first + rows]
+                + blocks[1] * gx[1, chunk, first : first + rows],
                 axis=0,
                 keepdims=True,
             )
@@ -459,7 +464,7 @@
         [VMEM] * 2 + [pl.BlockSpec(memory_space=pltpu.SMEM), ANY],
         (g, conv_weight, lengths, pltpu.with_memory_space_constraint(offsets, pltpu.HBM)),
         [
-            pltpu.VMEM((rows + 16, width), F32),
+            pltpu.VMEM((width // LANE, rows + 16, LANE), F32),
             pltpu.SMEM((1, 2), jnp.int32),
             pltpu.SemaphoreType.DMA,
         ],
@@ -472,7 +477,7 @@
         (shape((rows, feats), BF), shape((3 * rows + 16, width // 2), BF)),
         [VMEM] * 8,
         (q, k, v, near, far, g, stream, facts),
-        ext_scratch + [pltpu.VMEM((rows + 16, width // 2), F32)],
+        ext_scratch + [pltpu.VMEM((width // 2 // LANE, rows + 16, LANE), F32)],
         flops=2**32,
     )
     conv_got = over_core(conv_send)
@@ -485,7 +490,7 @@
         ),
         [VMEM] * 7,
         (att, near, far, g, conv_weight, inner, facts),
-        [pltpu.VMEM((64, width), F32), pltpu.VMEM((feats, rows), BF)],
+        [pltpu.VMEM((width // LANE, 64, LANE), F32), pltpu.VMEM((feats, rows), BF)],
     )
     core_got = over_core(send)
     w_order = W_ORDER if cps == 4 else tuple(range(1, cps))
@@ -502,7 +507,7 @@
         [VMEM] * 8,
         (att, w_cols, stream, g, near, far, facts, conv_got),
         [
-            pltpu.VMEM((2, rows + 16, width // 2), F32),
+            pltpu.VMEM((2, width // 2 // LANE, rows + 16, LANE), F32),
             pltpu.VMEM((2, rows, width // 2), F32),
         ],
     )

time: 43.7 us -> 43.4 us (level)
  Pallas kernels: 11.1 us -> 10.5 us
  waiting for transfers between devices: 14.6 us -> 15.2 us
    pallas_call x12, Pallas kernels: 9.94 us -> 9.34 us  [call(): pl.pallas_call(kernel, out_shape=outs, in_specs=ins, out_specs=jax.tree.m...]
  transfers between devices with their start and end apart: 17 -> 17, of which waited for: 9 -> 9; matrix products, arithmetic and copies ran while one was open for 0% -> 0% of each run, Pallas kernels for 20% -> 19%
where the time goes in v6:
time: 43.4 us; the launch traced here: 43.2 us
  starting transfers between devices  16.1 us (37%)
  waiting for transfers between devices  15.2 us (35%)
  Pallas kernels  10.5 us (24%)
  between operations  1.45 us (3%)
    pallas_call x12, Pallas kernels, call(): pl.pallas_call(kernel, out_shape=outs, in_specs=ins, out_specs=jax.tree.m...  9.34 us
    ppermute x3, waiting for transfers between devices, over_z(): lax.ppermute(array, 'dp', [(i, i ^ 2 * by) for i in range(dps)])  7.34 us
    ppermute x6, starting transfers between devices, over_cp(): lax.ppermute(arrays[by - 1], 'cp', [(i, i ^ by) for i in range(cps)])  5.3 us
    ppermute x4, starting transfers between devices, over_core(): return lax.ppermute(array, 'dp', [(i, i ^ 1) for i in range(dps)])  4.2 us
    ppermute x6, waiting for transfers between devices, over_cp(): lax.ppermute(arrays[by - 1], 'cp', [(i, i ^ by) for i in range(cps)])  3.18 us
    ppermute x3, starting transfers between devices, over_z(): lax.ppermute(array, 'dp', [(i, i ^ 2 * by) for i in range(dps)])  2.71 us
    ppermute x1, starting transfers between devices, body(): first = lax.ppermute(onward, 'cp', upward)  2.36 us
    ppermute x1, waiting for transfers between devices, body(): first = lax.ppermute(onward, 'cp', upward)  2.13 us
  transfers between devices with their start and end apart: 17, of which 9 were waited for; matrix products, arithmetic and copies ran while one was open for 0% of the time, Pallas kernels for 19%

profile of v6, /device:TPU:19, one launch (start us, length us, event | category | flops | bytes accessed | tf_op | source)
XLA Modules:
  0.0 43.2 jit_solution(176745507409069738)
XLA Ops:
  0.7 1.2 %shard_map.136 = (bf16[112,512]{1,0:T(8,128)(2,1)S(1)}, bf16[64,512]{1,0:T(8,128)(2,1)S(1)}, bf16[128,512]{1,0:T(8,128)(2,1)S(1)}) custom-call(bf16[192,512]{1,0:T(8,128)(2,1)} %bitcast.14, bf16[192,512]{1,0:T(8,128)(2,1)} %bitcast.17, bf16[192,1024]{1,0:T(8,128)(2,1)} %bitcast.9, bf16[128,1024]{1,0:T(8,128)(2,1)} %w.5), custom_call_target="tpu_custom_call" | custom-call | tf_op jit(solution)/shard_map/pallas_call | solution.py:101
  1.8 1.3 %collective-permute-start = (bf16[112,512]{1,0:T(8,128)(2,1)S(1)}, bf16[112,512]{1,0:T(8,128)(2,1)S(1)}, u32[]{:S(2)}, u32[]{:S(2)}) collective-permute-start(bf16[112,512]{1,0:T(8,128)(2,1)S(1)} %get-tuple-element.34), channel_id=1, source_target_pairs={{0,8},{8,16},{16,24},{24,0},{1,9},{9,17},{17,25},{25,1},{2,10},{10... | collective-permute-start | bytes 344072 | tf_op jit(solution)/shard_map/ppermute | solution.py:459
  3.4 2.1 %collective-permute-start.5 = (bf16[128,512]{1,0:T(8,128)(2,1)S(1)}, bf16[128,512]{1,0:T(8,128)(2,1)S(1)}, u32[]{:S(2)}, u32[]{:S(2)}) collective-permute-start(bf16[128,512]{1,0:T(8,128)(2,1)S(1)} %get-tuple-element.41), channel_id=1, source_target_pairs={{0,24},{8,16},{16,8},{24,0},{1,25},{9,17},{17,9},{25,1},{2,26},{10... | collective-permute-start | bytes 393224 | tf_op jit(solution)/shard_map/ppermute | solution.py:443
  6.7 0.8 %shard_map.137 = (bf16[192,1024]{1,0:T(8,128)(2,1)S(1)}, s32[8,128]{1,0:T(8,128)S(1)}) custom-call(bf16[192,1024]{1,0:T(8,128)(2,1)S(1)} %bitcast.10, f32[7,1024]{1,0:T(8,128)S(1)} %copy-done.7, s32[1]{0:T(128)S(6)} %copy.15.lengths, s32[1,2]{1,0:T(1,128)} %offsets.1), custom_call_target="tpu_custom_call" | custom-call | tf_op jit(solution)/shard_map/pallas_call | solution.py:47
  7.5 0.5 %collective-permute-done.1.far = bf16[64,512]{1,0:T(8,128)(2,1)S(1)} collective-permute-done((bf16[64,512]{1,0:T(8,128)(2,1)S(1)}, bf16[64,512]{1,0:T(8,128)(2,1)S(1)}, u32[]{:S(2)}, u32[]{:S(2)}) %collective-permute-start.1) | collective-permute-done | bytes 65568 | tf_op jit(solution)/shard_map/ppermute | solution.py:460
  8.0 1.5 %shard_map.138 = (bf16[192,512]{1,0:T(8,128)(2,1)S(1)}, bf16[592,512]{1,0:T(8,128)(2,1)S(1)}) custom-call(bf16[192,512]{1,0:T(8,128)(2,1)S(1)} %bitcast.23, bf16[192,512]{1,0:T(8,128)(2,1)S(1)} %bitcast.15, bf16[192,512]{1,0:T(8,128)(2,1)S(1)} %bitcast.18, bf16[112,512]{1,0:T(8,128)(2,1)S(1)} %collective-permute-done.near, ...), custom_call_target="tpu_custom_call" | custom-call | flops 4294967296 | tf_op jit(solution)/shard_map/pallas_call | solution.py:47
  9.5 3.1 %collective-permute-start.6 = (bf16[592,512]{1,0:T(8,128)(2,1)S(1)}, bf16[592,512]{1,0:T(8,128)(2,1)S(1)}, u32[]{:S(2)}, u32[]{:S(2)}) collective-permute-start(bf16[592,512]{1,0:T(8,128)(2,1)S(1)} %get-tuple-element.42), channel_id=1, source_target_pairs={{0,1},{1,0},{2,3},{3,2},{4,5},{5,4},{6,7},{7,6},{8,9},{9,8},{10,11... | collective-permute-start | bytes 1818632 | tf_op jit(solution)/shard_map/ppermute | solution.py:456
  12.7 1.0 %shard_map.139 = (bf16[192,1024]{1,0:T(8,128)(2,1)}, bf16[4,64,1024]{2,1,0:T(8,128)(2,1)S(1)}, f32[4,64,1024]{2,1,0:T(8,128)S(1)}) custom-call(bf16[192,512]{1,0:T(8,128)(2,1)S(1)} %get-tuple-element.37.att, bf16[112,512]{1,0:T(8,128)(2,1)S(1)} %collective-permute-done.near, bf16[64,512]{1,0:T(8,128)(2,1)S(1)} %collective-permute-done.1.far, ...), custom_call_target="tpu_custom_call" | custom-call | tf_op jit(solution)/shard_map/pallas_call | solution.py:47
  14.0 0.4 collective-permute-done.6.other
  14.3 0.9 %shard_map.141.conv = f32[8,512]{1,0:T(8,128)S(1)} custom-call(bf16[192,512]{1,0:T(8,128)(2,1)S(1)} %get-tuple-element.37.att, bf16[512,512]{1,0:T(8,128)(2,1)S(1)} %shard_map.140.wx, bf16[192,1024]{1,0:T(8,128)(2,1)S(1)} %bitcast.21, bf16[192,1024]{1,0:T(8,128)(2,1)S(1)} %bitcast.13, bf16[112,512]{1,0:T(8,128)(2,1)S(1)} %collective-permute-done.near, ...), custom_call_target="tpu_custom_call" | custom-call | tf_op jit(solution)/shard_map/pallas_call | solution.py:47
  15.7 0.5 %collective-permute-start.7 = (bf16[3,128,512]{2,1,0:T(8,128)(2,1)S(1)}, bf16[3,128,512]{2,1,0:T(8,128)(2,1)S(1)}, u32[]{:S(2)}, u32[]{:S(2)}) collective-permute-start(bf16[3,128,512]{2,1,0:T(8,128)(2,1)S(1)} %shard_map.143), channel_id=1, source_target_pairs={{0,1},{1,0},{2,3},{3,2},{4,5},{5,4},{6,7},{7,6},{8,9},{9,8},{10,11... | collective-permute-start | bytes 1179656 | tf_op jit(solution)/shard_map/ppermute | solution.py:456
  16.2 0.8 %collective-permute-start.8 = (bf16[16,4352]{1,0:T(8,128)(2,1)S(1)}, bf16[16,4352]{1,0:T(8,128)(2,1)S(1)}, u32[]{:S(2)}, u32[]{:S(2)}) collective-permute-start(bf16[16,4352]{1,0:T(8,128)(2,1)S(1)} %get-tuple-element.51), channel_id=1, source_target_pairs={{0,8},{8,0},{16,24},{24,16},{1,9},{9,1},{17,25},{25,17},{2,10},{10... | collective-permute-start | bytes 417800 | tf_op jit(solution)/shard_map/ppermute | solution.py:443
  17.1 1.7 %collective-permute-start.10 = (bf16[16,4352]{1,0:T(8,128)(2,1)S(1)}, bf16[16,4352]{1,0:T(8,128)(2,1)S(1)}, u32[]{:S(2)}, u32[]{:S(2)}) collective-permute-start(bf16[16,4352]{1,0:T(8,128)(2,1)S(1)} %get-tuple-element.53), channel_id=1, source_target_pairs={{0,24},{8,16},{16,8},{24,0},{1,25},{9,17},{17,9},{25,1},{2,26},{10... | collective-permute-start | bytes 417800 | tf_op jit(solution)/shard_map/ppermute | solution.py:443
  18.8 3.2 %shard_map.144 = (bf16[192,512]{1,0:T(8,128)(2,1)}, f32[192,512]{1,0:T(8,128)S(1)}, f32[192,512]{1,0:T(8,128)S(1)}, bf16[96,512]{1,0:T(8,128)(2,1)S(1)}, bf16[48...) custom-call(f32[16,4352]{1,0:T(8,128)S(1)} %get-tuple-element.43.after.refs_0_, bf16[192,512]{1,0:T(8,128)(2,1)S(1)} %bitcast.24, ...), custom_call_target="tpu_custom_call" | custom-call | bytes 10485760 | tf_op jit(solution)/shard_map/pallas_call | solution.py:47
  22.0 3.0 %collective-permute-done.10.refs_3_ = bf16[16,4352]{1,0:T(8,128)(2,1)S(1)} collective-permute-done((bf16[16,4352]{1,0:T(8,128)(2,1)S(1)}, bf16[16,4352]{1,0:T(8,128)(2,1)S(1)}, u32[]{:S(2)}, u32[]{:S(2)}) %collective-permute-start.10) | collective-permute-done | bytes 139296 | tf_op jit(solution)/shard_map/ppermute | solution.py:443
  25.2 1.3 %collective-permute-start.14 = (bf16[16,4352]{1,0:T(8,128)(2,1)S(1)}, bf16[16,4352]{1,0:T(8,128)(2,1)S(1)}, u32[]{:S(2)}, u32[]{:S(2)}) collective-permute-start(bf16[16,4352]{1,0:T(8,128)(2,1)S(1)} %get-tuple-element.59.refs_0_), channel_id=1, source_target_pairs={{0,2},{1,3},{2,0},{3,1},{4,6},{5,7},{6,4},{7,5},{8,10},{9,11},{10,... | collective-permute-start | bytes 417800 | tf_op jit(solution)/shard_map/ppermute | solution.py:450
  26.5 1.3 %collective-permute-start.13 = (bf16[16,4352]{1,0:T(8,128)(2,1)S(1)}, bf16[16,4352]{1,0:T(8,128)(2,1)S(1)}, u32[]{:S(2)}, u32[]{:S(2)}) collective-permute-start(bf16[16,4352]{1,0:T(8,128)(2,1)S(1)} %get-tuple-element.59.refs_0_), channel_id=1, source_target_pairs={{0,6},{1,7},{2,4},{3,5},{4,2},{5,3},{6,0},{7,1},{8,14},{9,15},{10,... | collective-permute-start | bytes 417800 | tf_op jit(solution)/shard_map/ppermute | solution.py:450
  27.8 2.4 %collective-permute-start.12 = (bf16[48,512]{1,0:T(8,128)(2,1)S(1)}, bf16[48,512]{1,0:T(8,128)(2,1)S(1)}, u32[]{:S(2)}, u32[]{:S(2)}) collective-permute-start(bf16[48,512]{1,0:T(8,128)(2,1)S(1)} %get-tuple-element.55), channel_id=1, source_target_pairs={{0,8},{8,16},{16,24},{24,0},{1,9},{9,17},{17,25},{25,1},{2,10},{10... | collective-permute-start | bytes 147464 | tf_op jit(solution)/shard_map/ppermute | solution.py:555
  30.1 2.1 %collective-permute-done.12.first = bf16[48,512]{1,0:T(8,128)(2,1)S(1)} collective-permute-done((bf16[48,512]{1,0:T(8,128)(2,1)S(1)}, bf16[48,512]{1,0:T(8,128)(2,1)S(1)}, u32[]{:S(2)}, u32[]{:S(2)}) %collective-permute-start.12) | collective-permute-done | bytes 49184 | tf_op jit(solution)/shard_map/ppermute | solution.py:555
  32.4 0.8 %shard_map.146 = (bf16[192,512]{1,0:T(8,128)(2,1)}, bf16[192,512]{1,0:T(8,128)(2,1)}, f32[8,128]{1,0:T(8,128)S(1)}) custom-call(f32[192,512]{1,0:T(8,128)S(1)} %get-tuple-element.46.key_g, f32[192,512]{1,0:T(8,128)S(1)} %get-tuple-element.47.value_g, bf16[96,512]{1,0:T(8,128)(2,1)S(1)} %collective-permute-done.11.last, ...), custom_call_target="tpu_custom_call" | custom-call | tf_op jit(solution)/shard_map/pallas_call | solution.py:47
  33.2 7.3 %collective-permute-done.13.refs_1_ = bf16[16,4352]{1,0:T(8,128)(2,1)S(1)} collective-permute-done((bf16[16,4352]{1,0:T(8,128)(2,1)S(1)}, bf16[16,4352]{1,0:T(8,128)(2,1)S(1)}, u32[]{:S(2)}, u32[]{:S(2)}) %collective-permute-start.13) | collective-permute-done | bytes 139296 | tf_op jit(solution)/shard_map/ppermute | solution.py:450
  40.6 0.6 %collective-permute-start.16 = (f32[16,4352]{1,0:T(8,128)S(1)}, f32[16,4352]{1,0:T(8,128)S(1)}, u32[]{:S(2)}, u32[]{:S(2)}) collective-permute-start(f32[16,4352]{1,0:T(8,128)S(1)} %shard_map.147.mine), channel_id=1, source_target_pairs={{0,1},{1,0},{2,3},{3,2},{4,5},{5,4},{6,7},{7,6},{8,9},{9,8},{10,11... | collective-permute-start | bytes 835592 | tf_op jit(solution)/shard_map/ppermute | solution.py:456
  41.2 1.2 %collective-permute-done.16.theirs = f32[16,4352]{1,0:T(8,128)S(1)} collective-permute-done((f32[16,4352]{1,0:T(8,128)S(1)}, f32[16,4352]{1,0:T(8,128)S(1)}, u32[]{:S(2)}, u32[]{:S(2)}) %collective-permute-start.16) | collective-permute-done | bytes 278560 | tf_op jit(solution)/shard_map/ppermute | solution.py:456
  42.4 0.8 %shard_map.148 = (f32[128,1024]{1,0:T(8,128)}, f32[7,1024]{1,0:T(8,128)}) custom-call(f32[8,128]{1,0:T(8,128)S(1)} %get-tuple-element.58.after, f32[16,4352]{1,0:T(8,128)S(1)} %shard_map.147.mine, f32[16,4352]{1,0:T(8,128)S(1)} %collective-permute-done.16.theirs), custom_call_target="tpu_custom_call" | custom-call | tf_op jit(solution)/shard_map/pallas_call | solution.py:47
  (39 shorter events, 2.2 us)
Async XLA Ops:
  0.6 6.0 %copy-start = (bf16[1,192,1024]{2,1,0:T(8,128)(2,1)S(1)}, bf16[1,192,1024]{2,1,0:T(8,128)(2,1)}, u32[]{:S(2)}) copy-start(bf16[1,192,1024]{2,1,0:T(8,128)(2,1)} %param.13) | copy-start | bytes 1179652
  0.6 6.0 %copy-start.7 = (f32[7,1024]{1,0:T(8,128)S(1)}, f32[7,1024]{1,0:T(8,128)}, u32[]{:S(2)}) copy-start(f32[7,1024]{1,0:T(8,128)} %taps.3) | copy-start | bytes 86020
  0.7 7.3 %copy-start.4 = (bf16[1,192,1024]{2,1,0:T(8,128)(2,1)S(1)}, bf16[1,192,1024]{2,1,0:T(8,128)(2,1)}, u32[]{:S(2)}) copy-start(bf16[1,192,1024]{2,1,0:T(8,128)(2,1)} %param.12) | copy-start | bytes 1179652
  0.7 7.3 %copy-start.6 = (bf16[1,192,512]{2,1,0:T(8,128)(2,1)S(1)}, bf16[1,192,512]{2,1,0:T(8,128)(2,1)}, u32[]{:S(2)}) copy-start(bf16[1,192,512]{2,1,0:T(8,128)(2,1)} %param.9) | copy-start | bytes 589828
  1.8 6.1 %collective-permute-start = (bf16[112,512]{1,0:T(8,128)(2,1)S(1)}, bf16[112,512]{1,0:T(8,128)(2,1)S(1)}, u32[]{:S(2)}, u32[]{:S(2)}) collective-permute-start(bf16[112,512]{1,0:T(8,128)(2,1)S(1)} %get-tuple-element.34), channel_id=1, source_target_pairs={{0,8},{8,16},{16,24},{24,0},{1,9},{9,17},{17,25},{25,1},{2,10},{10... | collective-permute-start | bytes 344072 | tf_op jit(solution)/shard_map/ppermute | solution.py:459
  3.1 4.9 %collective-permute-start.1 = (bf16[64,512]{1,0:T(8,128)(2,1)S(1)}, bf16[64,512]{1,0:T(8,128)(2,1)S(1)}, u32[]{:S(2)}, u32[]{:S(2)}) collective-permute-start(bf16[64,512]{1,0:T(8,128)(2,1)S(1)} %get-tuple-element.35), channel_id=1, source_target_pairs={{0,24},{8,0},{16,8},{24,16},{1,25},{9,1},{17,9},{25,17},{2,26},{10... | collective-permute-start | bytes 196616 | tf_op jit(solution)/shard_map/ppermute | solution.py:460
  3.4 10.3 %collective-permute-start.5 = (bf16[128,512]{1,0:T(8,128)(2,1)S(1)}, bf16[128,512]{1,0:T(8,128)(2,1)S(1)}, u32[]{:S(2)}, u32[]{:S(2)}) collective-permute-start(bf16[128,512]{1,0:T(8,128)(2,1)S(1)} %get-tuple-element.41), channel_id=1, source_target_pairs={{0,24},{8,16},{16,8},{24,0},{1,25},{9,17},{17,9},{25,1},{2,26},{10... | collective-permute-start | bytes 393224 | tf_op jit(solution)/shard_map/ppermute | solution.py:443
  5.5 8.4 %collective-permute-start.4 = (bf16[128,512]{1,0:T(8,128)(2,1)S(1)}, bf16[128,512]{1,0:T(8,128)(2,1)S(1)}, u32[]{:S(2)}, u32[]{:S(2)}) collective-permute-start(bf16[128,512]{1,0:T(8,128)(2,1)S(1)} %get-tuple-element.41), channel_id=1, source_target_pairs={{0,16},{8,24},{16,0},{24,8},{1,17},{9,25},{17,1},{25,9},{2,18},{10... | collective-permute-start | bytes 393224 | tf_op jit(solution)/shard_map/ppermute | solution.py:443
  5.7 8.2 %collective-permute-start.3 = (bf16[128,512]{1,0:T(8,128)(2,1)S(1)}, bf16[128,512]{1,0:T(8,128)(2,1)S(1)}, u32[]{:S(2)}, u32[]{:S(2)}) collective-permute-start(bf16[128,512]{1,0:T(8,128)(2,1)S(1)} %get-tuple-element.41), channel_id=1, source_target_pairs={{0,8},{8,0},{16,24},{24,16},{1,9},{9,1},{17,25},{25,17},{2,10},{10... | collective-permute-start | bytes 393224 | tf_op jit(solution)/shard_map/ppermute | solution.py:443
  6.7 1.3 %copy-start.2 = (bf16[1,192,512]{2,1,0:T(8,128)(2,1)S(1)}, bf16[1,192,512]{2,1,0:T(8,128)(2,1)}, u32[]{:S(2)}) copy-start(bf16[1,192,512]{2,1,0:T(8,128)(2,1)} %param.10) | copy-start | bytes 589828
  6.7 1.3 %copy-start.3 = (bf16[1,192,512]{2,1,0:T(8,128)(2,1)S(1)}, bf16[1,192,512]{2,1,0:T(8,128)(2,1)}, u32[]{:S(2)}) copy-start(bf16[1,192,512]{2,1,0:T(8,128)(2,1)} %param.11) | copy-start | bytes 589828
  9.5 4.8 %collective-permute-start.6 = (bf16[592,512]{1,0:T(8,128)(2,1)S(1)}, bf16[592,512]{1,0:T(8,128)(2,1)S(1)}, u32[]{:S(2)}, u32[]{:S(2)}) collective-permute-start(bf16[592,512]{1,0:T(8,128)(2,1)S(1)} %get-tuple-element.42), channel_id=1, source_target_pairs={{0,1},{1,0},{2,3},{3,2},{4,5},{5,4},{6,7},{7,6},{8,9},{9,8},{10,11... | collective-permute-start | bytes 1818632 | tf_op jit(solution)/shard_map/ppermute | solution.py:456
  13.7 1.9 %collective-permute-start.2 = (bf16[4,64,1024]{2,1,0:T(8,128)(2,1)S(1)}, bf16[4,64,1024]{2,1,0:T(8,128)(2,1)S(1)}, u32[]{:S(2)}, u32[]{:S(2)}) collective-permute-start(bf16[4,64,1024]{2,1,0:T(8,128)(2,1)S(1)} %get-tuple-element.40.after), channel_id=1, source_target_pairs={{0,1},{1,0},{2,3},{3,2},{4,5},{5,4},{6,7},{7,6},{8,9},{9,8},{10,11... | collective-permute-start | bytes 1572872 | tf_op jit(solution)/shard_map/ppermute | solution.py:456
  15.7 3.2 %copy-start.5 = (bf16[192,1024]{1,0:T(8,128)(2,1)S(1)}, bf16[192,1024]{1,0:T(8,128)(2,1)}, u32[]{:S(2)}) copy-start(bf16[192,1024]{1,0:T(8,128)(2,1)} %get-tuple-element.44.stream_grad) | copy-start | bytes 1179652
  15.7 3.1 %collective-permute-start.7 = (bf16[3,128,512]{2,1,0:T(8,128)(2,1)S(1)}, bf16[3,128,512]{2,1,0:T(8,128)(2,1)S(1)}, u32[]{:S(2)}, u32[]{:S(2)}) collective-permute-start(bf16[3,128,512]{2,1,0:T(8,128)(2,1)S(1)} %shard_map.143), channel_id=1, source_target_pairs={{0,1},{1,0},{2,3},{3,2},{4,5},{5,4},{6,7},{7,6},{8,9},{9,8},{10,11... | collective-permute-start | bytes 1179656 | tf_op jit(solution)/shard_map/ppermute | solution.py:456
  16.2 5.8 %collective-permute-start.8 = (bf16[16,4352]{1,0:T(8,128)(2,1)S(1)}, bf16[16,4352]{1,0:T(8,128)(2,1)S(1)}, u32[]{:S(2)}, u32[]{:S(2)}) collective-permute-start(bf16[16,4352]{1,0:T(8,128)(2,1)S(1)} %get-tuple-element.51), channel_id=1, source_target_pairs={{0,8},{8,0},{16,24},{24,16},{1,9},{9,1},{17,25},{25,17},{2,10},{10... | collective-permute-start | bytes 417800 | tf_op jit(solution)/shard_map/ppermute | solution.py:443
  16.9 5.1 %collective-permute-start.9 = (bf16[16,4352]{1,0:T(8,128)(2,1)S(1)}, bf16[16,4352]{1,0:T(8,128)(2,1)S(1)}, u32[]{:S(2)}, u32[]{:S(2)}) collective-permute-start(bf16[16,4352]{1,0:T(8,128)(2,1)S(1)} %get-tuple-element.52), channel_id=1, source_target_pairs={{0,16},{8,24},{16,0},{24,8},{1,17},{9,25},{17,1},{25,9},{2,18},{10... | collective-permute-start | bytes 417800 | tf_op jit(solution)/shard_map/ppermute | solution.py:443
  17.1 7.8 %collective-permute-start.10 = (bf16[16,4352]{1,0:T(8,128)(2,1)S(1)}, bf16[16,4352]{1,0:T(8,128)(2,1)S(1)}, u32[]{:S(2)}, u32[]{:S(2)}) collective-permute-start(bf16[16,4352]{1,0:T(8,128)(2,1)S(1)} %get-tuple-element.53), channel_id=1, source_target_pairs={{0,24},{8,16},{16,8},{24,0},{1,25},{9,17},{17,9},{25,1},{2,26},{10... | collective-permute-start | bytes 417800 | tf_op jit(solution)/shard_map/ppermute | solution.py:443
  25.1 8.2 %collective-permute-start.15 = (bf16[16,4352]{1,0:T(8,128)(2,1)S(1)}, bf16[16,4352]{1,0:T(8,128)(2,1)S(1)}, u32[]{:S(2)}, u32[]{:S(2)}) collective-permute-start(bf16[16,4352]{1,0:T(8,128)(2,1)S(1)} %get-tuple-element.59.refs_0_), channel_id=1, source_target_pairs={{0,4},{1,5},{2,6},{3,7},{4,0},{5,1},{6,2},{7,3},{8,12},{9,13},{10,... | collective-permute-start | bytes 417800 | tf_op jit(solution)/shard_map/ppermute | solution.py:450
  25.2 8.0 %collective-permute-start.14 = (bf16[16,4352]{1,0:T(8,128)(2,1)S(1)}, bf16[16,4352]{1,0:T(8,128)(2,1)S(1)}, u32[]{:S(2)}, u32[]{:S(2)}) collective-permute-start(bf16[16,4352]{1,0:T(8,128)(2,1)S(1)} %get-tuple-element.59.refs_0_), channel_id=1, source_target_pairs={{0,2},{1,3},{2,0},{3,1},{4,6},{5,7},{6,4},{7,5},{8,10},{9,11},{10,... | collective-permute-start | bytes 417800 | tf_op jit(solution)/shard_map/ppermute | solution.py:450
  26.5 14.1 %collective-permute-start.13 = (bf16[16,4352]{1,0:T(8,128)(2,1)S(1)}, bf16[16,4352]{1,0:T(8,128)(2,1)S(1)}, u32[]{:S(2)}, u32[]{:S(2)}) collective-permute-start(bf16[16,4352]{1,0:T(8,128)(2,1)S(1)} %get-tuple-element.59.refs_0_), channel_id=1, source_target_pairs={{0,6},{1,7},{2,4},{3,5},{4,2},{5,3},{6,0},{7,1},{8,14},{9,15},{10,... | collective-permute-start | bytes 417800 | tf_op jit(solution)/shard_map/ppermute | solution.py:450
  27.8 4.7 %collective-permute-start.11 = (bf16[96,512]{1,0:T(8,128)(2,1)S(1)}, bf16[96,512]{1,0:T(8,128)(2,1)S(1)}, u32[]{:S(2)}, u32[]{:S(2)}) collective-permute-start(bf16[96,512]{1,0:T(8,128)(2,1)S(1)} %get-tuple-element.54), channel_id=1, source_target_pairs={{0,24},{8,0},{16,8},{24,16},{1,25},{9,1},{17,9},{25,17},{2,26},{10... | collective-permute-start | bytes 294920 | tf_op jit(solution)/shard_map/ppermute | solution.py:554
  27.8 4.5 %collective-permute-start.12 = (bf16[48,512]{1,0:T(8,128)(2,1)S(1)}, bf16[48,512]{1,0:T(8,128)(2,1)S(1)}, u32[]{:S(2)}, u32[]{:S(2)}) collective-permute-start(bf16[48,512]{1,0:T(8,128)(2,1)S(1)} %get-tuple-element.55), channel_id=1, source_target_pairs={{0,8},{8,16},{16,24},{24,0},{1,9},{9,17},{17,25},{25,1},{2,10},{10... | collective-permute-start | bytes 147464 | tf_op jit(solution)/shard_map/ppermute | solution.py:555
  40.6 1.7 %collective-permute-start.16 = (f32[16,4352]{1,0:T(8,128)S(1)}, f32[16,4352]{1,0:T(8,128)S(1)}, u32[]{:S(2)}, u32[]{:S(2)}) collective-permute-start(f32[16,4352]{1,0:T(8,128)S(1)} %shard_map.147.mine), channel_id=1, source_target_pairs={{0,1},{1,0},{2,3},{3,2},{4,5},{5,4},{6,7},{7,6},{8,9},{9,8},{10,11... | collective-permute-start | bytes 835592 | tf_op jit(solution)/shard_map/ppermute | solution.py:456
  (1 other events, 1.2 us)

commit v7 on v6

--- a/solution.py
+++ b/solution.py
@@ -298,12 +298,8 @@
     return terms[0]
 
 
-def cp_sum_kernel(after, back, onward, *refs):
-    got = refs[:-3]
-    part, back_out, onward_out = refs[-3:]
-    part[...] = tree_sum([ref[...].astype(F32) for ref in got]).astype(BF)
-    back_out[...] = back[...]
-    onward_out[...] = onward[...]
+def cp_sum_kernel(after, *refs):
+    refs[-1][...] = tree_sum([ref[...].astype(F32) for ref in refs[:-1]]).astype(BF)
 
 
 def z_sum_kernel(after, *refs):
@@ -545,11 +541,11 @@
         + [pltpu.VMEM((rows, feats), BF), pltpu.VMEM((feats, width), BF)],
         moved=10 * 2**20,
     )
-    part, back, onward = call(
+    part = call(
         cp_sum_kernel,
-        (shape((16, wide), BF), shape(back.shape, BF), shape(onward.shape, BF)),
-        [VMEM] * (cps + 3),
-        (bwd_done, back, onward, own, *ordered(cp_got, CP_ORDER)),
+        shape((16, wide), BF),
+        [VMEM] * (cps + 1),
+        (bwd_done, own, *ordered(cp_got, CP_ORDER)),
     )
     last = lax.ppermute(back, "cp", downward)
     first = lax.ppermute(onward, "cp", upward)

time: 43.4 us -> 43.4 us (level)
  no operation moved by 1% of the time
where the time goes in v7:
time: 43.4 us; the launch traced here: 43.2 us
  starting transfers between devices  16.1 us (37%)
  waiting for transfers between devices  15.1 us (35%)
  Pallas kernels  10.5 us (24%)
  between operations  1.45 us (3%)
    pallas_call x12, Pallas kernels, call(): pl.pallas_call(kernel, out_shape=outs, in_specs=ins, out_specs=jax.tree.m...  9.35 us
    ppermute x3, waiting for transfers between devices, over_z(): lax.ppermute(array, 'dp', [(i, i ^ 2 * by) for i in range(dps)])  7.34 us
    ppermute x6, starting transfers between devices, over_cp(): lax.ppermute(arrays[by - 1], 'cp', [(i, i ^ by) for i in range(cps)])  5.33 us
    ppermute x4, starting transfers between devices, over_core(): return lax.ppermute(array, 'dp', [(i, i ^ 1) for i in range(dps)])  4.2 us
    ppermute x6, waiting for transfers between devices, over_cp(): lax.ppermute(arrays[by - 1], 'cp', [(i, i ^ by) for i in range(cps)])  3.15 us
    ppermute x3, starting transfers between devices, over_z(): lax.ppermute(array, 'dp', [(i, i ^ 2 * by) for i in range(dps)])  2.71 us
    ppermute x1, starting transfers between devices, body(): first = lax.ppermute(onward, 'cp', upward)  2.36 us
    ppermute x1, waiting for transfers between devices, body(): first = lax.ppermute(onward, 'cp', upward)  2.24 us
  transfers between devices with their start and end apart: 17, of which 9 were waited for; matrix products, arithmetic and copies ran while one was open for 0% of the time, Pallas kernels for 19%

profile of v7, /device:TPU:19, one launch (start us, length us, event | category | flops | bytes accessed | tf_op | source)
XLA Modules:
  0.0 43.2 jit_solution(7180449037392943550)
XLA Ops:
  0.7 1.2 %shard_map.136 = (bf16[112,512]{1,0:T(8,128)(2,1)S(1)}, bf16[64,512]{1,0:T(8,128)(2,1)S(1)}, bf16[128,512]{1,0:T(8,128)(2,1)S(1)}) custom-call(bf16[192,512]{1,0:T(8,128)(2,1)} %bitcast.14, bf16[192,512]{1,0:T(8,128)(2,1)} %bitcast.17, bf16[192,1024]{1,0:T(8,128)(2,1)} %bitcast.9, bf16[128,1024]{1,0:T(8,128)(2,1)} %w.5), custom_call_target="tpu_custom_call" | custom-call | tf_op jit(solution)/shard_map/pallas_call | solution.py:101
  1.8 1.3 %collective-permute-start = (bf16[112,512]{1,0:T(8,128)(2,1)S(1)}, bf16[112,512]{1,0:T(8,128)(2,1)S(1)}, u32[]{:S(2)}, u32[]{:S(2)}) collective-permute-start(bf16[112,512]{1,0:T(8,128)(2,1)S(1)} %get-tuple-element.31), channel_id=1, source_target_pairs={{0,8},{8,16},{16,24},{24,0},{1,9},{9,17},{17,25},{25,1},{2,10},{10... | collective-permute-start | bytes 344072 | tf_op jit(solution)/shard_map/ppermute | solution.py:455
  3.4 2.1 %collective-permute-start.5 = (bf16[128,512]{1,0:T(8,128)(2,1)S(1)}, bf16[128,512]{1,0:T(8,128)(2,1)S(1)}, u32[]{:S(2)}, u32[]{:S(2)}) collective-permute-start(bf16[128,512]{1,0:T(8,128)(2,1)S(1)} %get-tuple-element.38), channel_id=1, source_target_pairs={{0,24},{8,16},{16,8},{24,0},{1,25},{9,17},{17,9},{25,1},{2,26},{10... | collective-permute-start | bytes 393224 | tf_op jit(solution)/shard_map/ppermute | solution.py:439
  6.7 0.8 %shard_map.137 = (bf16[192,1024]{1,0:T(8,128)(2,1)S(1)}, s32[8,128]{1,0:T(8,128)S(1)}) custom-call(bf16[192,1024]{1,0:T(8,128)(2,1)S(1)} %bitcast.10, f32[7,1024]{1,0:T(8,128)S(1)} %copy-done.7, s32[1]{0:T(128)S(6)} %copy.15.lengths, s32[1,2]{1,0:T(1,128)} %offsets.1), custom_call_target="tpu_custom_call" | custom-call | tf_op jit(solution)/shard_map/pallas_call | solution.py:47
  7.5 0.5 %collective-permute-done.1.far = bf16[64,512]{1,0:T(8,128)(2,1)S(1)} collective-permute-done((bf16[64,512]{1,0:T(8,128)(2,1)S(1)}, bf16[64,512]{1,0:T(8,128)(2,1)S(1)}, u32[]{:S(2)}, u32[]{:S(2)}) %collective-permute-start.1) | collective-permute-done | bytes 65568 | tf_op jit(solution)/shard_map/ppermute | solution.py:456
  8.0 1.5 %shard_map.138 = (bf16[192,512]{1,0:T(8,128)(2,1)S(1)}, bf16[592,512]{1,0:T(8,128)(2,1)S(1)}) custom-call(bf16[192,512]{1,0:T(8,128)(2,1)S(1)} %bitcast.23, bf16[192,512]{1,0:T(8,128)(2,1)S(1)} %bitcast.15, bf16[192,512]{1,0:T(8,128)(2,1)S(1)} %bitcast.18, bf16[112,512]{1,0:T(8,128)(2,1)S(1)} %collective-permute-done.near, ...), custom_call_target="tpu_custom_call" | custom-call | flops 4294967296 | tf_op jit(solution)/shard_map/pallas_call | solution.py:47
  9.5 3.1 %collective-permute-start.6 = (bf16[592,512]{1,0:T(8,128)(2,1)S(1)}, bf16[592,512]{1,0:T(8,128)(2,1)S(1)}, u32[]{:S(2)}, u32[]{:S(2)}) collective-permute-start(bf16[592,512]{1,0:T(8,128)(2,1)S(1)} %get-tuple-element.39), channel_id=1, source_target_pairs={{0,1},{1,0},{2,3},{3,2},{4,5},{5,4},{6,7},{7,6},{8,9},{9,8},{10,11... | collective-permute-start | bytes 1818632 | tf_op jit(solution)/shard_map/ppermute | solution.py:452
  12.7 1.0 %shard_map.139 = (bf16[192,1024]{1,0:T(8,128)(2,1)}, bf16[4,64,1024]{2,1,0:T(8,128)(2,1)S(1)}, f32[4,64,1024]{2,1,0:T(8,128)S(1)}) custom-call(bf16[192,512]{1,0:T(8,128)(2,1)S(1)} %get-tuple-element.34.att, bf16[112,512]{1,0:T(8,128)(2,1)S(1)} %collective-permute-done.near, bf16[64,512]{1,0:T(8,128)(2,1)S(1)} %collective-permute-done.1.far, ...), custom_call_target="tpu_custom_call" | custom-call | tf_op jit(solution)/shard_map/pallas_call | solution.py:47
  14.0 0.4 collective-permute-done.6.other
  14.3 0.9 %shard_map.141.conv = f32[8,512]{1,0:T(8,128)S(1)} custom-call(bf16[192,512]{1,0:T(8,128)(2,1)S(1)} %get-tuple-element.34.att, bf16[512,512]{1,0:T(8,128)(2,1)S(1)} %shard_map.140.wx, bf16[192,1024]{1,0:T(8,128)(2,1)S(1)} %bitcast.21, bf16[192,1024]{1,0:T(8,128)(2,1)S(1)} %bitcast.13, bf16[112,512]{1,0:T(8,128)(2,1)S(1)} %collective-permute-done.near, ...), custom_call_target="tpu_custom_call" | custom-call | tf_op jit(solution)/shard_map/pallas_call | solution.py:47
  15.7 0.5 %collective-permute-start.7 = (bf16[3,128,512]{2,1,0:T(8,128)(2,1)S(1)}, bf16[3,128,512]{2,1,0:T(8,128)(2,1)S(1)}, u32[]{:S(2)}, u32[]{:S(2)}) collective-permute-start(bf16[3,128,512]{2,1,0:T(8,128)(2,1)S(1)} %shard_map.143), channel_id=1, source_target_pairs={{0,1},{1,0},{2,3},{3,2},{4,5},{5,4},{6,7},{7,6},{8,9},{9,8},{10,11... | collective-permute-start | bytes 1179656 | tf_op jit(solution)/shard_map/ppermute | solution.py:452
  16.2 0.8 %collective-permute-start.10 = (bf16[16,4352]{1,0:T(8,128)(2,1)S(1)}, bf16[16,4352]{1,0:T(8,128)(2,1)S(1)}, u32[]{:S(2)}, u32[]{:S(2)}) collective-permute-start(bf16[16,4352]{1,0:T(8,128)(2,1)S(1)} %get-tuple-element.51), channel_id=1, source_target_pairs={{0,8},{8,0},{16,24},{24,16},{1,9},{9,1},{17,25},{25,17},{2,10},{10... | collective-permute-start | bytes 417800 | tf_op jit(solution)/shard_map/ppermute | solution.py:439
  17.2 1.7 %collective-permute-start.12 = (bf16[16,4352]{1,0:T(8,128)(2,1)S(1)}, bf16[16,4352]{1,0:T(8,128)(2,1)S(1)}, u32[]{:S(2)}, u32[]{:S(2)}) collective-permute-start(bf16[16,4352]{1,0:T(8,128)(2,1)S(1)} %get-tuple-element.53), channel_id=1, source_target_pairs={{0,24},{8,16},{16,8},{24,0},{1,25},{9,17},{17,9},{25,1},{2,26},{10... | collective-permute-start | bytes 417800 | tf_op jit(solution)/shard_map/ppermute | solution.py:439
  18.9 3.2 %shard_map.144 = (bf16[192,512]{1,0:T(8,128)(2,1)}, f32[192,512]{1,0:T(8,128)S(1)}, f32[192,512]{1,0:T(8,128)S(1)}, bf16[96,512]{1,0:T(8,128)(2,1)S(1)}, bf16[48...) custom-call(f32[16,4352]{1,0:T(8,128)S(1)} %get-tuple-element.40.after.refs_0_, bf16[192,512]{1,0:T(8,128)(2,1)S(1)} %bitcast.24, ...), custom_call_target="tpu_custom_call" | custom-call | bytes 10485760 | tf_op jit(solution)/shard_map/pallas_call | solution.py:47
  22.1 2.9 %collective-permute-done.12.refs_3_ = bf16[16,4352]{1,0:T(8,128)(2,1)S(1)} collective-permute-done((bf16[16,4352]{1,0:T(8,128)(2,1)S(1)}, bf16[16,4352]{1,0:T(8,128)(2,1)S(1)}, u32[]{:S(2)}, u32[]{:S(2)}) %collective-permute-start.12) | collective-permute-done | bytes 139296 | tf_op jit(solution)/shard_map/ppermute | solution.py:439
  25.2 1.3 %collective-permute-start.14 = (bf16[16,4352]{1,0:T(8,128)(2,1)S(1)}, bf16[16,4352]{1,0:T(8,128)(2,1)S(1)}, u32[]{:S(2)}, u32[]{:S(2)}) collective-permute-start(bf16[16,4352]{1,0:T(8,128)(2,1)S(1)} %shard_map.146.refs_0_), channel_id=1, source_target_pairs={{0,2},{1,3},{2,0},{3,1},{4,6},{5,7},{6,4},{7,5},{8,10},{9,11},{10,... | collective-permute-start | bytes 417800 | tf_op jit(solution)/shard_map/ppermute | solution.py:446
  26.5 1.3 %collective-permute-start.13 = (bf16[16,4352]{1,0:T(8,128)(2,1)S(1)}, bf16[16,4352]{1,0:T(8,128)(2,1)S(1)}, u32[]{:S(2)}, u32[]{:S(2)}) collective-permute-start(bf16[16,4352]{1,0:T(8,128)(2,1)S(1)} %shard_map.146.refs_0_), channel_id=1, source_target_pairs={{0,6},{1,7},{2,4},{3,5},{4,2},{5,3},{6,0},{7,1},{8,14},{9,15},{10,... | collective-permute-start | bytes 417800 | tf_op jit(solution)/shard_map/ppermute | solution.py:446
  27.8 2.4 %collective-permute-start.9 = (bf16[48,512]{1,0:T(8,128)(2,1)S(1)}, bf16[48,512]{1,0:T(8,128)(2,1)S(1)}, u32[]{:S(2)}, u32[]{:S(2)}) collective-permute-start(bf16[48,512]{1,0:T(8,128)(2,1)S(1)} %get-tuple-element.46), channel_id=1, source_target_pairs={{0,8},{8,16},{16,24},{24,0},{1,9},{9,17},{17,25},{25,1},{2,10},{10... | collective-permute-start | bytes 147464 | tf_op jit(solution)/shard_map/ppermute | solution.py:551
  30.2 2.2 %collective-permute-done.9.first = bf16[48,512]{1,0:T(8,128)(2,1)S(1)} collective-permute-done((bf16[48,512]{1,0:T(8,128)(2,1)S(1)}, bf16[48,512]{1,0:T(8,128)(2,1)S(1)}, u32[]{:S(2)}, u32[]{:S(2)}) %collective-permute-start.9) | collective-permute-done | bytes 49184 | tf_op jit(solution)/shard_map/ppermute | solution.py:551
  32.5 0.8 %shard_map.145 = (bf16[192,512]{1,0:T(8,128)(2,1)}, bf16[192,512]{1,0:T(8,128)(2,1)}, f32[8,128]{1,0:T(8,128)S(1)}) custom-call(f32[192,512]{1,0:T(8,128)S(1)} %get-tuple-element.43.key_g, f32[192,512]{1,0:T(8,128)S(1)} %get-tuple-element.44.value_g, bf16[96,512]{1,0:T(8,128)(2,1)S(1)} %collective-permute-done.8.last, ...), custom_call_target="tpu_custom_call" | custom-call | tf_op jit(solution)/shard_map/pallas_call | solution.py:47
  33.3 7.3 %collective-permute-done.13.refs_1_ = bf16[16,4352]{1,0:T(8,128)(2,1)S(1)} collective-permute-done((bf16[16,4352]{1,0:T(8,128)(2,1)S(1)}, bf16[16,4352]{1,0:T(8,128)(2,1)S(1)}, u32[]{:S(2)}, u32[]{:S(2)}) %collective-permute-start.13) | collective-permute-done | bytes 139296 | tf_op jit(solution)/shard_map/ppermute | solution.py:446
  40.7 0.6 %collective-permute-start.16 = (f32[16,4352]{1,0:T(8,128)S(1)}, f32[16,4352]{1,0:T(8,128)S(1)}, u32[]{:S(2)}, u32[]{:S(2)}) collective-permute-start(f32[16,4352]{1,0:T(8,128)S(1)} %shard_map.147.mine), channel_id=1, source_target_pairs={{0,1},{1,0},{2,3},{3,2},{4,5},{5,4},{6,7},{7,6},{8,9},{9,8},{10,11... | collective-permute-start | bytes 835592 | tf_op jit(solution)/shard_map/ppermute | solution.py:452
  41.2 1.2 %collective-permute-done.16.theirs = f32[16,4352]{1,0:T(8,128)S(1)} collective-permute-done((f32[16,4352]{1,0:T(8,128)S(1)}, f32[16,4352]{1,0:T(8,128)S(1)}, u32[]{:S(2)}, u32[]{:S(2)}) %collective-permute-start.16) | collective-permute-done | bytes 278560 | tf_op jit(solution)/shard_map/ppermute | solution.py:452
  42.4 0.8 %shard_map.148 = (f32[128,1024]{1,0:T(8,128)}, f32[7,1024]{1,0:T(8,128)}) custom-call(f32[8,128]{1,0:T(8,128)S(1)} %get-tuple-element.49.after, f32[16,4352]{1,0:T(8,128)S(1)} %shard_map.147.mine, f32[16,4352]{1,0:T(8,128)S(1)} %collective-permute-done.16.theirs), custom_call_target="tpu_custom_call" | custom-call | tf_op jit(solution)/shard_map/pallas_call | solution.py:47
  (39 shorter events, 2.1 us)
Async XLA Ops:
  0.6 6.0 %copy-start = (bf16[1,192,1024]{2,1,0:T(8,128)(2,1)S(1)}, bf16[1,192,1024]{2,1,0:T(8,128)(2,1)}, u32[]{:S(2)}) copy-start(bf16[1,192,1024]{2,1,0:T(8,128)(2,1)} %param.13) | copy-start | bytes 1179652
  0.6 6.0 %copy-start.7 = (f32[7,1024]{1,0:T(8,128)S(1)}, f32[7,1024]{1,0:T(8,128)}, u32[]{:S(2)}) copy-start(f32[7,1024]{1,0:T(8,128)} %taps.3) | copy-start | bytes 86020
  0.7 7.3 %copy-start.4 = (bf16[1,192,1024]{2,1,0:T(8,128)(2,1)S(1)}, bf16[1,192,1024]{2,1,0:T(8,128)(2,1)}, u32[]{:S(2)}) copy-start(bf16[1,192,1024]{2,1,0:T(8,128)(2,1)} %param.12) | copy-start | bytes 1179652
  0.7 7.3 %copy-start.6 = (bf16[1,192,512]{2,1,0:T(8,128)(2,1)S(1)}, bf16[1,192,512]{2,1,0:T(8,128)(2,1)}, u32[]{:S(2)}) copy-start(bf16[1,192,512]{2,1,0:T(8,128)(2,1)} %param.9) | copy-start | bytes 589828
  1.8 6.1 %collective-permute-start = (bf16[112,512]{1,0:T(8,128)(2,1)S(1)}, bf16[112,512]{1,0:T(8,128)(2,1)S(1)}, u32[]{:S(2)}, u32[]{:S(2)}) collective-permute-start(bf16[112,512]{1,0:T(8,128)(2,1)S(1)} %get-tuple-element.31), channel_id=1, source_target_pairs={{0,8},{8,16},{16,24},{24,0},{1,9},{9,17},{17,25},{25,1},{2,10},{10... | collective-permute-start | bytes 344072 | tf_op jit(solution)/shard_map/ppermute | solution.py:455
  3.1 4.9 %collective-permute-start.1 = (bf16[64,512]{1,0:T(8,128)(2,1)S(1)}, bf16[64,512]{1,0:T(8,128)(2,1)S(1)}, u32[]{:S(2)}, u32[]{:S(2)}) collective-permute-start(bf16[64,512]{1,0:T(8,128)(2,1)S(1)} %get-tuple-element.32), channel_id=1, source_target_pairs={{0,24},{8,0},{16,8},{24,16},{1,25},{9,1},{17,9},{25,17},{2,26},{10... | collective-permute-start | bytes 196616 | tf_op jit(solution)/shard_map/ppermute | solution.py:456
  3.4 10.3 %collective-permute-start.5 = (bf16[128,512]{1,0:T(8,128)(2,1)S(1)}, bf16[128,512]{1,0:T(8,128)(2,1)S(1)}, u32[]{:S(2)}, u32[]{:S(2)}) collective-permute-start(bf16[128,512]{1,0:T(8,128)(2,1)S(1)} %get-tuple-element.38), channel_id=1, source_target_pairs={{0,24},{8,16},{16,8},{24,0},{1,25},{9,17},{17,9},{25,1},{2,26},{10... | collective-permute-start | bytes 393224 | tf_op jit(solution)/shard_map/ppermute | solution.py:439
  5.5 8.4 %collective-permute-start.4 = (bf16[128,512]{1,0:T(8,128)(2,1)S(1)}, bf16[128,512]{1,0:T(8,128)(2,1)S(1)}, u32[]{:S(2)}, u32[]{:S(2)}) collective-permute-start(bf16[128,512]{1,0:T(8,128)(2,1)S(1)} %get-tuple-element.38), channel_id=1, source_target_pairs={{0,16},{8,24},{16,0},{24,8},{1,17},{9,25},{17,1},{25,9},{2,18},{10... | collective-permute-start | bytes 393224 | tf_op jit(solution)/shard_map/ppermute | solution.py:439
  5.7 8.2 %collective-permute-start.3 = (bf16[128,512]{1,0:T(8,128)(2,1)S(1)}, bf16[128,512]{1,0:T(8,128)(2,1)S(1)}, u32[]{:S(2)}, u32[]{:S(2)}) collective-permute-start(bf16[128,512]{1,0:T(8,128)(2,1)S(1)} %get-tuple-element.38), channel_id=1, source_target_pairs={{0,8},{8,0},{16,24},{24,16},{1,9},{9,1},{17,25},{25,17},{2,10},{10... | collective-permute-start | bytes 393224 | tf_op jit(solution)/shard_map/ppermute | solution.py:439
  6.7 1.3 %copy-start.2 = (bf16[1,192,512]{2,1,0:T(8,128)(2,1)S(1)}, bf16[1,192,512]{2,1,0:T(8,128)(2,1)}, u32[]{:S(2)}) copy-start(bf16[1,192,512]{2,1,0:T(8,128)(2,1)} %param.10) | copy-start | bytes 589828
  6.7 1.3 %copy-start.3 = (bf16[1,192,512]{2,1,0:T(8,128)(2,1)S(1)}, bf16[1,192,512]{2,1,0:T(8,128)(2,1)}, u32[]{:S(2)}) copy-start(bf16[1,192,512]{2,1,0:T(8,128)(2,1)} %param.11) | copy-start | bytes 589828
  9.5 4.8 %collective-permute-start.6 = (bf16[592,512]{1,0:T(8,128)(2,1)S(1)}, bf16[592,512]{1,0:T(8,128)(2,1)S(1)}, u32[]{:S(2)}, u32[]{:S(2)}) collective-permute-start(bf16[592,512]{1,0:T(8,128)(2,1)S(1)} %get-tuple-element.39), channel_id=1, source_target_pairs={{0,1},{1,0},{2,3},{3,2},{4,5},{5,4},{6,7},{7,6},{8,9},{9,8},{10,11... | collective-permute-start | bytes 1818632 | tf_op jit(solution)/shard_map/ppermute | solution.py:452
  13.7 1.9 %collective-permute-start.2 = (bf16[4,64,1024]{2,1,0:T(8,128)(2,1)S(1)}, bf16[4,64,1024]{2,1,0:T(8,128)(2,1)S(1)}, u32[]{:S(2)}, u32[]{:S(2)}) collective-permute-start(bf16[4,64,1024]{2,1,0:T(8,128)(2,1)S(1)} %get-tuple-element.37.after), channel_id=1, source_target_pairs={{0,1},{1,0},{2,3},{3,2},{4,5},{5,4},{6,7},{7,6},{8,9},{9,8},{10,11... | collective-permute-start | bytes 1572872 | tf_op jit(solution)/shard_map/ppermute | solution.py:452
  15.7 3.2 %copy-start.5 = (bf16[192,1024]{1,0:T(8,128)(2,1)S(1)}, bf16[192,1024]{1,0:T(8,128)(2,1)}, u32[]{:S(2)}) copy-start(bf16[192,1024]{1,0:T(8,128)(2,1)} %get-tuple-element.41.stream_grad) | copy-start | bytes 1179652
  15.7 3.1 %collective-permute-start.7 = (bf16[3,128,512]{2,1,0:T(8,128)(2,1)S(1)}, bf16[3,128,512]{2,1,0:T(8,128)(2,1)S(1)}, u32[]{:S(2)}, u32[]{:S(2)}) collective-permute-start(bf16[3,128,512]{2,1,0:T(8,128)(2,1)S(1)} %shard_map.143), channel_id=1, source_target_pairs={{0,1},{1,0},{2,3},{3,2},{4,5},{5,4},{6,7},{7,6},{8,9},{9,8},{10,11... | collective-permute-start | bytes 1179656 | tf_op jit(solution)/shard_map/ppermute | solution.py:452
  16.2 5.9 %collective-permute-start.10 = (bf16[16,4352]{1,0:T(8,128)(2,1)S(1)}, bf16[16,4352]{1,0:T(8,128)(2,1)S(1)}, u32[]{:S(2)}, u32[]{:S(2)}) collective-permute-start(bf16[16,4352]{1,0:T(8,128)(2,1)S(1)} %get-tuple-element.51), channel_id=1, source_target_pairs={{0,8},{8,0},{16,24},{24,16},{1,9},{9,1},{17,25},{25,17},{2,10},{10... | collective-permute-start | bytes 417800 | tf_op jit(solution)/shard_map/ppermute | solution.py:439
  16.9 5.1 %collective-permute-start.11 = (bf16[16,4352]{1,0:T(8,128)(2,1)S(1)}, bf16[16,4352]{1,0:T(8,128)(2,1)S(1)}, u32[]{:S(2)}, u32[]{:S(2)}) collective-permute-start(bf16[16,4352]{1,0:T(8,128)(2,1)S(1)} %get-tuple-element.52), channel_id=1, source_target_pairs={{0,16},{8,24},{16,0},{24,8},{1,17},{9,25},{17,1},{25,9},{2,18},{10... | collective-permute-start | bytes 417800 | tf_op jit(solution)/shard_map/ppermute | solution.py:439
  17.2 7.8 %collective-permute-start.12 = (bf16[16,4352]{1,0:T(8,128)(2,1)S(1)}, bf16[16,4352]{1,0:T(8,128)(2,1)S(1)}, u32[]{:S(2)}, u32[]{:S(2)}) collective-permute-start(bf16[16,4352]{1,0:T(8,128)(2,1)S(1)} %get-tuple-element.53), channel_id=1, source_target_pairs={{0,24},{8,16},{16,8},{24,0},{1,25},{9,17},{17,9},{25,1},{2,26},{10... | collective-permute-start | bytes 417800 | tf_op jit(solution)/shard_map/ppermute | solution.py:439
  25.1 8.2 %collective-permute-start.15 = (bf16[16,4352]{1,0:T(8,128)(2,1)S(1)}, bf16[16,4352]{1,0:T(8,128)(2,1)S(1)}, u32[]{:S(2)}, u32[]{:S(2)}) collective-permute-start(bf16[16,4352]{1,0:T(8,128)(2,1)S(1)} %shard_map.146.refs_0_), channel_id=1, source_target_pairs={{0,4},{1,5},{2,6},{3,7},{4,0},{5,1},{6,2},{7,3},{8,12},{9,13},{10,... | collective-permute-start | bytes 417800 | tf_op jit(solution)/shard_map/ppermute | solution.py:446
  25.2 8.1 %collective-permute-start.14 = (bf16[16,4352]{1,0:T(8,128)(2,1)S(1)}, bf16[16,4352]{1,0:T(8,128)(2,1)S(1)}, u32[]{:S(2)}, u32[]{:S(2)}) collective-permute-start(bf16[16,4352]{1,0:T(8,128)(2,1)S(1)} %shard_map.146.refs_0_), channel_id=1, source_target_pairs={{0,2},{1,3},{2,0},{3,1},{4,6},{5,7},{6,4},{7,5},{8,10},{9,11},{10,... | collective-permute-start | bytes 417800 | tf_op jit(solution)/shard_map/ppermute | solution.py:446
  26.5 14.1 %collective-permute-start.13 = (bf16[16,4352]{1,0:T(8,128)(2,1)S(1)}, bf16[16,4352]{1,0:T(8,128)(2,1)S(1)}, u32[]{:S(2)}, u32[]{:S(2)}) collective-permute-start(bf16[16,4352]{1,0:T(8,128)(2,1)S(1)} %shard_map.146.refs_0_), channel_id=1, source_target_pairs={{0,6},{1,7},{2,4},{3,5},{4,2},{5,3},{6,0},{7,1},{8,14},{9,15},{10,... | collective-permute-start | bytes 417800 | tf_op jit(solution)/shard_map/ppermute | solution.py:446
  27.8 4.7 %collective-permute-start.8 = (bf16[96,512]{1,0:T(8,128)(2,1)S(1)}, bf16[96,512]{1,0:T(8,128)(2,1)S(1)}, u32[]{:S(2)}, u32[]{:S(2)}) collective-permute-start(bf16[96,512]{1,0:T(8,128)(2,1)S(1)} %get-tuple-element.45), channel_id=1, source_target_pairs={{0,24},{8,0},{16,8},{24,16},{1,25},{9,1},{17,9},{25,17},{2,26},{10... | collective-permute-start | bytes 294920 | tf_op jit(solution)/shard_map/ppermute | solution.py:550
  27.8 4.6 %collective-permute-start.9 = (bf16[48,512]{1,0:T(8,128)(2,1)S(1)}, bf16[48,512]{1,0:T(8,128)(2,1)S(1)}, u32[]{:S(2)}, u32[]{:S(2)}) collective-permute-start(bf16[48,512]{1,0:T(8,128)(2,1)S(1)} %get-tuple-element.46), channel_id=1, source_target_pairs={{0,8},{8,16},{16,24},{24,0},{1,9},{9,17},{17,25},{25,1},{2,10},{10... | collective-permute-start | bytes 147464 | tf_op jit(solution)/shard_map/ppermute | solution.py:551
  40.7 1.7 %collective-permute-start.16 = (f32[16,4352]{1,0:T(8,128)S(1)}, f32[16,4352]{1,0:T(8,128)S(1)}, u32[]{:S(2)}, u32[]{:S(2)}) collective-permute-start(f32[16,4352]{1,0:T(8,128)S(1)} %shard_map.147.mine), channel_id=1, source_target_pairs={{0,1},{1,0},{2,3},{3,2},{4,5},{5,4},{6,7},{7,6},{8,9},{9,8},{10,11... | collective-permute-start | bytes 835592 | tf_op jit(solution)/shard_map/ppermute | solution.py:452
  (1 other events, 1.2 us)

commit v8 on v6

--- a/solution.py
+++ b/solution.py
@@ -24,7 +24,6 @@
 NEG = -1e30
 W_ORDER = (1, 2, 3)
 CP_ORDER = (1, 2, 3)
-Z_ORDER = (3, 1, 2)
 BF = jnp.bfloat16
 F32 = jnp.float32
 VMEM = pl.BlockSpec(memory_space=pltpu.VMEM)
@@ -445,12 +444,8 @@
         ]
         return [got[order.index(by)] for by in range(1, cps)]
 
-    def over_z(array):
-        got = [
-            lax.ppermute(array, "dp", [(i, i ^ (2 * by)) for i in range(dps)])
-            for by in range(floors - 1, 0, -1)
-        ]
-        return got[::-1]
+    def over_z(array, by):
+        return lax.ppermute(array, "dp", [(i, i ^ (2 * by)) for i in range(dps)])
 
     def over_core(array):
         return lax.ppermute(array, "dp", [(i, i ^ 1) for i in range(dps)])
@@ -558,6 +553,7 @@
         (shape((rows, feats), BF),) * 2 + (token,),
         [VMEM] * 4,
         (key_g, value_g, last, first),
+        flops=2**30,
     )
     if floors != 4:
         core = lax.axis_index("dp") % 2
@@ -572,11 +568,13 @@
         weight_grad = lax.psum(weights, "dp")
         conv_grad = lax.psum(taps, ("cp", "dp"))[:KW]
     else:
+        across = over_z(part, 2)
+        beside = over_z(part, 1)
         mine = call(
             z_sum_kernel,
             shape((16, wide), F32),
             [VMEM] * (floors + 1),
-            (join_done, part, *ordered(over_z(part), Z_ORDER)),
+            (join_done, part, beside, across, over_z(across, 1)),
         )
         weight_grad, conv_grad = call(
             final_kernel,

time: 43.4 us -> 43.3 us (level)
  the two profiles are of different devices: /device:TPU:19 before, /device:TPU:0 now
where the time goes in v8:
time: 43.3 us; the launch traced here: 43.1 us
  starting transfers between devices  18.8 us (43%)
  waiting for transfers between devices  12.3 us (28%)
  Pallas kernels  10.5 us (24%)
  between operations  1.5 us (3%)
    pallas_call x12, Pallas kernels, call(): pl.pallas_call(kernel, out_shape=outs, in_specs=ins, out_specs=jax.tree.m...  9.36 us
    ppermute x6, starting transfers between devices, over_cp(): lax.ppermute(arrays[by - 1], 'cp', [(i, i ^ by) for i in range(cps)])  7.04 us
    ppermute x3, waiting for transfers between devices, over_z(): return lax.ppermute(array, 'dp', [(i, i ^ 2 * by) for i in range(dps)])  5.46 us
    ppermute x3, starting transfers between devices, over_z(): return lax.ppermute(array, 'dp', [(i, i ^ 2 * by) for i in range(dps)])  4.99 us
    ppermute x6, waiting for transfers between devices, over_cp(): lax.ppermute(arrays[by - 1], 'cp', [(i, i ^ by) for i in range(cps)])  4.41 us
    ppermute x1, starting transfers between devices, body(): near = lax.ppermute(ahead, 'cp', upward)  2.99 us
    ppermute x4, waiting for transfers between devices, over_core(): return lax.ppermute(array, 'dp', [(i, i ^ 1) for i in range(dps)])  1.55 us
    ppermute x1, starting transfers between devices, body(): last = lax.ppermute(back, 'cp', downward)  1.17 us
  transfers between devices with their start and end apart: 17, of which 8 were waited for; matrix products, arithmetic and copies ran while one was open for 0% of the time, Pallas kernels for 19%

profile of v8, /device:TPU:0, one launch (start us, length us, event | category | flops | bytes accessed | tf_op | source)
XLA Modules:
  0.0 43.1 jit_solution(14526996976854664433)
XLA Ops:
  0.7 1.2 %shard_map.136 = (bf16[112,512]{1,0:T(8,128)(2,1)S(1)}, bf16[64,512]{1,0:T(8,128)(2,1)S(1)}, bf16[128,512]{1,0:T(8,128)(2,1)S(1)}) custom-call(bf16[192,512]{1,0:T(8,128)(2,1)} %bitcast.14, bf16[192,512]{1,0:T(8,128)(2,1)} %bitcast.17, bf16[192,1024]{1,0:T(8,128)(2,1)} %bitcast.9, bf16[128,1024]{1,0:T(8,128)(2,1)} %w.5), custom_call_target="tpu_custom_call" | custom-call | tf_op jit(solution)/shard_map/pallas_call | solution.py:100
  1.8 3.0 %collective-permute-start = (bf16[112,512]{1,0:T(8,128)(2,1)S(1)}, bf16[112,512]{1,0:T(8,128)(2,1)S(1)}, u32[]{:S(2)}, u32[]{:S(2)}) collective-permute-start(bf16[112,512]{1,0:T(8,128)(2,1)S(1)} %get-tuple-element.34), channel_id=1, source_target_pairs={{0,8},{8,16},{16,24},{24,0},{1,9},{9,17},{17,25},{25,1},{2,10},{10... | collective-permute-start | bytes 344072 | tf_op jit(solution)/shard_map/ppermute | solution.py:454
  4.8 1.0 %collective-permute-start.1 = (bf16[64,512]{1,0:T(8,128)(2,1)S(1)}, bf16[64,512]{1,0:T(8,128)(2,1)S(1)}, u32[]{:S(2)}, u32[]{:S(2)}) collective-permute-start(bf16[64,512]{1,0:T(8,128)(2,1)S(1)} %get-tuple-element.35), channel_id=1, source_target_pairs={{0,24},{8,0},{16,8},{24,16},{1,25},{9,1},{17,9},{25,17},{2,26},{10... | collective-permute-start | bytes 196616 | tf_op jit(solution)/shard_map/ppermute | solution.py:455
  5.9 2.0 %collective-permute-start.5 = (bf16[128,512]{1,0:T(8,128)(2,1)S(1)}, bf16[128,512]{1,0:T(8,128)(2,1)S(1)}, u32[]{:S(2)}, u32[]{:S(2)}) collective-permute-start(bf16[128,512]{1,0:T(8,128)(2,1)S(1)} %get-tuple-element.41), channel_id=1, source_target_pairs={{0,24},{8,16},{16,8},{24,0},{1,25},{9,17},{17,9},{25,1},{2,26},{10... | collective-permute-start | bytes 393224 | tf_op jit(solution)/shard_map/ppermute | solution.py:442
  8.3 1.0 %collective-permute-start.3 = (bf16[128,512]{1,0:T(8,128)(2,1)S(1)}, bf16[128,512]{1,0:T(8,128)(2,1)S(1)}, u32[]{:S(2)}, u32[]{:S(2)}) collective-permute-start(bf16[128,512]{1,0:T(8,128)(2,1)S(1)} %get-tuple-element.41), channel_id=1, source_target_pairs={{0,8},{8,0},{16,24},{24,16},{1,9},{9,1},{17,25},{25,17},{2,10},{10... | collective-permute-start | bytes 393224 | tf_op jit(solution)/shard_map/ppermute | solution.py:442
  10.9 0.9 %collective-permute-done.1.far = bf16[64,512]{1,0:T(8,128)(2,1)S(1)} collective-permute-done((bf16[64,512]{1,0:T(8,128)(2,1)S(1)}, bf16[64,512]{1,0:T(8,128)(2,1)S(1)}, u32[]{:S(2)}, u32[]{:S(2)}) %collective-permute-start.1) | collective-permute-done | bytes 65568 | tf_op jit(solution)/shard_map/ppermute | solution.py:455
  11.8 1.5 %shard_map.138 = (bf16[192,512]{1,0:T(8,128)(2,1)S(1)}, bf16[592,512]{1,0:T(8,128)(2,1)S(1)}) custom-call(bf16[192,512]{1,0:T(8,128)(2,1)S(1)} %bitcast.23, bf16[192,512]{1,0:T(8,128)(2,1)S(1)} %bitcast.15, bf16[192,512]{1,0:T(8,128)(2,1)S(1)} %bitcast.18, bf16[112,512]{1,0:T(8,128)(2,1)S(1)} %collective-permute-done.near, ...), custom_call_target="tpu_custom_call" | custom-call | flops 4294967296 | tf_op jit(solution)/shard_map/pallas_call | solution.py:46
  13.4 1.0 %shard_map.139 = (bf16[192,1024]{1,0:T(8,128)(2,1)}, bf16[4,64,1024]{2,1,0:T(8,128)(2,1)S(1)}, f32[4,64,1024]{2,1,0:T(8,128)S(1)}) custom-call(bf16[192,512]{1,0:T(8,128)(2,1)S(1)} %get-tuple-element.37.att, bf16[112,512]{1,0:T(8,128)(2,1)S(1)} %collective-permute-done.near, bf16[64,512]{1,0:T(8,128)(2,1)S(1)} %collective-permute-done.1.far, ...), custom_call_target="tpu_custom_call" | custom-call | tf_op jit(solution)/shard_map/pallas_call | solution.py:46
  15.2 1.0 %collective-permute-done.3.refs_0_ = bf16[128,512]{1,0:T(8,128)(2,1)S(1)} collective-permute-done((bf16[128,512]{1,0:T(8,128)(2,1)S(1)}, bf16[128,512]{1,0:T(8,128)(2,1)S(1)}, u32[]{:S(2)}, u32[]{:S(2)}) %collective-permute-start.3) | collective-permute-done | bytes 131104 | tf_op jit(solution)/shard_map/ppermute | solution.py:442
  16.3 0.9 %shard_map.141.conv = f32[8,512]{1,0:T(8,128)S(1)} custom-call(bf16[192,512]{1,0:T(8,128)(2,1)S(1)} %get-tuple-element.37.att, bf16[512,512]{1,0:T(8,128)(2,1)S(1)} %shard_map.140.wx, bf16[192,1024]{1,0:T(8,128)(2,1)S(1)} %bitcast.21, bf16[192,1024]{1,0:T(8,128)(2,1)S(1)} %bitcast.13, bf16[112,512]{1,0:T(8,128)(2,1)S(1)} %collective-permute-done.near, ...), custom_call_target="tpu_custom_call" | custom-call | tf_op jit(solution)/shard_map/pallas_call | solution.py:46
  17.5 1.1 %collective-permute-start.8 = (bf16[16,4352]{1,0:T(8,128)(2,1)S(1)}, bf16[16,4352]{1,0:T(8,128)(2,1)S(1)}, u32[]{:S(2)}, u32[]{:S(2)}) collective-permute-start(bf16[16,4352]{1,0:T(8,128)(2,1)S(1)} %get-tuple-element.51), channel_id=1, source_target_pairs={{0,8},{8,0},{16,24},{24,16},{1,9},{9,1},{17,25},{25,17},{2,10},{10... | collective-permute-start | bytes 417800 | tf_op jit(solution)/shard_map/ppermute | solution.py:442
  18.6 1.0 %collective-permute-start.9 = (bf16[16,4352]{1,0:T(8,128)(2,1)S(1)}, bf16[16,4352]{1,0:T(8,128)(2,1)S(1)}, u32[]{:S(2)}, u32[]{:S(2)}) collective-permute-start(bf16[16,4352]{1,0:T(8,128)(2,1)S(1)} %get-tuple-element.52), channel_id=1, source_target_pairs={{0,16},{8,24},{16,0},{24,8},{1,17},{9,25},{17,1},{25,9},{2,18},{10... | collective-permute-start | bytes 417800 | tf_op jit(solution)/shard_map/ppermute | solution.py:442
  19.6 1.4 %collective-permute-start.10 = (bf16[16,4352]{1,0:T(8,128)(2,1)S(1)}, bf16[16,4352]{1,0:T(8,128)(2,1)S(1)}, u32[]{:S(2)}, u32[]{:S(2)}) collective-permute-start(bf16[16,4352]{1,0:T(8,128)(2,1)S(1)} %get-tuple-element.53), channel_id=1, source_target_pairs={{0,24},{8,16},{16,8},{24,0},{1,25},{9,17},{17,9},{25,1},{2,26},{10... | collective-permute-start | bytes 417800 | tf_op jit(solution)/shard_map/ppermute | solution.py:442
  21.0 3.2 %shard_map.144 = (bf16[192,512]{1,0:T(8,128)(2,1)}, f32[192,512]{1,0:T(8,128)S(1)}, f32[192,512]{1,0:T(8,128)S(1)}, bf16[96,512]{1,0:T(8,128)(2,1)S(1)}, bf16[48...) custom-call(f32[16,4352]{1,0:T(8,128)S(1)} %get-tuple-element.43.after.refs_0_, bf16[192,512]{1,0:T(8,128)(2,1)S(1)} %bitcast.24, ...), custom_call_target="tpu_custom_call" | custom-call | bytes 10485760 | tf_op jit(solution)/shard_map/pallas_call | solution.py:46
  24.2 3.0 %collective-permute-done.9.refs_2_ = bf16[16,4352]{1,0:T(8,128)(2,1)S(1)} collective-permute-done((bf16[16,4352]{1,0:T(8,128)(2,1)S(1)}, bf16[16,4352]{1,0:T(8,128)(2,1)S(1)}, u32[]{:S(2)}, u32[]{:S(2)}) %collective-permute-start.9) | collective-permute-done | bytes 139296 | tf_op jit(solution)/shard_map/ppermute | solution.py:442
  27.3 2.7 %collective-permute-start.14 = (bf16[16,4352]{1,0:T(8,128)(2,1)S(1)}, bf16[16,4352]{1,0:T(8,128)(2,1)S(1)}, u32[]{:S(2)}, u32[]{:S(2)}) collective-permute-start(bf16[16,4352]{1,0:T(8,128)(2,1)S(1)} %get-tuple-element.59.refs_0_), channel_id=1, source_target_pairs={{0,4},{1,5},{2,6},{3,7},{4,0},{5,1},{6,2},{7,3},{8,12},{9,13},{10,... | collective-permute-start | bytes 417800 | tf_op jit(solution)/shard_map/ppermute | solution.py:448
  30.0 1.2 %collective-permute-start.11 = (bf16[96,512]{1,0:T(8,128)(2,1)S(1)}, bf16[96,512]{1,0:T(8,128)(2,1)S(1)}, u32[]{:S(2)}, u32[]{:S(2)}) collective-permute-start(bf16[96,512]{1,0:T(8,128)(2,1)S(1)} %get-tuple-element.54), channel_id=1, source_target_pairs={{0,24},{8,0},{16,8},{24,16},{1,25},{9,1},{17,9},{25,17},{2,26},{10... | collective-permute-start | bytes 294920 | tf_op jit(solution)/shard_map/ppermute | solution.py:549
  31.1 0.9 %collective-permute-start.12 = (bf16[48,512]{1,0:T(8,128)(2,1)S(1)}, bf16[48,512]{1,0:T(8,128)(2,1)S(1)}, u32[]{:S(2)}, u32[]{:S(2)}) collective-permute-start(bf16[48,512]{1,0:T(8,128)(2,1)S(1)} %get-tuple-element.55), channel_id=1, source_target_pairs={{0,8},{8,16},{16,24},{24,0},{1,9},{9,17},{17,25},{25,1},{2,10},{10... | collective-permute-start | bytes 147464 | tf_op jit(solution)/shard_map/ppermute | solution.py:550
  32.0 1.6 %collective-permute-start.13 = (bf16[16,4352]{1,0:T(8,128)(2,1)S(1)}, bf16[16,4352]{1,0:T(8,128)(2,1)S(1)}, u32[]{:S(2)}, u32[]{:S(2)}) collective-permute-start(bf16[16,4352]{1,0:T(8,128)(2,1)S(1)} %get-tuple-element.59.refs_0_), channel_id=1, source_target_pairs={{0,2},{1,3},{2,0},{3,1},{4,6},{5,7},{6,4},{7,5},{8,10},{9,11},{10,... | collective-permute-start | bytes 417800 | tf_op jit(solution)/shard_map/ppermute | solution.py:448
  33.6 2.0 %collective-permute-done.14.refs_2_ = bf16[16,4352]{1,0:T(8,128)(2,1)S(1)} collective-permute-done((bf16[16,4352]{1,0:T(8,128)(2,1)S(1)}, bf16[16,4352]{1,0:T(8,128)(2,1)S(1)}, u32[]{:S(2)}, u32[]{:S(2)}) %collective-permute-start.14) | collective-permute-done | bytes 139296 | tf_op jit(solution)/shard_map/ppermute | solution.py:448
  37.1 0.8 %collective-permute-done.13.refs_1_ = bf16[16,4352]{1,0:T(8,128)(2,1)S(1)} collective-permute-done((bf16[16,4352]{1,0:T(8,128)(2,1)S(1)}, bf16[16,4352]{1,0:T(8,128)(2,1)S(1)}, u32[]{:S(2)}, u32[]{:S(2)}) %collective-permute-start.13) | collective-permute-done | bytes 139296 | tf_op jit(solution)/shard_map/ppermute | solution.py:448
  38.0 2.7 %collective-permute-done.15.refs_3_ = bf16[16,4352]{1,0:T(8,128)(2,1)S(1)} collective-permute-done((bf16[16,4352]{1,0:T(8,128)(2,1)S(1)}, bf16[16,4352]{1,0:T(8,128)(2,1)S(1)}, u32[]{:S(2)}, u32[]{:S(2)}) %collective-permute-start.15) | collective-permute-done | bytes 139296 | tf_op jit(solution)/shard_map/ppermute | solution.py:448
  40.8 1.5 %collective-permute-done.16.theirs = f32[16,4352]{1,0:T(8,128)S(1)} collective-permute-done((f32[16,4352]{1,0:T(8,128)S(1)}, f32[16,4352]{1,0:T(8,128)S(1)}, u32[]{:S(2)}, u32[]{:S(2)}) %collective-permute-start.16) | collective-permute-done | bytes 278560 | tf_op jit(solution)/shard_map/ppermute | solution.py:451
  42.3 0.8 %shard_map.148 = (f32[128,1024]{1,0:T(8,128)}, f32[7,1024]{1,0:T(8,128)}) custom-call(f32[8,128]{1,0:T(8,128)S(1)} %get-tuple-element.58.after, f32[16,4352]{1,0:T(8,128)S(1)} %shard_map.147.mine, f32[16,4352]{1,0:T(8,128)S(1)} %collective-permute-done.16.theirs), custom_call_target="tpu_custom_call" | custom-call | tf_op jit(solution)/shard_map/pallas_call | solution.py:46
  (39 shorter events, 4.3 us)
Async XLA Ops:
  0.6 9.4 %copy-start = (bf16[1,192,1024]{2,1,0:T(8,128)(2,1)S(1)}, bf16[1,192,1024]{2,1,0:T(8,128)(2,1)}, u32[]{:S(2)}) copy-start(bf16[1,192,1024]{2,1,0:T(8,128)(2,1)} %param.13) | copy-start | bytes 1179652
  0.6 9.4 %copy-start.7 = (f32[7,1024]{1,0:T(8,128)S(1)}, f32[7,1024]{1,0:T(8,128)}, u32[]{:S(2)}) copy-start(f32[7,1024]{1,0:T(8,128)} %taps.3) | copy-start | bytes 86020
  0.7 11.1 %copy-start.4 = (bf16[1,192,1024]{2,1,0:T(8,128)(2,1)S(1)}, bf16[1,192,1024]{2,1,0:T(8,128)(2,1)}, u32[]{:S(2)}) copy-start(bf16[1,192,1024]{2,1,0:T(8,128)(2,1)} %param.12) | copy-start | bytes 1179652
  0.7 11.1 %copy-start.6 = (bf16[1,192,512]{2,1,0:T(8,128)(2,1)S(1)}, bf16[1,192,512]{2,1,0:T(8,128)(2,1)}, u32[]{:S(2)}) copy-start(bf16[1,192,512]{2,1,0:T(8,128)(2,1)} %param.9) | copy-start | bytes 589828
  1.8 9.9 %collective-permute-start = (bf16[112,512]{1,0:T(8,128)(2,1)S(1)}, bf16[112,512]{1,0:T(8,128)(2,1)S(1)}, u32[]{:S(2)}, u32[]{:S(2)}) collective-permute-start(bf16[112,512]{1,0:T(8,128)(2,1)S(1)} %get-tuple-element.34), channel_id=1, source_target_pairs={{0,8},{8,16},{16,24},{24,0},{1,9},{9,17},{17,25},{25,1},{2,10},{10... | collective-permute-start | bytes 344072 | tf_op jit(solution)/shard_map/ppermute | solution.py:454
  4.8 6.9 %collective-permute-start.1 = (bf16[64,512]{1,0:T(8,128)(2,1)S(1)}, bf16[64,512]{1,0:T(8,128)(2,1)S(1)}, u32[]{:S(2)}, u32[]{:S(2)}) collective-permute-start(bf16[64,512]{1,0:T(8,128)(2,1)S(1)} %get-tuple-element.35), channel_id=1, source_target_pairs={{0,24},{8,0},{16,8},{24,16},{1,25},{9,1},{17,9},{25,17},{2,26},{10... | collective-permute-start | bytes 196616 | tf_op jit(solution)/shard_map/ppermute | solution.py:455
  5.9 9.0 %collective-permute-start.5 = (bf16[128,512]{1,0:T(8,128)(2,1)S(1)}, bf16[128,512]{1,0:T(8,128)(2,1)S(1)}, u32[]{:S(2)}, u32[]{:S(2)}) collective-permute-start(bf16[128,512]{1,0:T(8,128)(2,1)S(1)} %get-tuple-element.41), channel_id=1, source_target_pairs={{0,24},{8,16},{16,8},{24,0},{1,25},{9,17},{17,9},{25,1},{2,26},{10... | collective-permute-start | bytes 393224 | tf_op jit(solution)/shard_map/ppermute | solution.py:442
  7.8 7.4 %collective-permute-start.4 = (bf16[128,512]{1,0:T(8,128)(2,1)S(1)}, bf16[128,512]{1,0:T(8,128)(2,1)S(1)}, u32[]{:S(2)}, u32[]{:S(2)}) collective-permute-start(bf16[128,512]{1,0:T(8,128)(2,1)S(1)} %get-tuple-element.41), channel_id=1, source_target_pairs={{0,16},{8,24},{16,0},{24,8},{1,17},{9,25},{17,1},{25,9},{2,18},{10... | collective-permute-start | bytes 393224 | tf_op jit(solution)/shard_map/ppermute | solution.py:442
  8.3 7.9 %collective-permute-start.3 = (bf16[128,512]{1,0:T(8,128)(2,1)S(1)}, bf16[128,512]{1,0:T(8,128)(2,1)S(1)}, u32[]{:S(2)}, u32[]{:S(2)}) collective-permute-start(bf16[128,512]{1,0:T(8,128)(2,1)S(1)} %get-tuple-element.41), channel_id=1, source_target_pairs={{0,8},{8,0},{16,24},{24,16},{1,9},{9,1},{17,25},{25,17},{2,10},{10... | collective-permute-start | bytes 393224 | tf_op jit(solution)/shard_map/ppermute | solution.py:442
  10.0 1.7 %copy-start.2 = (bf16[1,192,512]{2,1,0:T(8,128)(2,1)S(1)}, bf16[1,192,512]{2,1,0:T(8,128)(2,1)}, u32[]{:S(2)}) copy-start(bf16[1,192,512]{2,1,0:T(8,128)(2,1)} %param.10) | copy-start | bytes 589828
  13.3 3.0 %collective-permute-start.6 = (bf16[592,512]{1,0:T(8,128)(2,1)S(1)}, bf16[592,512]{1,0:T(8,128)(2,1)S(1)}, u32[]{:S(2)}, u32[]{:S(2)}) collective-permute-start(bf16[592,512]{1,0:T(8,128)(2,1)S(1)} %get-tuple-element.42), channel_id=1, source_target_pairs={{0,1},{1,0},{2,3},{3,2},{4,5},{5,4},{6,7},{7,6},{8,9},{9,8},{10,11... | collective-permute-start | bytes 1818632 | tf_op jit(solution)/shard_map/ppermute | solution.py:451
  13.4 2.9 %copy-start.1 = (bf16[128,1024]{1,0:T(8,128)(2,1)S(1)}, bf16[128,1024]{1,0:T(8,128)(2,1)}, u32[]{:S(2)}) copy-start(bf16[128,1024]{1,0:T(8,128)(2,1)} %w.5) | copy-start | bytes 786436
  14.4 2.8 %collective-permute-start.2 = (bf16[4,64,1024]{2,1,0:T(8,128)(2,1)S(1)}, bf16[4,64,1024]{2,1,0:T(8,128)(2,1)S(1)}, u32[]{:S(2)}, u32[]{:S(2)}) collective-permute-start(bf16[4,64,1024]{2,1,0:T(8,128)(2,1)S(1)} %get-tuple-element.40.after), channel_id=1, source_target_pairs={{0,1},{1,0},{2,3},{3,2},{4,5},{5,4},{6,7},{7,6},{8,9},{9,8},{10,11... | collective-permute-start | bytes 1572872 | tf_op jit(solution)/shard_map/ppermute | solution.py:451
  17.3 3.7 %copy-start.5 = (bf16[192,1024]{1,0:T(8,128)(2,1)S(1)}, bf16[192,1024]{1,0:T(8,128)(2,1)}, u32[]{:S(2)}) copy-start(bf16[192,1024]{1,0:T(8,128)(2,1)} %get-tuple-element.44.stream_grad) | copy-start | bytes 1179652
  17.4 3.6 %collective-permute-start.7 = (bf16[3,128,512]{2,1,0:T(8,128)(2,1)S(1)}, bf16[3,128,512]{2,1,0:T(8,128)(2,1)S(1)}, u32[]{:S(2)}, u32[]{:S(2)}) collective-permute-start(bf16[3,128,512]{2,1,0:T(8,128)(2,1)S(1)} %shard_map.143), channel_id=1, source_target_pairs={{0,1},{1,0},{2,3},{3,2},{4,5},{5,4},{6,7},{7,6},{8,9},{9,8},{10,11... | collective-permute-start | bytes 1179656 | tf_op jit(solution)/shard_map/ppermute | solution.py:451
  17.5 6.7 %collective-permute-start.8 = (bf16[16,4352]{1,0:T(8,128)(2,1)S(1)}, bf16[16,4352]{1,0:T(8,128)(2,1)S(1)}, u32[]{:S(2)}, u32[]{:S(2)}) collective-permute-start(bf16[16,4352]{1,0:T(8,128)(2,1)S(1)} %get-tuple-element.51), channel_id=1, source_target_pairs={{0,8},{8,0},{16,24},{24,16},{1,9},{9,1},{17,25},{25,17},{2,10},{10... | collective-permute-start | bytes 417800 | tf_op jit(solution)/shard_map/ppermute | solution.py:442
  18.6 8.6 %collective-permute-start.9 = (bf16[16,4352]{1,0:T(8,128)(2,1)S(1)}, bf16[16,4352]{1,0:T(8,128)(2,1)S(1)}, u32[]{:S(2)}, u32[]{:S(2)}) collective-permute-start(bf16[16,4352]{1,0:T(8,128)(2,1)S(1)} %get-tuple-element.52), channel_id=1, source_target_pairs={{0,16},{8,24},{16,0},{24,8},{1,17},{9,25},{17,1},{25,9},{2,18},{10... | collective-permute-start | bytes 417800 | tf_op jit(solution)/shard_map/ppermute | solution.py:442
  19.6 7.6 %collective-permute-start.10 = (bf16[16,4352]{1,0:T(8,128)(2,1)S(1)}, bf16[16,4352]{1,0:T(8,128)(2,1)S(1)}, u32[]{:S(2)}, u32[]{:S(2)}) collective-permute-start(bf16[16,4352]{1,0:T(8,128)(2,1)S(1)} %get-tuple-element.53), channel_id=1, source_target_pairs={{0,24},{8,16},{16,8},{24,0},{1,25},{9,17},{17,9},{25,1},{2,26},{10... | collective-permute-start | bytes 417800 | tf_op jit(solution)/shard_map/ppermute | solution.py:442
  27.3 8.2 %collective-permute-start.14 = (bf16[16,4352]{1,0:T(8,128)(2,1)S(1)}, bf16[16,4352]{1,0:T(8,128)(2,1)S(1)}, u32[]{:S(2)}, u32[]{:S(2)}) collective-permute-start(bf16[16,4352]{1,0:T(8,128)(2,1)S(1)} %get-tuple-element.59.refs_0_), channel_id=1, source_target_pairs={{0,4},{1,5},{2,6},{3,7},{4,0},{5,1},{6,2},{7,3},{8,12},{9,13},{10,... | collective-permute-start | bytes 417800 | tf_op jit(solution)/shard_map/ppermute | solution.py:448
  30.0 6.3 %collective-permute-start.11 = (bf16[96,512]{1,0:T(8,128)(2,1)S(1)}, bf16[96,512]{1,0:T(8,128)(2,1)S(1)}, u32[]{:S(2)}, u32[]{:S(2)}) collective-permute-start(bf16[96,512]{1,0:T(8,128)(2,1)S(1)} %get-tuple-element.54), channel_id=1, source_target_pairs={{0,24},{8,0},{16,8},{24,16},{1,25},{9,1},{17,9},{25,17},{2,26},{10... | collective-permute-start | bytes 294920 | tf_op jit(solution)/shard_map/ppermute | solution.py:549
  31.1 5.2 %collective-permute-start.12 = (bf16[48,512]{1,0:T(8,128)(2,1)S(1)}, bf16[48,512]{1,0:T(8,128)(2,1)S(1)}, u32[]{:S(2)}, u32[]{:S(2)}) collective-permute-start(bf16[48,512]{1,0:T(8,128)(2,1)S(1)} %get-tuple-element.55), channel_id=1, source_target_pairs={{0,8},{8,16},{16,24},{24,0},{1,9},{9,17},{17,25},{25,1},{2,10},{10... | collective-permute-start | bytes 147464 | tf_op jit(solution)/shard_map/ppermute | solution.py:550
  32.0 6.0 %collective-permute-start.13 = (bf16[16,4352]{1,0:T(8,128)(2,1)S(1)}, bf16[16,4352]{1,0:T(8,128)(2,1)S(1)}, u32[]{:S(2)}, u32[]{:S(2)}) collective-permute-start(bf16[16,4352]{1,0:T(8,128)(2,1)S(1)} %get-tuple-element.59.refs_0_), channel_id=1, source_target_pairs={{0,2},{1,3},{2,0},{3,1},{4,6},{5,7},{6,4},{7,5},{8,10},{9,11},{10,... | collective-permute-start | bytes 417800 | tf_op jit(solution)/shard_map/ppermute | solution.py:448
  35.6 5.1 %collective-permute-start.15 = (bf16[16,4352]{1,0:T(8,128)(2,1)S(1)}, bf16[16,4352]{1,0:T(8,128)(2,1)S(1)}, u32[]{:S(2)}, u32[]{:S(2)}) collective-permute-start(bf16[16,4352]{1,0:T(8,128)(2,1)S(1)} %collective-permute-done.14.refs_2_), channel_id=1, source_target_pairs={{0,2},{1,3},{2,0},{3,1},{4,6},{5,7},{6,4},{7,5},{8,10},{9,11},{10,... | collective-permute-start | bytes 417800 | tf_op jit(solution)/shard_map/ppermute | solution.py:448
  40.7 1.6 %collective-permute-start.16 = (f32[16,4352]{1,0:T(8,128)S(1)}, f32[16,4352]{1,0:T(8,128)S(1)}, u32[]{:S(2)}, u32[]{:S(2)}) collective-permute-start(f32[16,4352]{1,0:T(8,128)S(1)} %shard_map.147.mine), channel_id=1, source_target_pairs={{0,1},{1,0},{2,3},{3,2},{4,5},{5,4},{6,7},{7,6},{8,9},{9,8},{10,11... | collective-permute-start | bytes 835592 | tf_op jit(solution)/shard_map/ppermute | solution.py:451
  (1 other events, 1.7 us)
